TPU v7x, 32 devices: a whole 2x2x4 slice. The times are simulated.
32 devices in a mesh: pair: 2 (over x), blk: 4 (over z), rows: 4 (over y, core).
Axes of the slice: x: 2, y: 2, z: 4, core: 2. Of those that a mesh axis runs over, the one named last changes fastest.
Arguments:
- tiles: float32 [2, 2048, 131072], P('pair', None, ('blk', 'rows')), may hold values from -0.0234375 to 0.0234375
- trial: float32 [2, 131072, 1024], P('pair', ('blk', 'rows')), may hold values from -6 to 6
Outputs:
- products: float32 [2, 2048, 1024], P('pair', ('blk', 'rows'))
All inputs are finite; a program needn't handle non-finite values.
Results may differ from a plain program's by a relative error of at most 0.000076.
Values sent between devices are 32-bit elements; how exact they have to be, the bound alone decides.
No kernel may reach another device: no remote copies, remote signals or barrier semaphores. Data moves between devices by JAX's collectives and lax.ppermute only.
A program may use at most 256 MiB of HBM per device.

v0:
```python
import jax
import jax.numpy as jnp
from jax import lax
from jax.sharding import PartitionSpec as P


def swapped(value, axis, apart):
    mask = 2**apart
    pairs = [(source, source ^ mask) for source in range(lax.axis_size(axis))]
    return lax.ppermute(value, axis, pairs)


def shards(tiles, trial):
    own_block = trial[0]
    partner_block = swapped(own_block, "pair", 0)
    parity_sign = 1.0 - 2.0 * lax.axis_index("pair").astype(jnp.float32)
    combined = partner_block + parity_sign * own_block
    matrix = tiles[0]
    local_rows = lax.psum_scatter(
        jnp.dot(
            matrix, combined, precision=lax.Precision.HIGHEST, preferred_element_type=jnp.float32
        ),
        ("blk", "rows"),
        scatter_dimension=0,
        tiled=True,
    )
    partner_rows = swapped(local_rows, "pair", 0)
    result = 0.5 * (partner_rows + parity_sign * local_rows)
    return result[None]


def solution(mesh):
    in_specs = (P("pair", None, ("blk", "rows")), P("pair", ("blk", "rows"), None))
    out_specs = P("pair", ("blk", "rows"), None)
    return jax.shard_map(shards, mesh=mesh, in_specs=in_specs, out_specs=out_specs, check_vma=False)
```

profile of v0, /device:TPU:0, one launch (start us, length us, event | category | flops | bytes accessed | tf_op | source)
XLA Modules:
  0.0 1319.0 jit_solution(14398919606401992998)
XLA Ops:
  6.5 0.0 reduce-scatter.2.cloned.1.call-start
  6.5 2.9 collective-permute-start
  9.5 720.1 %collective-permute-done = f32[8192,1024]{1,0:T(8,128)} collective-permute-done((f32[8192,1024]{1,0:T(8,128)}, f32[8192,1024]{1,0:T(8,128)}, u32[]{:S(2)}, u32[]{:S(2)}) %collective-permute-start) | collective-permute-done | bytes 33554464 | tf_op jit(solution)/shard_map/ppermute | solution.py:10
  729.5 33.2 %fusion.14 = f32[8192,1024]{1,0:T(8,128)} fusion(f32[8192,1024]{1,0:T(8,128)} %collective-permute-done, f32[]{:T(128)S(6)} %sub.3, f32[1,8192,1024]{2,1,0:T(8,128)} %param.3), kind=kLoop, calls=%fused_computation.2.clone.clone.clone.1 | loop fusion | flops 16777216 | bytes 100663296 | tf_op jit(solution)/shard_map/dot_general | solution.py:20
  762.7 426.9 %fusion.5 = f32[2048,1024]{0,1:T(8,128)} fusion(f32[1,2048,8192]{2,1,0:T(8,128)} %param.2, f32[8192,1024]{1,0:T(8,128)} %fusion.14), kind=kOutput, calls=%fused_computation.5 | convolution fusion | flops 206158430208 | bytes 109051904 | tf_op jit(solution)/shard_map/dot_general | solution.py:20
  1189.7 0.0 reduce-scatter.2.cloned.1.call-update
  1189.7 106.5 %reduce-scatter.2.cloned.1.call-done = f32[128,1024]{0,1:T(8,128)} async-done(((f32[2048,1024]{0,1:T(8,128)}), f32[128,1024]{0,1:T(8,128)}) %reduce-scatter.2.cloned.1.call-update) | async-done | bytes 524304 | tf_op jit(solution)/shard_map/reduce_scatter | solution.py:19
  1296.2 1.5 collective-permute-start.1
  1297.6 12.4 collective-permute-done.1
  1310.1 1.1 multiply_bitcast_fusion
  1311.2 1.0 copy.3
Async XLA Ops:
  6.5 1289.6 %reduce-scatter.2.cloned.1.call-start = ((), (), s32[]{:S(2)}) async-start(), calls=%async_computation.1 | async-start | bytes 8912896 | tf_op jit(solution)/shard_map/reduce_scatter | solution.py:19
  6.5 723.0 %collective-permute-start = (f32[8192,1024]{1,0:T(8,128)}, f32[8192,1024]{1,0:T(8,128)}, u32[]{:S(2)}, u32[]{:S(2)}) collective-permute-start(f32[8192,1024]{1,0:T(8,128)} %bitcast.20), channel_id=1, source_target_pairs={{0,16},{16,0},{1,17},{17,1},{2,18},{18,2},{3,19},{19,3},{4,20},{20... | collective-permute-start | bytes 100663304 | tf_op jit(solution)/shard_map/ppermute | solution.py:10
  1296.2 13.9 %collective-permute-start.1 = (f32[128,1024]{0,1:T(8,128)}, f32[128,1024]{0,1:T(8,128)S(1)}, u32[]{:S(2)}, u32[]{:S(2)}) collective-permute-start(f32[128,1024]{0,1:T(8,128)} %reduce-scatter.2.cloned.1.call-done), channel_id=1, source_target_pairs={{0,16},{16,0},{1,17},{17,1},{2,18},{18,2},{3,19},{19,3},{4,20},{20... | collective-permute-start | bytes 1572872 | tf_op jit(solution)/shard_map/ppermute | solution.py:10
Sparse Core Ops, SparseCore 0:
  1189.8 106.3 reduce-scatter.1
where the time goes:
time: 1320 us
  waiting for transfers between devices  839 us (64%)
  matrix products  427 us (32%)
  other arithmetic  34.3 us (3%)
  between operations  13.4 us (1%)
    ppermute x2, waiting for transfers between devices, swapped(): return lax.ppermute(value, axis, pairs)  733 us
    dot_general x1, matrix products, shards(): jnp.dot(matrix, combined, precision=lax.Precision.HIGHEST, preferred_elem...  427 us
    reduce_scatter x1, waiting for transfers between devices, shards(): lax.psum_scatter(jnp.dot(matrix, combined, precision=lax.Precision.HIGHES...  106 us
    dot_general x1, other arithmetic, shards(): jnp.dot(matrix, combined, precision=lax.Precision.HIGHEST, preferred_elem...  33.2 us
  transfers between devices with their start and end apart: 3, of which 3 were waited for; matrix products, arithmetic and copies ran while one was open for 0% of the time, Pallas kernels for 0%

commit v1 on v0

v1 whole, which is shorter than its diff:
```python
import functools
import math

import jax
import jax.numpy as jnp
from jax import lax
from jax.experimental import pallas as pl
from jax.experimental.pallas import tpu as pltpu
from jax.sharding import PartitionSpec as P

LANES = 128
VMEM_BYTES = 60 * 2**20


AXES = ("pair", "blk", "rows")


def swapped(value, mask):
    devices = math.prod(lax.axis_size(axis) for axis in AXES)
    return lax.ppermute(value, AXES, [(source, source ^ mask) for source in range(devices)])


def after(value, *others):
    return lax.optimization_barrier((value, *others))[0]


def parted(value, low, bits):
    mine = (lax.axis_index(AXES) >> low) & (2**bits - 1)
    value = value.reshape(-1, 2**bits, *value.shape[-2:])
    return [lax.dynamic_index_in_dim(value, mine ^ m, 1, keepdims=False) for m in range(2**bits)]


def scattered_sum(value, low, steps):
    for bits in steps:
        blocks = parted(value, low, bits)
        value = sum((swapped(blocks[m], m << low) for m in range(1, 2**bits)), blocks[0])
        low += bits
    return value


def scattered_halves(value, low, bits, sign):
    pair = 2 ** (low + bits)
    blocks = parted(value, low, bits)
    own = sum((swapped(blocks[m], m << low) for m in range(1, 2**bits)), blocks[0])
    other = sum(swapped(blocks[m], m << low | pair) for m in range(2**bits))
    return 0.5 * (other + sign * own)


def halves(value):
    high = value.astype(jnp.bfloat16)
    low = (value - high.astype(jnp.float32)).astype(jnp.bfloat16)
    return high, low


def split_kernel(matrix_ref, high_ref, low_ref):
    high_ref[...], low_ref[...] = halves(matrix_ref[...])


def split_matrix(matrix):
    rows, depth = matrix.shape
    step = min(rows, 128)
    spec = pl.BlockSpec((step, depth), lambda i: (i, 0))
    part = jax.ShapeDtypeStruct(matrix.shape, jnp.bfloat16)
    return pl.pallas_call(
        split_kernel,
        grid=(rows // step,),
        in_specs=[spec],
        out_specs=[spec, spec],
        out_shape=[part, part],
        compiler_params=pltpu.CompilerParams(vmem_limit_bytes=VMEM_BYTES),
        cost_estimate=pl.CostEstimate(flops=0, bytes_accessed=8 * rows * depth, transcendentals=0),
        name="split_matrix",
    )(matrix)


def product_kernel(added, sign_ref, *refs):
    high_ref, low_ref, own_ref, partner_ref = refs[:4]
    total_ref, out_ref, both = (refs[4:] if added else (None, *refs[4:]))
    width = out_ref.shape[1]

    @pl.when(pl.program_id(0) == 0)
    def _():
        combined = partner_ref[...] + sign_ref[0] * own_ref[...]
        both[:, :width], both[:, width:] = halves(combined)

    right = both[...]
    result = jnp.dot(low_ref[...], right, preferred_element_type=jnp.float32)
    result += jnp.dot(high_ref[...], right, preferred_element_type=jnp.float32)
    result = result[:, width:] + result[:, :width]
    out_ref[...] = result + total_ref[...] if added else result


def product(sign, high, low, own, partner, column, start, total=None):
    rows = high.shape[0]
    depth, width = partner.shape
    step = min(rows, 1024, max(256, 2**21 // depth))
    place = start // depth
    matrix_spec = pl.BlockSpec((step, depth), lambda i: (i, place))
    out_spec = pl.BlockSpec((step, width), lambda i: (i, 0))
    in_specs = [
        pl.BlockSpec(memory_space=pltpu.SMEM),
        matrix_spec,
        matrix_spec,
        pl.BlockSpec((depth, width), lambda i: (place, column)),
        pl.BlockSpec((depth, width), lambda i: (0, 0)),
    ]
    operands = [sign, high, low, own, partner]
    if total is not None:
        in_specs.append(out_spec)
        operands.append(total)
    return pl.pallas_call(
        functools.partial(product_kernel, total is not None),
        grid=(rows // step,),
        in_specs=in_specs,
        out_specs=out_spec,
        out_shape=jax.ShapeDtypeStruct((rows, width), jnp.float32),
        scratch_shapes=[pltpu.VMEM((depth, 2 * width), jnp.bfloat16)],
        compiler_params=pltpu.CompilerParams(vmem_limit_bytes=VMEM_BYTES),
        cost_estimate=pl.CostEstimate(flops=0, bytes_accessed=0, transcendentals=0),
        name="product",
    )(*operands)


def pieces_of(depth, vectors):
    last = vectors // LANES - 1
    least = max(LANES, depth // 8)
    pieces = [(last, 0, least)] + [(chunk, 0, depth) for chunk in range(last - 1)]
    pieces += [(last - 1, 0, depth // 2), (last - 1, depth // 2, depth // 2)]
    pieces += [(last, least, least), (last, depth // 2, depth // 2), (last, 2 * least, least)]
    half = max(LANES, least // 2)
    return pieces + [(last, start, half) for start in range(3 * least, depth // 2, half)]


def shards(tiles, trial):
    own, matrix = trial[0], tiles[0]
    depth, vectors = own.shape
    sign = 1.0 - 2.0 * lax.axis_index("pair").astype(jnp.float32)
    pieces = pieces_of(depth, vectors)
    pair = lax.axis_size("blk") * lax.axis_size("rows")
    bits = pair.bit_length() - 1

    def by_owner(value):
        return value.reshape(pair, -1, value.shape[-1])

    def block(index, *others):
        chunk, start, size = pieces[index]
        source = after(own, *others) if others else own
        return source[start : start + size, chunk * LANES : (chunk + 1) * LANES]

    ahead, cut_ahead = 2, 6
    blocks = {index: block(index) for index in range(ahead)}
    arrived = [swapped(blocks[index], pair) for index in range(ahead)]
    high, low = split_matrix(after(matrix, *blocks.values()))
    totals, covered, sums = {}, {}, {}
    done = high
    for index, (chunk, start, size) in enumerate(pieces):
        partner = arrived[index]
        for later in range(ahead, min(index + cut_ahead + 1, len(pieces))):
            if later not in blocks:
                blocks[later] = block(later, done)
                partner = after(partner, blocks[later])
        if index + ahead < len(pieces):
            arrived.append(swapped(after(blocks[index + ahead], arrived[index], done), pair))
        done = product(sign[None], high, low, own, partner, chunk, start, totals.get(chunk))
        totals[chunk] = done
        covered[chunk] = covered.get(chunk, 0) + size
        if covered[chunk] == depth and index + 1 < len(pieces):
            if pieces[index + 1][0] == pieces[-1][0]:
                done = after(done, arrived[index + 1])
            steps = [2] * (bits // 2) + [1] * (bits % 2)
            done = sums[chunk] = scattered_sum(by_owner(done), 0, steps)[0]

    early = jnp.concatenate([sums[chunk] for chunk in sorted(sums)], axis=1)
    early_partner = swapped(after(early, arrived[-1]), pair)
    steps = [1] + [2] * ((bits - 2) // 2) + [1] * (bits % 2)
    late = after(scattered_sum(by_owner(done), 0, steps), early_partner)
    result = jnp.concatenate(
        [0.5 * (early_partner + sign * early), scattered_halves(late, bits - 1, 1, sign)[0]], axis=1
    )
    return result[None]


def solution(mesh):
    in_specs = (P("pair", None, ("blk", "rows")), P("pair", ("blk", "rows"), None))
    out_specs = P("pair", ("blk", "rows"), None)
    return jax.shard_map(shards, mesh=mesh, in_specs=in_specs, out_specs=out_specs, check_vma=False)
```

time: 1320 us -> 774 us (0.59)
  waiting for transfers between devices: 839 us -> 321 us
  matrix products: 427 us -> 0 us
  Pallas kernels: 0 us -> 310 us
  starting transfers between devices: 4.4 us -> 77.9 us
  local copies, waits for them, and re-layouts: 1 us -> 46.2 us
  other arithmetic: 34.3 us -> 9.3 us
    dot_general x1 -> x0, matrix products: 427 us -> none  [shards(): jnp.dot(matrix, combined, precision=lax.Precision.HIGHEST, preferred_elem...]
    ppermute x2 -> x64, waiting for transfers between devices: 733 us -> 321 us  [swapped(): lax.ppermute(value, AXES, [(source, source ^ mask) for source in range(de...]
    pallas_call x0 -> x15, Pallas kernels: none -> 310 us  [the longest x14 265 us: product(): pl.pallas_call(functools.partial(product_kernel, total is not None), grid...]
    reduce_scatter x1 -> x0, waiting for transfers between devices: 106 us -> none  [shards(): lax.psum_scatter(jnp.dot(matrix, combined, precision=lax.Precision.HIGHES...]
    ppermute x2 -> x64, starting transfers between devices: 4.4 us -> 77.9 us  [swapped(): lax.ppermute(value, AXES, [(source, source ^ mask) for source in range(de...]
    slice x0 -> x10, local copies, waits for them, and re-layouts: none -> 35.1 us  [block(): return source[start:start + size, chunk * LANES:(chunk + 1) * LANES]]
    dot_general x1 -> x0, other arithmetic: 33.2 us -> none  [shards(): jnp.dot(matrix, combined, precision=lax.Precision.HIGHEST, preferred_elem...]
  transfers between devices with their start and end apart: 3 -> 64, of which waited for: 3 -> 49; matrix products, arithmetic and copies ran while one was open for 0% -> 7% of each run, Pallas kernels for 0% -> 40%
where the time goes in v1:
time: 774 us; the launch traced here: 765 us
  waiting for transfers between devices  321 us (41%)
  Pallas kernels  310 us (40%)
  starting transfers between devices  77.9 us (10%)
  local copies, waits for them, and re-layouts  46.2 us (6%)
  other arithmetic  9.3 us (1%)
    ppermute x64, waiting for transfers between devices, swapped(): lax.ppermute(value, AXES, [(source, source ^ mask) for source in range(de...  321 us
    pallas_call x14, Pallas kernels, product(): pl.pallas_call(functools.partial(product_kernel, total is not None), grid...  265 us
    ppermute x64, starting transfers between devices, swapped(): lax.ppermute(value, AXES, [(source, source ^ mask) for source in range(de...  77.9 us
    pallas_call x1, Pallas kernels, split_matrix(): pl.pallas_call(split_kernel, grid=(rows // step,), in_specs=[spec], out_s...  44.9 us
    slice x10, local copies, waits for them, and re-layouts, block(): return source[start:start + size, chunk * LANES:(chunk + 1) * LANES]  35.1 us
  transfers between devices with their start and end apart: 64, of which 49 were waited for; matrix products, arithmetic and copies ran while one was open for 7% of the time, Pallas kernels for 40%

profile of v1, /device:TPU:0, one launch (start us, length us, event | category | flops | bytes accessed | tf_op | source)
XLA Modules:
  0.0 765.4 jit_solution(15844690333314444174)
XLA Ops:
  1.1 3.0 collective-permute-start.1
  4.1 4.4 slice.57
  8.5 44.9 %split_matrix.1 = (bf16[2048,8192]{1,0:T(8,128)(2,1)}, bf16[2048,8192]{1,0:T(8,128)(2,1)}) custom-call(f32[2048,8192]{1,0:T(8,128)} %bitcast.1.matrix_ref), custom_call_target="tpu_custom_call" | custom-call | bytes 134217728 | tf_op jit(solution)/shard_map/split_matrix/pallas_call | solution.py:64
  53.4 14.9 %fusion.16 = (f32[8192,128]{1,0:T(8,128)}, f32[8192,128]{1,0:T(8,128)}, f32[8192,128]{1,0:T(8,128)}, f32[8192,128]{1,0:T(8,128)}, f32[8192,128]{1,0:T(8,128)}) fusion(f32[8192,1024]{1,0:T(8,128)} %bitcast.139), kind=kLoop, calls=%fused_computation.90 | loop fusion | bytes 41943040 | tf_op jit(solution)/shard_map/slice | solution.py:148
  68.3 2.1 collective-permute-start.8
  70.4 5.9 product.14.refs_4_
  76.3 30.5 %collective-permute-done.refs_3_ = f32[8192,128]{1,0:T(8,128)} collective-permute-done((f32[8192,128]{1,0:T(8,128)}, f32[8192,128]{1,0:T(8,128)}, u32[]{:S(2)}, u32[]{:S(2)}) %collective-permute-start) | collective-permute-done | bytes 4194336 | tf_op jit(solution)/shard_map/ppermute | solution.py:20
  108.9 3.0 slice.49
  111.9 30.4 %product.15 = f32[2048,128]{1,0:T(8,128)} custom-call(f32[1]{0:T(128)} %bitcast.sign_ref, bf16[2048,8192]{1,0:T(8,128)(2,1)} %get-tuple-element.44.refs_0_, bf16[2048,8192]{1,0:T(8,128)(2,1)} %get-tuple-element.45.refs_1_, f32[8192,1024]{1,0:T(8,128)} %bitcast.142, f32[8192,128]{1,0:T(8,128)} %collective-permute-done.refs_3_), custom_call_target="tpu_custom_call" | custom-call | tf_op jit(solution)/shard_map/product/pallas_call | solution.py:111
  145.7 6.1 collective-permute-done.4
  151.8 6.0 collective-permute-done.3
  160.5 2.5 collective-permute-start.7
  163.2 4.0 collective-permute-done.7
  169.2 27.5 %collective-permute-done.8.refs_3_ = f32[8192,128]{1,0:T(8,128)} collective-permute-done((f32[8192,128]{1,0:T(8,128)}, f32[8192,128]{1,0:T(8,128)}, u32[]{:S(2)}, u32[]{:S(2)}) %collective-permute-start.8) | collective-permute-done | bytes 4194336 | tf_op jit(solution)/shard_map/ppermute | solution.py:20
  196.7 2.1 collective-permute-start.22
  198.8 3.0 slice.50
  201.8 30.7 %product.16 = f32[2048,128]{1,0:T(8,128)} custom-call(f32[1]{0:T(128)} %bitcast.sign_ref, bf16[2048,8192]{1,0:T(8,128)(2,1)} %get-tuple-element.44.refs_0_, bf16[2048,8192]{1,0:T(8,128)(2,1)} %get-tuple-element.45.refs_1_, f32[8192,1024]{1,0:T(8,128)} %bitcast.144, f32[8192,128]{1,0:T(8,128)} %collective-permute-done.8.refs_3_), custom_call_target="tpu_custom_call" | custom-call | tf_op jit(solution)/shard_map/product/pallas_call | solution.py:111
  235.9 6.1 collective-permute-done.11
  242.0 6.0 collective-permute-done.10
  250.7 2.5 collective-permute-start.14
  253.4 4.0 collective-permute-done.14
  260.6 26.0 %collective-permute-done.15.refs_3_ = f32[8192,128]{1,0:T(8,128)} collective-permute-done((f32[8192,128]{1,0:T(8,128)}, f32[8192,128]{1,0:T(8,128)}, u32[]{:S(2)}, u32[]{:S(2)}) %collective-permute-start.15) | collective-permute-done | bytes 4194336 | tf_op jit(solution)/shard_map/ppermute | solution.py:20
  286.6 30.5 %product.17 = f32[2048,128]{1,0:T(8,128)} custom-call(f32[1]{0:T(128)} %bitcast.sign_ref, bf16[2048,8192]{1,0:T(8,128)(2,1)} %get-tuple-element.44.refs_0_, bf16[2048,8192]{1,0:T(8,128)(2,1)} %get-tuple-element.45.refs_1_, f32[8192,1024]{1,0:T(8,128)} %bitcast.146, f32[8192,128]{1,0:T(8,128)} %collective-permute-done.15.refs_3_), custom_call_target="tpu_custom_call" | custom-call | tf_op jit(solution)/shard_map/product/pallas_call | solution.py:111
  322.6 6.1 collective-permute-done.18
  328.7 6.0 collective-permute-done.17
  337.4 2.5 collective-permute-start.21
  340.1 4.0 collective-permute-done.21
  346.2 30.3 %collective-permute-done.22.refs_3_ = f32[8192,128]{1,0:T(8,128)} collective-permute-done((f32[8192,128]{1,0:T(8,128)}, f32[8192,128]{1,0:T(8,128)}, u32[]{:S(2)}, u32[]{:S(2)}) %collective-permute-start.22) | collective-permute-done | bytes 4194336 | tf_op jit(solution)/shard_map/ppermute | solution.py:20
  376.5 2.1 collective-permute-start.36
  378.5 3.1 slice.52
  381.7 30.4 %product.18 = f32[2048,128]{1,0:T(8,128)} custom-call(f32[1]{0:T(128)} %bitcast.sign_ref, bf16[2048,8192]{1,0:T(8,128)(2,1)} %get-tuple-element.44.refs_0_, bf16[2048,8192]{1,0:T(8,128)(2,1)} %get-tuple-element.45.refs_1_, f32[8192,1024]{1,0:T(8,128)} %bitcast.148, f32[8192,128]{1,0:T(8,128)} %collective-permute-done.22.refs_3_), custom_call_target="tpu_custom_call" | custom-call | tf_op jit(solution)/shard_map/product/pallas_call | solution.py:111
  415.4 6.1 collective-permute-done.25
  421.6 6.0 collective-permute-done.24
  430.3 2.5 collective-permute-start.28
  433.0 4.0 collective-permute-done.28
  440.1 26.3 %collective-permute-done.29.refs_3_ = f32[8192,128]{1,0:T(8,128)} collective-permute-done((f32[8192,128]{1,0:T(8,128)}, f32[8192,128]{1,0:T(8,128)}, u32[]{:S(2)}, u32[]{:S(2)}) %collective-permute-start.29) | collective-permute-done | bytes 4194336 | tf_op jit(solution)/shard_map/ppermute | solution.py:20
  466.4 30.5 %product.19 = f32[2048,128]{1,0:T(8,128)} custom-call(f32[1]{0:T(128)} %bitcast.sign_ref, bf16[2048,8192]{1,0:T(8,128)(2,1)} %get-tuple-element.44.refs_0_, bf16[2048,8192]{1,0:T(8,128)(2,1)} %get-tuple-element.45.refs_1_, f32[8192,1024]{1,0:T(8,128)} %bitcast.150, f32[8192,128]{1,0:T(8,128)} %collective-permute-done.29.refs_3_), custom_call_target="tpu_custom_call" | custom-call | tf_op jit(solution)/shard_map/product/pallas_call | solution.py:111
  498.1 2.2 collective-permute-start.32
  500.4 6.6 collective-permute-done.32
  507.0 5.8 collective-permute-done.31
  515.7 2.5 collective-permute-start.35
  519.8 2.6 collective-permute-done.35
  524.4 31.8 %collective-permute-done.36.refs_3_ = f32[8192,128]{1,0:T(8,128)} collective-permute-done((f32[8192,128]{1,0:T(8,128)}, f32[8192,128]{1,0:T(8,128)}, u32[]{:S(2)}, u32[]{:S(2)}) %collective-permute-start.36) | collective-permute-done | bytes 4194336 | tf_op jit(solution)/shard_map/ppermute | solution.py:20
  560.0 30.9 %product.20 = f32[2048,128]{1,0:T(8,128)} custom-call(f32[1]{0:T(128)} %bitcast.sign_ref, bf16[2048,8192]{1,0:T(8,128)(2,1)} %get-tuple-element.44.refs_0_, bf16[2048,8192]{1,0:T(8,128)(2,1)} %get-tuple-element.45.refs_1_, f32[8192,1024]{1,0:T(8,128)} %bitcast.152, f32[8192,128]{1,0:T(8,128)} %collective-permute-done.36.refs_3_), custom_call_target="tpu_custom_call" | custom-call | tf_op jit(solution)/shard_map/product/pallas_call | solution.py:111
  594.3 6.1 collective-permute-done.39
  600.4 6.0 collective-permute-done.38
  609.1 2.5 collective-permute-start.42
  611.8 4.0 collective-permute-done.42
  620.2 16.9 %product.21.refs_4_ = f32[2048,128]{1,0:T(8,128)} custom-call(f32[1]{0:T(128)} %bitcast.sign_ref, bf16[2048,8192]{1,0:T(8,128)(2,1)} %get-tuple-element.44.refs_0_, bf16[2048,8192]{1,0:T(8,128)(2,1)} %get-tuple-element.45.refs_1_, f32[8192,1024]{1,0:T(8,128)} %bitcast.154, f32[4096,128]{1,0:T(8,128)} %copy-done), custom_call_target="tpu_custom_call" | custom-call | tf_op jit(solution)/shard_map/product/pallas_call | solution.py:111
  637.1 9.0 %collective-permute-done.43.refs_3_ = f32[4096,128]{1,0:T(8,128)} collective-permute-done((f32[4096,128]{1,0:T(8,128)}, f32[4096,128]{1,0:T(8,128)}, u32[]{:S(2)}, u32[]{:S(2)}) %collective-permute-start.43) | collective-permute-done | bytes 2097184 | tf_op jit(solution)/shard_map/ppermute | solution.py:20
  648.2 18.2 %product.22 = f32[2048,128]{1,0:T(8,128)} custom-call(f32[1]{0:T(128)} %bitcast.sign_ref, bf16[2048,8192]{1,0:T(8,128)(2,1)} %get-tuple-element.44.refs_0_, bf16[2048,8192]{1,0:T(8,128)(2,1)} %get-tuple-element.45.refs_1_, f32[8192,1024]{1,0:T(8,128)} %bitcast.155, f32[4096,128]{1,0:T(8,128)} %collective-permute-done.43.refs_3_, f32[2048,128]{1,0:T(8,128)} %product.21.refs_4_), custom_call_target="tpu_custom_call" | custom-call | tf_op jit(solution)/shard_map/product/pallas_call | solution.py:111
  670.0 6.1 collective-permute-done.48
  676.1 6.0 collective-permute-done.47
  684.8 2.5 collective-permute-start.51
  687.5 3.9 collective-permute-done.51
  691.4 2.1 collective-permute-done.50
  694.1 6.7 product.23.refs_4_
  704.3 18.2 %product.24.refs_4_ = f32[2048,128]{1,0:T(8,128)} custom-call(f32[1]{0:T(128)} %bitcast.sign_ref, bf16[2048,8192]{1,0:T(8,128)(2,1)} %get-tuple-element.44.refs_0_, bf16[2048,8192]{1,0:T(8,128)(2,1)} %get-tuple-element.45.refs_1_, f32[8192,1024]{1,0:T(8,128)} %bitcast.157, f32[4096,128]{1,0:T(8,128)} %copy-done.1, f32[2048,128]{1,0:T(8,128)} %product.23.refs_4_), custom_call_target="tpu_custom_call" | custom-call | tf_op jit(solution)/shard_map/product/pallas_call | solution.py:111
  723.8 6.9 product.25.refs_4_
  731.5 4.5 product.26.refs_4_
  736.7 4.5 product.27
  748.9 4.4 collective-permute-done.58
  755.3 2.7 collective-permute-start.63
  760.9 3.2 collective-permute-done.62
  (139 shorter events, 91.8 us)
Async XLA Ops:
  1.1 67.2 %collective-permute-start.1 = (f32[1024,128]{1,0:T(8,128)S(1)}, f32[1024,128]{1,0:T(8,128)S(1)}, u32[]{:S(2)}, u32[]{:S(2)}) collective-permute-start(f32[1024,128]{1,0:T(8,128)S(1)} %slice.56), channel_id=1, source_target_pairs={{0,16},{1,17},{2,18},{3,19},{4,20},{5,21},{6,22},{7,23},{8,24},{9,... | collective-permute-start | bytes 1572872 | tf_op jit(solution)/shard_map/ppermute | solution.py:20
  8.5 98.3 %collective-permute-start = (f32[8192,128]{1,0:T(8,128)}, f32[8192,128]{1,0:T(8,128)}, u32[]{:S(2)}, u32[]{:S(2)}) collective-permute-start(f32[8192,128]{1,0:T(8,128)} %slice.57), channel_id=1, source_target_pairs={{0,16},{1,17},{2,18},{3,19},{4,20},{5,21},{6,22},{7,23},{8,24},{9,... | collective-permute-start | bytes 12582920 | tf_op jit(solution)/shard_map/ppermute | solution.py:20
  68.3 128.4 %collective-permute-start.8 = (f32[8192,128]{1,0:T(8,128)}, f32[8192,128]{1,0:T(8,128)}, u32[]{:S(2)}, u32[]{:S(2)}) collective-permute-start(f32[8192,128]{1,0:T(8,128)} %get-tuple-element.54), channel_id=1, source_target_pairs={{0,16},{1,17},{2,18},{3,19},{4,20},{5,21},{6,22},{7,23},{8,24},{9,... | collective-permute-start | bytes 12582920 | tf_op jit(solution)/shard_map/ppermute | solution.py:20
  106.8 179.8 %collective-permute-start.15 = (f32[8192,128]{1,0:T(8,128)}, f32[8192,128]{1,0:T(8,128)}, u32[]{:S(2)}, u32[]{:S(2)}) collective-permute-start(f32[8192,128]{1,0:T(8,128)} %get-tuple-element.57), channel_id=1, source_target_pairs={{0,16},{1,17},{2,18},{3,19},{4,20},{5,21},{6,22},{7,23},{8,24},{9,... | collective-permute-start | bytes 12582920 | tf_op jit(solution)/shard_map/ppermute | solution.py:20
  143.4 2.2 collective-permute-start.2
  143.5 8.3 %collective-permute-start.4 = (f32[4,128,128]{2,1,0:T(8,128)S(1)}, f32[4,128,128]{2,1,0:T(8,128)S(1)}, u32[]{:S(2)}, u32[]{:S(2)}) collective-permute-start(f32[4,128,128]{2,1,0:T(8,128)S(1)} %get-tuple-element.119), channel_id=1, source_target_pairs={{0,3},{1,2},{2,1},{3,0},{4,7},{5,6},{6,5},{7,4},{8,11},{9,10},{10,... | collective-permute-start | bytes 786440 | tf_op jit(solution)/shard_map/ppermute | solution.py:20
  145.1 12.7 %collective-permute-start.3 = (f32[4,128,128]{2,1,0:T(8,128)S(1)}, f32[4,128,128]{2,1,0:T(8,128)S(1)}, u32[]{:S(2)}, u32[]{:S(2)}) collective-permute-start(f32[4,128,128]{2,1,0:T(8,128)S(1)} %get-tuple-element.120), channel_id=1, source_target_pairs={{0,2},{1,3},{2,0},{3,1},{4,6},{5,7},{6,4},{7,5},{8,10},{9,11},{10,... | collective-permute-start | bytes 786440 | tf_op jit(solution)/shard_map/ppermute | solution.py:20
  158.8 4.3 collective-permute-start.5
  160.5 6.7 collective-permute-start.7
  163.0 6.3 collective-permute-start.6
  196.7 179.8 %collective-permute-start.22 = (f32[8192,128]{1,0:T(8,128)}, f32[8192,128]{1,0:T(8,128)}, u32[]{:S(2)}, u32[]{:S(2)}) collective-permute-start(f32[8192,128]{1,0:T(8,128)} %get-tuple-element.60), channel_id=1, source_target_pairs={{0,16},{1,17},{2,18},{3,19},{4,20},{5,21},{6,22},{7,23},{8,24},{9,... | collective-permute-start | bytes 12582920 | tf_op jit(solution)/shard_map/ppermute | solution.py:20
  233.7 2.2 collective-permute-start.9
  233.8 8.3 %collective-permute-start.11 = (f32[4,128,128]{2,1,0:T(8,128)S(1)}, f32[4,128,128]{2,1,0:T(8,128)S(1)}, u32[]{:S(2)}, u32[]{:S(2)}) collective-permute-start(f32[4,128,128]{2,1,0:T(8,128)S(1)} %get-tuple-element.116), channel_id=1, source_target_pairs={{0,3},{1,2},{2,1},{3,0},{4,7},{5,6},{6,5},{7,4},{8,11},{9,10},{10,... | collective-permute-start | bytes 786440 | tf_op jit(solution)/shard_map/ppermute | solution.py:20
  235.4 12.7 %collective-permute-start.10 = (f32[4,128,128]{2,1,0:T(8,128)S(1)}, f32[4,128,128]{2,1,0:T(8,128)S(1)}, u32[]{:S(2)}, u32[]{:S(2)}) collective-permute-start(f32[4,128,128]{2,1,0:T(8,128)S(1)} %get-tuple-element.117), channel_id=1, source_target_pairs={{0,2},{1,3},{2,0},{3,1},{4,6},{5,7},{6,4},{7,5},{8,10},{9,11},{10,... | collective-permute-start | bytes 786440 | tf_op jit(solution)/shard_map/ppermute | solution.py:20
  249.1 4.3 collective-permute-start.12
  250.7 6.7 collective-permute-start.14
  253.2 6.3 collective-permute-start.13
  317.1 149.2 %collective-permute-start.29 = (f32[8192,128]{1,0:T(8,128)}, f32[8192,128]{1,0:T(8,128)}, u32[]{:S(2)}, u32[]{:S(2)}) collective-permute-start(f32[8192,128]{1,0:T(8,128)} %get-tuple-element.63), channel_id=1, source_target_pairs={{0,16},{1,17},{2,18},{3,19},{4,20},{5,21},{6,22},{7,23},{8,24},{9,... | collective-permute-start | bytes 12582920 | tf_op jit(solution)/shard_map/ppermute | solution.py:20
  320.3 2.2 collective-permute-start.16
  320.4 8.3 %collective-permute-start.18 = (f32[4,128,128]{2,1,0:T(8,128)S(1)}, f32[4,128,128]{2,1,0:T(8,128)S(1)}, u32[]{:S(2)}, u32[]{:S(2)}) collective-permute-start(f32[4,128,128]{2,1,0:T(8,128)S(1)} %get-tuple-element.113), channel_id=1, source_target_pairs={{0,3},{1,2},{2,1},{3,0},{4,7},{5,6},{6,5},{7,4},{8,11},{9,10},{10,... | collective-permute-start | bytes 786440 | tf_op jit(solution)/shard_map/ppermute | solution.py:20
  322.1 12.6 %collective-permute-start.17 = (f32[4,128,128]{2,1,0:T(8,128)S(1)}, f32[4,128,128]{2,1,0:T(8,128)S(1)}, u32[]{:S(2)}, u32[]{:S(2)}) collective-permute-start(f32[4,128,128]{2,1,0:T(8,128)S(1)} %get-tuple-element.114), channel_id=1, source_target_pairs={{0,2},{1,3},{2,0},{3,1},{4,6},{5,7},{6,4},{7,5},{8,10},{9,11},{10,... | collective-permute-start | bytes 786440 | tf_op jit(solution)/shard_map/ppermute | solution.py:20
  335.8 4.3 collective-permute-start.19
  337.4 6.7 collective-permute-start.21
  339.9 6.3 collective-permute-start.20
  376.5 179.8 %collective-permute-start.36 = (f32[8192,128]{1,0:T(8,128)}, f32[8192,128]{1,0:T(8,128)}, u32[]{:S(2)}, u32[]{:S(2)}) collective-permute-start(f32[8192,128]{1,0:T(8,128)} %get-tuple-element.66), channel_id=1, source_target_pairs={{0,16},{1,17},{2,18},{3,19},{4,20},{5,21},{6,22},{7,23},{8,24},{9,... | collective-permute-start | bytes 12582920 | tf_op jit(solution)/shard_map/ppermute | solution.py:20
  413.2 2.2 collective-permute-start.23
  413.3 8.3 %collective-permute-start.25 = (f32[4,128,128]{2,1,0:T(8,128)S(1)}, f32[4,128,128]{2,1,0:T(8,128)S(1)}, u32[]{:S(2)}, u32[]{:S(2)}) collective-permute-start(f32[4,128,128]{2,1,0:T(8,128)S(1)} %get-tuple-element.110), channel_id=1, source_target_pairs={{0,3},{1,2},{2,1},{3,0},{4,7},{5,6},{6,5},{7,4},{8,11},{9,10},{10,... | collective-permute-start | bytes 786440 | tf_op jit(solution)/shard_map/ppermute | solution.py:20
  414.9 12.6 %collective-permute-start.24 = (f32[4,128,128]{2,1,0:T(8,128)S(1)}, f32[4,128,128]{2,1,0:T(8,128)S(1)}, u32[]{:S(2)}, u32[]{:S(2)}) collective-permute-start(f32[4,128,128]{2,1,0:T(8,128)S(1)} %get-tuple-element.111), channel_id=1, source_target_pairs={{0,2},{1,3},{2,0},{3,1},{4,6},{5,7},{6,4},{7,5},{8,10},{9,11},{10,... | collective-permute-start | bytes 786440 | tf_op jit(solution)/shard_map/ppermute | solution.py:20
  428.6 4.3 collective-permute-start.26
  430.3 6.7 collective-permute-start.28
  432.8 6.2 collective-permute-start.27
  498.0 2.3 collective-permute-start.30
  498.1 8.9 %collective-permute-start.32 = (f32[4,128,128]{2,1,0:T(8,128)S(1)}, f32[4,128,128]{2,1,0:T(8,128)S(1)}, u32[]{:S(2)}, u32[]{:S(2)}) collective-permute-start(f32[4,128,128]{2,1,0:T(8,128)S(1)} %get-tuple-element.107), channel_id=1, source_target_pairs={{0,3},{1,2},{2,1},{3,0},{4,7},{5,6},{6,5},{7,4},{8,11},{9,10},{10,... | collective-permute-start | bytes 786440 | tf_op jit(solution)/shard_map/ppermute | solution.py:20
  500.3 12.5 %collective-permute-start.31 = (f32[4,128,128]{2,1,0:T(8,128)S(1)}, f32[4,128,128]{2,1,0:T(8,128)S(1)}, u32[]{:S(2)}, u32[]{:S(2)}) collective-permute-start(f32[4,128,128]{2,1,0:T(8,128)S(1)} %get-tuple-element.108), channel_id=1, source_target_pairs={{0,2},{1,3},{2,0},{3,1},{4,6},{5,7},{6,4},{7,5},{8,10},{9,11},{10,... | collective-permute-start | bytes 786440 | tf_op jit(solution)/shard_map/ppermute | solution.py:20
  513.9 5.9 collective-permute-start.33
  515.7 6.7 collective-permute-start.35
  518.1 6.3 collective-permute-start.34
  518.3 99.6 %collective-permute-start.44 = (f32[4096,128]{1,0:T(8,128)}, f32[4096,128]{1,0:T(8,128)S(1)}, u32[]{:S(2)}, u32[]{:S(2)}) collective-permute-start(f32[4096,128]{1,0:T(8,128)} %slice.49), channel_id=1, source_target_pairs={{0,16},{1,17},{2,18},{3,19},{4,20},{5,21},{6,22},{7,23},{8,24},{9,... | collective-permute-start | bytes 6291464 | tf_op jit(solution)/shard_map/ppermute | solution.py:20
  556.2 89.9 %collective-permute-start.43 = (f32[4096,128]{1,0:T(8,128)}, f32[4096,128]{1,0:T(8,128)}, u32[]{:S(2)}, u32[]{:S(2)}) collective-permute-start(f32[4096,128]{1,0:T(8,128)} %slice.50), channel_id=1, source_target_pairs={{0,16},{1,17},{2,18},{3,19},{4,20},{5,21},{6,22},{7,23},{8,24},{9,... | collective-permute-start | bytes 6291464 | tf_op jit(solution)/shard_map/ppermute | solution.py:20
  592.0 2.2 collective-permute-start.37
  592.1 8.3 %collective-permute-start.39 = (f32[4,128,128]{2,1,0:T(8,128)S(1)}, f32[4,128,128]{2,1,0:T(8,128)S(1)}, u32[]{:S(2)}, u32[]{:S(2)}) collective-permute-start(f32[4,128,128]{2,1,0:T(8,128)S(1)} %get-tuple-element.104), channel_id=1, source_target_pairs={{0,3},{1,2},{2,1},{3,0},{4,7},{5,6},{6,5},{7,4},{8,11},{9,10},{10,... | collective-permute-start | bytes 786440 | tf_op jit(solution)/shard_map/ppermute | solution.py:20
  593.7 12.7 %collective-permute-start.38 = (f32[4,128,128]{2,1,0:T(8,128)S(1)}, f32[4,128,128]{2,1,0:T(8,128)S(1)}, u32[]{:S(2)}, u32[]{:S(2)}) collective-permute-start(f32[4,128,128]{2,1,0:T(8,128)S(1)} %get-tuple-element.105), channel_id=1, source_target_pairs={{0,2},{1,3},{2,0},{3,1},{4,6},{5,7},{6,4},{7,5},{8,10},{9,11},{10,... | collective-permute-start | bytes 786440 | tf_op jit(solution)/shard_map/ppermute | solution.py:20
  607.5 4.3 collective-permute-start.40
  609.1 6.7 collective-permute-start.42
  611.6 6.3 collective-permute-start.41
  617.9 48.5 %collective-permute-start.45 = (f32[1024,128]{1,0:T(8,128)S(1)}, f32[1024,128]{1,0:T(8,128)S(1)}, u32[]{:S(2)}, u32[]{:S(2)}) collective-permute-start(f32[1024,128]{1,0:T(8,128)S(1)} %slice.51), channel_id=1, source_target_pairs={{0,16},{1,17},{2,18},{3,19},{4,20},{5,21},{6,22},{7,23},{8,24},{9,... | collective-permute-start | bytes 1572872 | tf_op jit(solution)/shard_map/ppermute | solution.py:20
  646.1 56.1 %collective-permute-start.53 = (f32[4096,128]{1,0:T(8,128)}, f32[4096,128]{1,0:T(8,128)S(1)}, u32[]{:S(2)}, u32[]{:S(2)}) collective-permute-start(f32[4096,128]{1,0:T(8,128)} %slice.52), channel_id=1, source_target_pairs={{0,16},{1,17},{2,18},{3,19},{4,20},{5,21},{6,22},{7,23},{8,24},{9,... | collective-permute-start | bytes 6291464 | tf_op jit(solution)/shard_map/ppermute | solution.py:20
  667.7 2.2 collective-permute-start.46
  667.8 8.3 %collective-permute-start.48 = (f32[4,128,128]{2,1,0:T(8,128)S(1)}, f32[4,128,128]{2,1,0:T(8,128)S(1)}, u32[]{:S(2)}, u32[]{:S(2)}) collective-permute-start(f32[4,128,128]{2,1,0:T(8,128)S(1)} %get-tuple-element.101), channel_id=1, source_target_pairs={{0,3},{1,2},{2,1},{3,0},{4,7},{5,6},{6,5},{7,4},{8,11},{9,10},{10,... | collective-permute-start | bytes 786440 | tf_op jit(solution)/shard_map/ppermute | solution.py:20
  669.5 12.7 %collective-permute-start.47 = (f32[4,128,128]{2,1,0:T(8,128)S(1)}, f32[4,128,128]{2,1,0:T(8,128)S(1)}, u32[]{:S(2)}, u32[]{:S(2)}) collective-permute-start(f32[4,128,128]{2,1,0:T(8,128)S(1)} %get-tuple-element.102), channel_id=1, source_target_pairs={{0,2},{1,3},{2,0},{3,1},{4,6},{5,7},{6,4},{7,5},{8,10},{9,11},{10,... | collective-permute-start | bytes 786440 | tf_op jit(solution)/shard_map/ppermute | solution.py:20
  683.2 4.3 collective-permute-start.49
  684.8 6.6 collective-permute-start.51
  687.3 6.2 collective-permute-start.50
  693.5 28.9 %collective-permute-start.52 = (f32[1024,128]{1,0:T(8,128)S(1)}, f32[1024,128]{1,0:T(8,128)S(1)}, u32[]{:S(2)}, u32[]{:S(2)}) collective-permute-start(f32[1024,128]{1,0:T(8,128)S(1)} %slice.53), channel_id=1, source_target_pairs={{0,16},{1,17},{2,18},{3,19},{4,20},{5,21},{6,22},{7,23},{8,24},{9,... | collective-permute-start | bytes 1572872 | tf_op jit(solution)/shard_map/ppermute | solution.py:20
  702.2 28.6 %collective-permute-start.56 = (f32[512,128]{1,0:T(8,128)}, f32[512,128]{1,0:T(8,128)S(1)}, u32[]{:S(2)}, u32[]{:S(2)}) collective-permute-start(f32[512,128]{1,0:T(8,128)} %slice.54), channel_id=1, source_target_pairs={{0,16},{1,17},{2,18},{3,19},{4,20},{5,21},{6,22},{7,23},{8,24},{9,... | collective-permute-start | bytes 786440 | tf_op jit(solution)/shard_map/ppermute | solution.py:20
  722.4 13.5 %collective-permute-start.54 = (f32[512,128]{1,0:T(8,128)}, f32[512,128]{1,0:T(8,128)S(1)}, u32[]{:S(2)}, u32[]{:S(2)}) collective-permute-start(f32[512,128]{1,0:T(8,128)} %slice.55), channel_id=1, source_target_pairs={{0,16},{1,17},{2,18},{3,19},{4,20},{5,21},{6,22},{7,23},{8,24},{9,... | collective-permute-start | bytes 786440 | tf_op jit(solution)/shard_map/ppermute | solution.py:20
  742.2 2.0 collective-permute-start.57
  742.3 12.9 %collective-permute-start.55 = (f32[128,896]{1,0:T(8,128)S(1)}, f32[128,896]{1,0:T(8,128)S(1)}, u32[]{:S(2)}, u32[]{:S(2)}) collective-permute-start(f32[128,896]{1,0:T(8,128)S(1)} %constant_dynamic-update-slice_fusion), channel_id=1, source_target_pairs={{0,16},{1,17},{2,18},{3,19},{4,20},{5,21},{6,22},{7,23},{8,24},{9,... | collective-permute-start | bytes 1376264 | tf_op jit(solution)/shard_map/ppermute | solution.py:20
  745.4 8.0 %collective-permute-start.58 = (f32[2,128,128]{2,1,0:T(8,128)S(1)}, f32[2,128,128]{2,1,0:T(8,128)S(1)}, u32[]{:S(2)}, u32[]{:S(2)}) collective-permute-start(f32[2,128,128]{2,1,0:T(8,128)S(1)} %get-tuple-element.121), channel_id=1, source_target_pairs={{0,2},{1,3},{2,0},{3,1},{4,6},{5,7},{6,4},{7,5},{8,10},{9,11},{10,... | collective-permute-start | bytes 393224 | tf_op jit(solution)/shard_map/ppermute | solution.py:20
  747.0 7.3 collective-permute-start.60
  748.5 6.5 collective-permute-start.59
  755.3 5.6 collective-permute-start.63
  757.9 6.2 collective-permute-start.62
  758.4 5.7 collective-permute-start.61
  (7 other events, 37.1 us)

commit v2 on v1

--- a/solution.py
+++ b/solution.py
@@ -115,6 +115,7 @@
         out_specs=out_spec,
         out_shape=jax.ShapeDtypeStruct((rows, width), jnp.float32),
         scratch_shapes=[pltpu.VMEM((depth, 2 * width), jnp.bfloat16)],
+        input_output_aliases={} if total is None else {5: 0},
         compiler_params=pltpu.CompilerParams(vmem_limit_bytes=VMEM_BYTES),
         cost_estimate=pl.CostEstimate(flops=0, bytes_accessed=0, transcendentals=0),
         name="product",
@@ -123,12 +124,14 @@
 
 def pieces_of(depth, vectors):
     last = vectors // LANES - 1
-    least = max(LANES, depth // 8)
+    least = max(LANES, depth // 16)
     pieces = [(last, 0, least)] + [(chunk, 0, depth) for chunk in range(last - 1)]
     pieces += [(last - 1, 0, depth // 2), (last - 1, depth // 2, depth // 2)]
-    pieces += [(last, least, least), (last, depth // 2, depth // 2), (last, 2 * least, least)]
-    half = max(LANES, least // 2)
-    return pieces + [(last, start, half) for start in range(3 * least, depth // 2, half)]
+    size = depth // 2
+    while size >= least:
+        pieces.append((last, size, size))
+        size //= 2
+    return pieces
 
 
 def shards(tiles, trial):
@@ -151,7 +154,7 @@
     blocks = {index: block(index) for index in range(ahead)}
     arrived = [swapped(blocks[index], pair) for index in range(ahead)]
     high, low = split_matrix(after(matrix, *blocks.values()))
-    totals, covered, sums = {}, {}, {}
+    totals, covered, waiting, sums = {}, {}, [], []
     done = high
     for index, (chunk, start, size) in enumerate(pieces):
         partner = arrived[index]
@@ -165,12 +168,14 @@
         totals[chunk] = done
         covered[chunk] = covered.get(chunk, 0) + size
         if covered[chunk] == depth and index + 1 < len(pieces):
-            if pieces[index + 1][0] == pieces[-1][0]:
-                done = after(done, arrived[index + 1])
-            steps = [2] * (bits // 2) + [1] * (bits % 2)
-            done = sums[chunk] = scattered_sum(by_owner(done), 0, steps)[0]
+            waiting.append(by_owner(done))
+            if len(waiting) == 2 or chunk == pieces[-1][0] - 1:
+                steps = [2] * (bits // 2) + [1] * (bits % 2)
+                done = scattered_sum(jnp.concatenate(waiting, axis=-1), 0, steps)[0]
+                sums.append(done)
+                waiting = []
 
-    early = jnp.concatenate([sums[chunk] for chunk in sorted(sums)], axis=1)
+    early = jnp.concatenate(sums, axis=1)
     early_partner = swapped(after(early, arrived[-1]), pair)
     steps = [1] + [2] * ((bits - 2) // 2) + [1] * (bits % 2)
     late = after(scattered_sum(by_owner(done), 0, steps), early_partner)

time: 774 us -> 759 us (0.981)
  waiting for transfers between devices: 321 us -> 353 us
  starting transfers between devices: 77.9 us -> 46.2 us
    ppermute x64 -> x45, waiting for transfers between devices: 321 us -> 353 us  [swapped(): lax.ppermute(value, AXES, [(source, source ^ mask) for source in range(de...]
    ppermute x64 -> x45, starting transfers between devices: 77.9 us -> 46.2 us  [swapped(): lax.ppermute(value, AXES, [(source, source ^ mask) for source in range(de...]
    pallas_call x14 -> x13, Pallas kernels: 265 us -> 262 us  [product(): pl.pallas_call(functools.partial(product_kernel, total is not None), grid...]
    slice x10 -> x9, local copies, waits for them, and re-layouts: 35.1 us -> 35.1 us  [block(): return source[start:start + size, chunk * LANES:(chunk + 1) * LANES]]
  transfers between devices with their start and end apart: 64 -> 45, of which waited for: 49 -> 35; matrix products, arithmetic and copies ran while one was open for 7% -> 6% of each run, Pallas kernels for 40% -> 40%
where the time goes in v2:
time: 759 us; the launch traced here: 758 us
  waiting for transfers between devices  353 us (47%)
  Pallas kernels  307 us (40%)
  starting transfers between devices  46.2 us (6%)
  local copies, waits for them, and re-layouts  40.3 us (5%)
  other arithmetic  10.7 us (1%)
    ppermute x45, waiting for transfers between devices, swapped(): lax.ppermute(value, AXES, [(source, source ^ mask) for source in range(de...  353 us
    pallas_call x13, Pallas kernels, product(): pl.pallas_call(functools.partial(product_kernel, total is not None), grid...  262 us
    ppermute x45, starting transfers between devices, swapped(): lax.ppermute(value, AXES, [(source, source ^ mask) for source in range(de...  46.2 us
    pallas_call x1, Pallas kernels, split_matrix(): pl.pallas_call(split_kernel, grid=(rows // step,), in_specs=[spec], out_s...  44.9 us
    slice x9, local copies, waits for them, and re-layouts, block(): return source[start:start + size, chunk * LANES:(chunk + 1) * LANES]  35.1 us
  transfers between devices with their start and end apart: 45, of which 35 were waited for; matrix products, arithmetic and copies ran while one was open for 6% of the time, Pallas kernels for 40%

profile of v2, /device:TPU:0, one launch (start us, length us, event | category | flops | bytes accessed | tf_op | source)
XLA Modules:
  0.0 757.7 jit_solution(12405471768101966155)
XLA Ops:
  1.0 3.0 collective-permute-start.1
  4.0 4.5 slice.53
  8.5 44.9 %split_matrix.1 = (bf16[2048,8192]{1,0:T(8,128)(2,1)}, bf16[2048,8192]{1,0:T(8,128)(2,1)}) custom-call(f32[2048,8192]{1,0:T(8,128)} %bitcast.1.matrix_ref), custom_call_target="tpu_custom_call" | custom-call | bytes 134217728 | tf_op jit(solution)/shard_map/split_matrix/pallas_call | solution.py:64
  53.3 15.2 %fusion.37 = (f32[8192,128]{1,0:T(8,128)}, f32[8192,128]{1,0:T(8,128)}, f32[8192,128]{1,0:T(8,128)}, f32[8192,128]{1,0:T(8,128)}, f32[8192,128]{1,0:T(8,128)}) fusion(f32[8192,1024]{1,0:T(8,128)} %bitcast.96), kind=kLoop, calls=%fused_computation.93 | loop fusion | bytes 41943040 | tf_op jit(solution)/shard_map/slice | solution.py:151
  68.6 2.1 collective-permute-start.2
  70.6 4.0 product.13.refs_4_
  74.6 27.6 %collective-permute-done.refs_3_ = f32[8192,128]{1,0:T(8,128)} collective-permute-done((f32[8192,128]{1,0:T(8,128)}, f32[8192,128]{1,0:T(8,128)}, u32[]{:S(2)}, u32[]{:S(2)}) %collective-permute-start) | collective-permute-done | bytes 4194336 | tf_op jit(solution)/shard_map/ppermute | solution.py:20
  102.9 3.0 slice.46
  105.9 30.3 %product.14 = f32[2048,128]{1,0:T(8,128)} custom-call(f32[1]{0:T(128)} %bitcast.sign_ref, bf16[2048,8192]{1,0:T(8,128)(2,1)} %get-tuple-element.40.refs_0_, bf16[2048,8192]{1,0:T(8,128)(2,1)} %get-tuple-element.41.refs_1_, f32[8192,1024]{1,0:T(8,128)} %bitcast.99, f32[8192,128]{1,0:T(8,128)} %collective-permute-done.refs_3_), custom_call_target="tpu_custom_call" | custom-call | tf_op jit(solution)/shard_map/product/pallas_call | solution.py:111
  136.3 55.9 %collective-permute-done.2.refs_3_ = f32[8192,128]{1,0:T(8,128)} collective-permute-done((f32[8192,128]{1,0:T(8,128)}, f32[8192,128]{1,0:T(8,128)}, u32[]{:S(2)}, u32[]{:S(2)}) %collective-permute-start.2) | collective-permute-done | bytes 4194336 | tf_op jit(solution)/shard_map/ppermute | solution.py:20
  192.7 3.0 slice.47
  195.8 30.4 %product.15 = f32[2048,128]{1,0:T(8,128)} custom-call(f32[1]{0:T(128)} %bitcast.sign_ref, bf16[2048,8192]{1,0:T(8,128)(2,1)} %get-tuple-element.40.refs_0_, bf16[2048,8192]{1,0:T(8,128)(2,1)} %get-tuple-element.41.refs_1_, f32[8192,1024]{1,0:T(8,128)} %bitcast.101, f32[8192,128]{1,0:T(8,128)} %collective-permute-done.2.refs_3_), custom_call_target="tpu_custom_call" | custom-call | tf_op jit(solution)/shard_map/product/pallas_call | solution.py:111
  226.2 2.4 fusion.30
  230.7 12.8 %collective-permute-done.4 = f32[4,128,256]{2,1,0:T(8,128)S(1)} collective-permute-done((f32[4,128,256]{2,1,0:T(8,128)}, f32[4,128,256]{2,1,0:T(8,128)S(1)}, u32[]{:S(2)}, u32[]{:S(2)}) %collective-permute-start.4) | collective-permute-done | bytes 524320 | tf_op jit(solution)/shard_map/ppermute | solution.py:20
  244.3 9.8 %collective-permute-done.5 = f32[4,128,256]{2,1,0:T(8,128)} collective-permute-done((f32[4,128,256]{2,1,0:T(8,128)}, f32[4,128,256]{2,1,0:T(8,128)}, u32[]{:S(2)}, u32[]{:S(2)}) %collective-permute-start.5) | collective-permute-done | bytes 524320 | tf_op jit(solution)/shard_map/ppermute | solution.py:20
  255.5 1.6 collective-permute-start.6
  257.0 2.5 collective-permute-start.8
  259.6 1.8 collective-permute-done.6
  261.4 5.2 collective-permute-done.8
  266.7 5.2 collective-permute-done.7
  272.6 9.4 %collective-permute-done.9.refs_3_ = f32[8192,128]{1,0:T(8,128)} collective-permute-done((f32[8192,128]{1,0:T(8,128)}, f32[8192,128]{1,0:T(8,128)}, u32[]{:S(2)}, u32[]{:S(2)}) %collective-permute-start.9) | collective-permute-done | bytes 4194336 | tf_op jit(solution)/shard_map/ppermute | solution.py:20
  282.6 3.2 slice.48
  285.9 30.4 %product.16 = f32[2048,128]{1,0:T(8,128)} custom-call(f32[1]{0:T(128)} %bitcast.sign_ref, bf16[2048,8192]{1,0:T(8,128)(2,1)} %get-tuple-element.40.refs_0_, bf16[2048,8192]{1,0:T(8,128)(2,1)} %get-tuple-element.41.refs_1_, f32[8192,1024]{1,0:T(8,128)} %bitcast.103, f32[8192,128]{1,0:T(8,128)} %collective-permute-done.9.refs_3_), custom_call_target="tpu_custom_call" | custom-call | tf_op jit(solution)/shard_map/product/pallas_call | solution.py:111
  316.2 55.7 %collective-permute-done.10.refs_3_ = f32[8192,128]{1,0:T(8,128)} collective-permute-done((f32[8192,128]{1,0:T(8,128)}, f32[8192,128]{1,0:T(8,128)}, u32[]{:S(2)}, u32[]{:S(2)}) %collective-permute-start.10) | collective-permute-done | bytes 4194336 | tf_op jit(solution)/shard_map/ppermute | solution.py:20
  372.5 2.3 slice.49
  374.8 30.4 %product.17 = f32[2048,128]{1,0:T(8,128)} custom-call(f32[1]{0:T(128)} %bitcast.sign_ref, bf16[2048,8192]{1,0:T(8,128)(2,1)} %get-tuple-element.40.refs_0_, bf16[2048,8192]{1,0:T(8,128)(2,1)} %get-tuple-element.41.refs_1_, f32[8192,1024]{1,0:T(8,128)} %bitcast.105, f32[8192,128]{1,0:T(8,128)} %collective-permute-done.10.refs_3_), custom_call_target="tpu_custom_call" | custom-call | tf_op jit(solution)/shard_map/product/pallas_call | solution.py:111
  408.5 12.9 %collective-permute-done.12 = f32[4,128,256]{2,1,0:T(8,128)S(1)} collective-permute-done((f32[4,128,256]{2,1,0:T(8,128)S(1)}, f32[4,128,256]{2,1,0:T(8,128)S(1)}, u32[]{:S(2)}, u32[]{:S(2)}) %collective-permute-start.12) | collective-permute-done | bytes 524320 | tf_op jit(solution)/shard_map/ppermute | solution.py:20
  421.4 10.3 %collective-permute-done.13 = f32[4,128,256]{2,1,0:T(8,128)S(1)} collective-permute-done((f32[4,128,256]{2,1,0:T(8,128)S(1)}, f32[4,128,256]{2,1,0:T(8,128)S(1)}, u32[]{:S(2)}, u32[]{:S(2)}) %collective-permute-start.13) | collective-permute-done | bytes 524320 | tf_op jit(solution)/shard_map/ppermute | solution.py:20
  431.9 1.6 collective-permute-start.14
  433.5 2.5 collective-permute-start.16
  436.1 2.0 collective-permute-done.14
  438.1 5.1 collective-permute-done.16
  443.2 5.4 collective-permute-done.15
  449.3 12.5 %collective-permute-done.17.refs_3_ = f32[8192,128]{1,0:T(8,128)} collective-permute-done((f32[8192,128]{1,0:T(8,128)}, f32[8192,128]{1,0:T(8,128)}, u32[]{:S(2)}, u32[]{:S(2)}) %collective-permute-start.17) | collective-permute-done | bytes 4194336 | tf_op jit(solution)/shard_map/ppermute | solution.py:20
  462.4 1.9 slice.50
  464.3 30.4 %product.18 = f32[2048,128]{1,0:T(8,128)} custom-call(f32[1]{0:T(128)} %bitcast.sign_ref, bf16[2048,8192]{1,0:T(8,128)(2,1)} %get-tuple-element.40.refs_0_, bf16[2048,8192]{1,0:T(8,128)(2,1)} %get-tuple-element.41.refs_1_, f32[8192,1024]{1,0:T(8,128)} %bitcast.107, f32[8192,128]{1,0:T(8,128)} %collective-permute-done.17.refs_3_), custom_call_target="tpu_custom_call" | custom-call | tf_op jit(solution)/shard_map/product/pallas_call | solution.py:111
  495.6 56.1 %collective-permute-done.18.refs_3_ = f32[8192,128]{1,0:T(8,128)} collective-permute-done((f32[8192,128]{1,0:T(8,128)}, f32[8192,128]{1,0:T(8,128)}, u32[]{:S(2)}, u32[]{:S(2)}) %collective-permute-start.18) | collective-permute-done | bytes 4194336 | tf_op jit(solution)/shard_map/ppermute | solution.py:20
  551.7 30.5 %product.19 = f32[2048,128]{1,0:T(8,128)} custom-call(f32[1]{0:T(128)} %bitcast.sign_ref, bf16[2048,8192]{1,0:T(8,128)(2,1)} %get-tuple-element.40.refs_0_, bf16[2048,8192]{1,0:T(8,128)(2,1)} %get-tuple-element.41.refs_1_, f32[8192,1024]{1,0:T(8,128)} %bitcast.109, f32[8192,128]{1,0:T(8,128)} %collective-permute-done.18.refs_3_), custom_call_target="tpu_custom_call" | custom-call | tf_op jit(solution)/shard_map/product/pallas_call | solution.py:111
  583.6 1.6 collective-permute-start.20
  586.1 12.3 %collective-permute-done.20 = f32[4,128,256]{2,1,0:T(8,128)S(1)} collective-permute-done((f32[4,128,256]{2,1,0:T(8,128)S(1)}, f32[4,128,256]{2,1,0:T(8,128)S(1)}, u32[]{:S(2)}, u32[]{:S(2)}) %collective-permute-start.20) | collective-permute-done | bytes 524320 | tf_op jit(solution)/shard_map/ppermute | solution.py:20
  598.4 10.3 %collective-permute-done.21 = f32[4,128,256]{2,1,0:T(8,128)S(1)} collective-permute-done((f32[4,128,256]{2,1,0:T(8,128)S(1)}, f32[4,128,256]{2,1,0:T(8,128)S(1)}, u32[]{:S(2)}, u32[]{:S(2)}) %collective-permute-start.21) | collective-permute-done | bytes 524320 | tf_op jit(solution)/shard_map/ppermute | solution.py:20
  608.9 1.6 collective-permute-start.22
  610.6 2.5 collective-permute-start.24
  613.2 1.9 collective-permute-done.22
  615.1 5.2 collective-permute-done.24
  620.3 5.3 collective-permute-done.23
  626.9 16.8 %product.20.refs_4_ = f32[2048,128]{1,0:T(8,128)} custom-call(f32[1]{0:T(128)} %bitcast.sign_ref, bf16[2048,8192]{1,0:T(8,128)(2,1)} %get-tuple-element.40.refs_0_, bf16[2048,8192]{1,0:T(8,128)(2,1)} %get-tuple-element.41.refs_1_, f32[8192,1024]{1,0:T(8,128)} %bitcast.110, f32[4096,128]{1,0:T(8,128)} %collective-permute-done.26.refs_3_), custom_call_target="tpu_custom_call" | custom-call | tf_op jit(solution)/shard_map/product/pallas_call | solution.py:111
  643.7 18.2 %product.21 = f32[2048,128]{1,0:T(8,128)} custom-call(f32[1]{0:T(128)} %bitcast.sign_ref, bf16[2048,8192]{1,0:T(8,128)(2,1)} %get-tuple-element.40.refs_0_, bf16[2048,8192]{1,0:T(8,128)(2,1)} %get-tuple-element.41.refs_1_, f32[8192,1024]{1,0:T(8,128)} %bitcast.111, f32[4096,128]{1,0:T(8,128)} %collective-permute-done.25.refs_3_, ...), custom_call_target="tpu_custom_call", output_to_operand_aliasing={{}: (5, {})} | custom-call | tf_op jit(solution)/shard_map/product/pallas_call | solution.py:111
  663.1 1.6 collective-permute-start.29
  666.7 4.6 collective-permute-done.29
  671.4 6.0 collective-permute-done.28
  678.5 2.7 collective-permute-start.32
  683.2 1.9 collective-permute-done.32
  685.1 2.8 collective-permute-done.31
  687.9 1.5 collective-permute-start.37
  689.4 18.2 %product.22.refs_4_ = f32[2048,128]{1,0:T(8,128)} custom-call(f32[1]{0:T(128)} %bitcast.sign_ref, bf16[2048,8192]{1,0:T(8,128)(2,1)} %get-tuple-element.40.refs_0_, bf16[2048,8192]{1,0:T(8,128)(2,1)} %get-tuple-element.41.refs_1_, f32[8192,1024]{1,0:T(8,128)} %bitcast.112, f32[4096,128]{1,0:T(8,128)} %copy-done.7, ...), custom_call_target="tpu_custom_call", output_to_operand_aliasing={{}: (5, {})} | custom-call | tf_op jit(solution)/shard_map/product/pallas_call | solution.py:111
  709.9 11.1 %product.23.refs_4_ = f32[2048,128]{1,0:T(8,128)} custom-call(f32[1]{0:T(128)} %bitcast.sign_ref, bf16[2048,8192]{1,0:T(8,128)(2,1)} %get-tuple-element.40.refs_0_, bf16[2048,8192]{1,0:T(8,128)(2,1)} %get-tuple-element.41.refs_1_, f32[8192,1024]{1,0:T(8,128)} %bitcast.113, f32[2048,128]{1,0:T(8,128)} %copy-done.12, ...), custom_call_target="tpu_custom_call", output_to_operand_aliasing={{}: (5, {})} | custom-call | tf_op jit(solution)/shard_map/product/pallas_call | solution.py:111
  721.8 6.7 product.24.refs_4_
  729.2 4.5 product.25
  736.9 1.6 collective-permute-start.39
  738.5 1.5 collective-permute-start.41
  740.4 4.4 collective-permute-done.39
  747.9 2.7 collective-permute-start.44
  753.6 3.3 collective-permute-done.43
  (108 shorter events, 38.8 us)
Async XLA Ops:
  1.0 67.6 %collective-permute-start.1 = (f32[512,128]{1,0:T(8,128)S(1)}, f32[512,128]{1,0:T(8,128)S(1)}, u32[]{:S(2)}, u32[]{:S(2)}) collective-permute-start(f32[512,128]{1,0:T(8,128)S(1)} %slice.52), channel_id=1, source_target_pairs={{0,16},{1,17},{2,18},{3,19},{4,20},{5,21},{6,22},{7,23},{8,24},{9,... | collective-permute-start | bytes 786440 | tf_op jit(solution)/shard_map/ppermute | solution.py:20
  8.4 93.8 %collective-permute-start = (f32[8192,128]{1,0:T(8,128)}, f32[8192,128]{1,0:T(8,128)}, u32[]{:S(2)}, u32[]{:S(2)}) collective-permute-start(f32[8192,128]{1,0:T(8,128)} %slice.53), channel_id=1, source_target_pairs={{0,16},{1,17},{2,18},{3,19},{4,20},{5,21},{6,22},{7,23},{8,24},{9,... | collective-permute-start | bytes 12582920 | tf_op jit(solution)/shard_map/ppermute | solution.py:20
  68.5 2.1 copy-start.15
  68.6 123.6 %collective-permute-start.2 = (f32[8192,128]{1,0:T(8,128)}, f32[8192,128]{1,0:T(8,128)}, u32[]{:S(2)}, u32[]{:S(2)}) collective-permute-start(f32[8192,128]{1,0:T(8,128)} %get-tuple-element.50), channel_id=1, source_target_pairs={{0,16},{1,17},{2,18},{3,19},{4,20},{5,21},{6,22},{7,23},{8,24},{9,... | collective-permute-start | bytes 12582920 | tf_op jit(solution)/shard_map/ppermute | solution.py:20
  102.3 179.8 %collective-permute-start.9 = (f32[8192,128]{1,0:T(8,128)}, f32[8192,128]{1,0:T(8,128)}, u32[]{:S(2)}, u32[]{:S(2)}) collective-permute-start(f32[8192,128]{1,0:T(8,128)} %get-tuple-element.53), channel_id=1, source_target_pairs={{0,16},{1,17},{2,18},{3,19},{4,20},{5,21},{6,22},{7,23},{8,24},{9,... | collective-permute-start | bytes 12582920 | tf_op jit(solution)/shard_map/ppermute | solution.py:20
  192.1 179.8 %collective-permute-start.10 = (f32[8192,128]{1,0:T(8,128)}, f32[8192,128]{1,0:T(8,128)}, u32[]{:S(2)}, u32[]{:S(2)}) collective-permute-start(f32[8192,128]{1,0:T(8,128)} %get-tuple-element.56), channel_id=1, source_target_pairs={{0,16},{1,17},{2,18},{3,19},{4,20},{5,21},{6,22},{7,23},{8,24},{9,... | collective-permute-start | bytes 12582920 | tf_op jit(solution)/shard_map/ppermute | solution.py:20
  195.8 30.4 %copy-start.1 = (f32[2048,128]{1,0:T(8,128)S(1)}, f32[2048,128]{1,0:T(8,128)}, u32[]{:S(2)}) copy-start(f32[2048,128]{1,0:T(8,128)} %product.14) | copy-start | bytes 3145732
  226.2 27.9 %copy-start.2 = (f32[2048,128]{1,0:T(8,128)S(1)}, f32[2048,128]{1,0:T(8,128)}, u32[]{:S(2)}) copy-start(f32[2048,128]{1,0:T(8,128)} %product.15) | copy-start | bytes 3145732
  228.6 2.1 collective-permute-start.3
  228.6 14.9 %collective-permute-start.4 = (f32[4,128,256]{2,1,0:T(8,128)}, f32[4,128,256]{2,1,0:T(8,128)S(1)}, u32[]{:S(2)}, u32[]{:S(2)}) collective-permute-start(f32[4,128,256]{2,1,0:T(8,128)} %get-tuple-element.85), channel_id=1, source_target_pairs={{0,2},{1,3},{2,0},{3,1},{4,6},{5,7},{6,4},{7,5},{8,10},{9,11},{10,... | collective-permute-start | bytes 1572872 | tf_op jit(solution)/shard_map/ppermute | solution.py:20
  230.0 24.1 %collective-permute-start.5 = (f32[4,128,256]{2,1,0:T(8,128)}, f32[4,128,256]{2,1,0:T(8,128)}, u32[]{:S(2)}, u32[]{:S(2)}) collective-permute-start(f32[4,128,256]{2,1,0:T(8,128)} %get-tuple-element.86), channel_id=1, source_target_pairs={{0,3},{1,2},{2,1},{3,0},{4,7},{5,6},{6,5},{7,4},{8,11},{9,10},{10,... | collective-permute-start | bytes 1572872 | tf_op jit(solution)/shard_map/ppermute | solution.py:20
  243.5 0.8 copy-start.14
  255.5 6.0 collective-permute-start.6
  257.0 9.7 %collective-permute-start.8 = (f32[1,128,256]{2,1,0:T(8,128)S(1)}, f32[1,128,256]{2,1,0:T(8,128)S(1)}, u32[]{:S(2)}, u32[]{:S(2)}) collective-permute-start(f32[1,128,256]{2,1,0:T(8,128)S(1)} %get-tuple-element.100), channel_id=1, source_target_pairs={{0,12},{1,13},{2,14},{3,15},{4,8},{5,9},{6,10},{7,11},{8,4},{9,5},... | collective-permute-start | bytes 393224 | tf_op jit(solution)/shard_map/ppermute | solution.py:20
  259.5 12.4 %collective-permute-start.7 = (f32[1,128,256]{2,1,0:T(8,128)S(1)}, f32[1,128,256]{2,1,0:T(8,128)S(1)}, u32[]{:S(2)}, u32[]{:S(2)}) collective-permute-start(f32[1,128,256]{2,1,0:T(8,128)S(1)} %get-tuple-element.101), channel_id=1, source_target_pairs={{0,8},{1,9},{2,10},{3,11},{4,12},{5,13},{6,14},{7,15},{8,0},{9,1},... | collective-permute-start | bytes 393224 | tf_op jit(solution)/shard_map/ppermute | solution.py:20
  282.0 179.8 %collective-permute-start.17 = (f32[8192,128]{1,0:T(8,128)}, f32[8192,128]{1,0:T(8,128)}, u32[]{:S(2)}, u32[]{:S(2)}) collective-permute-start(f32[8192,128]{1,0:T(8,128)} %get-tuple-element.59), channel_id=1, source_target_pairs={{0,16},{1,17},{2,18},{3,19},{4,20},{5,21},{6,22},{7,23},{8,24},{9,... | collective-permute-start | bytes 12582920 | tf_op jit(solution)/shard_map/ppermute | solution.py:20
  371.9 179.8 %collective-permute-start.18 = (f32[8192,128]{1,0:T(8,128)}, f32[8192,128]{1,0:T(8,128)}, u32[]{:S(2)}, u32[]{:S(2)}) collective-permute-start(f32[8192,128]{1,0:T(8,128)} %get-tuple-element.62), channel_id=1, source_target_pairs={{0,16},{1,17},{2,18},{3,19},{4,20},{5,21},{6,22},{7,23},{8,24},{9,... | collective-permute-start | bytes 12582920 | tf_op jit(solution)/shard_map/ppermute | solution.py:20
  374.8 30.4 %copy-start.3 = (f32[2048,128]{1,0:T(8,128)S(1)}, f32[2048,128]{1,0:T(8,128)}, u32[]{:S(2)}) copy-start(f32[2048,128]{1,0:T(8,128)} %product.16) | copy-start | bytes 3145732
  405.2 26.5 %copy-start.6 = (f32[2048,128]{1,0:T(8,128)S(1)}, f32[2048,128]{1,0:T(8,128)}, u32[]{:S(2)}) copy-start(f32[2048,128]{1,0:T(8,128)} %product.17) | copy-start | bytes 3145732
  406.6 2.0 collective-permute-start.11
  406.6 14.8 %collective-permute-start.12 = (f32[4,128,256]{2,1,0:T(8,128)S(1)}, f32[4,128,256]{2,1,0:T(8,128)S(1)}, u32[]{:S(2)}, u32[]{:S(2)}) collective-permute-start(f32[4,128,256]{2,1,0:T(8,128)S(1)} %get-tuple-element.82), channel_id=1, source_target_pairs={{0,2},{1,3},{2,0},{3,1},{4,6},{5,7},{6,4},{7,5},{8,10},{9,11},{10,... | collective-permute-start | bytes 1572872 | tf_op jit(solution)/shard_map/ppermute | solution.py:20
  408.2 53.6 %copy-start.8 = (f32[4096,128]{1,0:T(8,128)S(1)}, f32[4096,128]{1,0:T(8,128)}, u32[]{:S(2)}) copy-start(f32[4096,128]{1,0:T(8,128)} %slice.46) | copy-start | bytes 6291460
  408.2 23.6 %collective-permute-start.13 = (f32[4,128,256]{2,1,0:T(8,128)S(1)}, f32[4,128,256]{2,1,0:T(8,128)S(1)}, u32[]{:S(2)}, u32[]{:S(2)}) collective-permute-start(f32[4,128,256]{2,1,0:T(8,128)S(1)} %get-tuple-element.83), channel_id=1, source_target_pairs={{0,3},{1,2},{2,1},{3,0},{4,7},{5,6},{6,5},{7,4},{8,11},{9,10},{10,... | collective-permute-start | bytes 1572872 | tf_op jit(solution)/shard_map/ppermute | solution.py:20
  431.9 6.1 collective-permute-start.14
  433.5 9.7 %collective-permute-start.16 = (f32[1,128,256]{2,1,0:T(8,128)S(1)}, f32[1,128,256]{2,1,0:T(8,128)S(1)}, u32[]{:S(2)}, u32[]{:S(2)}) collective-permute-start(f32[1,128,256]{2,1,0:T(8,128)S(1)} %get-tuple-element.97), channel_id=1, source_target_pairs={{0,12},{1,13},{2,14},{3,15},{4,8},{5,9},{6,10},{7,11},{8,4},{9,5},... | collective-permute-start | bytes 393224 | tf_op jit(solution)/shard_map/ppermute | solution.py:20
  436.0 12.6 %collective-permute-start.15 = (f32[1,128,256]{2,1,0:T(8,128)S(1)}, f32[1,128,256]{2,1,0:T(8,128)S(1)}, u32[]{:S(2)}, u32[]{:S(2)}) collective-permute-start(f32[1,128,256]{2,1,0:T(8,128)S(1)} %get-tuple-element.98), channel_id=1, source_target_pairs={{0,8},{1,9},{2,10},{3,11},{4,12},{5,13},{6,14},{7,15},{8,0},{9,1},... | collective-permute-start | bytes 393224 | tf_op jit(solution)/shard_map/ppermute | solution.py:20
  461.8 164.5 %collective-permute-start.26 = (f32[4096,128]{1,0:T(8,128)S(1)}, f32[4096,128]{1,0:T(8,128)}, u32[]{:S(2)}, u32[]{:S(2)}) collective-permute-start(f32[4096,128]{1,0:T(8,128)S(1)} %copy-done.8), channel_id=1, source_target_pairs={{0,16},{1,17},{2,18},{3,19},{4,20},{5,21},{6,22},{7,23},{8,24},{9,... | collective-permute-start | bytes 6291464 | tf_op jit(solution)/shard_map/ppermute | solution.py:20
  495.6 86.6 %copy-start.4 = (f32[2048,128]{1,0:T(8,128)S(1)}, f32[2048,128]{1,0:T(8,128)}, u32[]{:S(2)}) copy-start(f32[2048,128]{1,0:T(8,128)} %product.18) | copy-start | bytes 3145732
  582.2 26.5 %copy-start.5 = (f32[2048,128]{1,0:T(8,128)S(1)}, f32[2048,128]{1,0:T(8,128)}, u32[]{:S(2)}) copy-start(f32[2048,128]{1,0:T(8,128)} %product.19) | copy-start | bytes 3145732
  583.5 2.5 collective-permute-start.19
  583.6 14.8 %collective-permute-start.20 = (f32[4,128,256]{2,1,0:T(8,128)S(1)}, f32[4,128,256]{2,1,0:T(8,128)S(1)}, u32[]{:S(2)}, u32[]{:S(2)}) collective-permute-start(f32[4,128,256]{2,1,0:T(8,128)S(1)} %get-tuple-element.79), channel_id=1, source_target_pairs={{0,2},{1,3},{2,0},{3,1},{4,6},{5,7},{6,4},{7,5},{8,10},{9,11},{10,... | collective-permute-start | bytes 1572872 | tf_op jit(solution)/shard_map/ppermute | solution.py:20
  585.2 23.5 %collective-permute-start.21 = (f32[4,128,256]{2,1,0:T(8,128)S(1)}, f32[4,128,256]{2,1,0:T(8,128)S(1)}, u32[]{:S(2)}, u32[]{:S(2)}) collective-permute-start(f32[4,128,256]{2,1,0:T(8,128)S(1)} %get-tuple-element.80), channel_id=1, source_target_pairs={{0,3},{1,2},{2,1},{3,0},{4,7},{5,6},{6,5},{7,4},{8,11},{9,10},{10,... | collective-permute-start | bytes 1572872 | tf_op jit(solution)/shard_map/ppermute | solution.py:20
  585.5 58.2 %collective-permute-start.25 = (f32[4096,128]{1,0:T(8,128)}, f32[4096,128]{1,0:T(8,128)}, u32[]{:S(2)}, u32[]{:S(2)}) collective-permute-start(f32[4096,128]{1,0:T(8,128)} %slice.47), channel_id=1, source_target_pairs={{0,16},{1,17},{2,18},{3,19},{4,20},{5,21},{6,22},{7,23},{8,24},{9,... | collective-permute-start | bytes 6291464 | tf_op jit(solution)/shard_map/ppermute | solution.py:20
  608.9 6.1 collective-permute-start.22
  610.6 9.7 %collective-permute-start.24 = (f32[1,128,256]{2,1,0:T(8,128)S(1)}, f32[1,128,256]{2,1,0:T(8,128)S(1)}, u32[]{:S(2)}, u32[]{:S(2)}) collective-permute-start(f32[1,128,256]{2,1,0:T(8,128)S(1)} %get-tuple-element.94), channel_id=1, source_target_pairs={{0,12},{1,13},{2,14},{3,15},{4,8},{5,9},{6,10},{7,11},{8,4},{9,5},... | collective-permute-start | bytes 393224 | tf_op jit(solution)/shard_map/ppermute | solution.py:20
  613.0 12.6 %collective-permute-start.23 = (f32[1,128,256]{2,1,0:T(8,128)S(1)}, f32[1,128,256]{2,1,0:T(8,128)S(1)}, u32[]{:S(2)}, u32[]{:S(2)}) collective-permute-start(f32[1,128,256]{2,1,0:T(8,128)S(1)} %get-tuple-element.95), channel_id=1, source_target_pairs={{0,8},{1,9},{2,10},{3,11},{4,12},{5,13},{6,14},{7,15},{8,0},{9,1},... | collective-permute-start | bytes 393224 | tf_op jit(solution)/shard_map/ppermute | solution.py:20
  626.3 61.6 %collective-permute-start.34 = (f32[4096,128]{1,0:T(8,128)}, f32[4096,128]{1,0:T(8,128)S(1)}, u32[]{:S(2)}, u32[]{:S(2)}) collective-permute-start(f32[4096,128]{1,0:T(8,128)} %slice.48), channel_id=1, source_target_pairs={{0,16},{1,17},{2,18},{3,19},{4,20},{5,21},{6,22},{7,23},{8,24},{9,... | collective-permute-start | bytes 6291464 | tf_op jit(solution)/shard_map/ppermute | solution.py:20
  663.0 3.7 collective-permute-start.27
  663.1 8.3 %collective-permute-start.29 = (f32[4,128,128]{2,1,0:T(8,128)S(1)}, f32[4,128,128]{2,1,0:T(8,128)S(1)}, u32[]{:S(2)}, u32[]{:S(2)}) collective-permute-start(f32[4,128,128]{2,1,0:T(8,128)S(1)} %get-tuple-element.88), channel_id=1, source_target_pairs={{0,3},{1,2},{2,1},{3,0},{4,7},{5,6},{6,5},{7,4},{8,11},{9,10},{10,... | collective-permute-start | bytes 786440 | tf_op jit(solution)/shard_map/ppermute | solution.py:20
  664.7 12.7 %collective-permute-start.28 = (f32[4,128,128]{2,1,0:T(8,128)S(1)}, f32[4,128,128]{2,1,0:T(8,128)S(1)}, u32[]{:S(2)}, u32[]{:S(2)}) collective-permute-start(f32[4,128,128]{2,1,0:T(8,128)S(1)} %get-tuple-element.89), channel_id=1, source_target_pairs={{0,2},{1,3},{2,0},{3,1},{4,6},{5,7},{6,4},{7,5},{8,10},{9,11},{10,... | collective-permute-start | bytes 786440 | tf_op jit(solution)/shard_map/ppermute | solution.py:20
  665.3 43.6 %collective-permute-start.33 = (f32[2048,128]{1,0:T(8,128)}, f32[2048,128]{1,0:T(8,128)S(1)}, u32[]{:S(2)}, u32[]{:S(2)}) collective-permute-start(f32[2048,128]{1,0:T(8,128)} %slice.49), channel_id=1, source_target_pairs={{0,16},{1,17},{2,18},{3,19},{4,20},{5,21},{6,22},{7,23},{8,24},{9,... | collective-permute-start | bytes 3145736 | tf_op jit(solution)/shard_map/ppermute | solution.py:20
  678.5 4.8 collective-permute-start.30
  678.5 6.6 collective-permute-start.32
  681.3 6.6 collective-permute-start.31
  687.9 1.6 copy-start.7
  687.9 33.1 %collective-permute-start.37 = (f32[1024,128]{1,0:T(8,128)}, f32[1024,128]{1,0:T(8,128)S(1)}, u32[]{:S(2)}, u32[]{:S(2)}) collective-permute-start(f32[1024,128]{1,0:T(8,128)} %slice.50), channel_id=1, source_target_pairs={{0,16},{1,17},{2,18},{3,19},{4,20},{5,21},{6,22},{7,23},{8,24},{9,... | collective-permute-start | bytes 1572872 | tf_op jit(solution)/shard_map/ppermute | solution.py:20
  708.9 1.0 copy-start.12
  708.9 19.6 %collective-permute-start.35 = (f32[512,128]{1,0:T(8,128)S(1)}, f32[512,128]{1,0:T(8,128)S(1)}, u32[]{:S(2)}, u32[]{:S(2)}) collective-permute-start(f32[512,128]{1,0:T(8,128)S(1)} %slice.51), channel_id=1, source_target_pairs={{0,16},{1,17},{2,18},{3,19},{4,20},{5,21},{6,22},{7,23},{8,24},{9,... | collective-permute-start | bytes 786440 | tf_op jit(solution)/shard_map/ppermute | solution.py:20
  721.0 0.8 copy-start.13
  728.4 6.5 copy-start.9
  728.4 6.5 copy-start.10
  728.4 6.5 copy-start.11
  728.5 0.7 copy-start.16
  733.6 3.2 copy-start
  734.8 2.0 collective-permute-start.38
  735.0 12.9 %collective-permute-start.36 = (f32[128,896]{1,0:T(8,128)S(1)}, f32[128,896]{1,0:T(8,128)S(1)}, u32[]{:S(2)}, u32[]{:S(2)}) collective-permute-start(f32[128,896]{1,0:T(8,128)S(1)} %pad_maximum_fusion), channel_id=1, source_target_pairs={{0,16},{1,17},{2,18},{3,19},{4,20},{5,21},{6,22},{7,23},{8,24},{9,... | collective-permute-start | bytes 1376264 | tf_op jit(solution)/shard_map/ppermute | solution.py:20
  736.9 8.0 %collective-permute-start.39 = (f32[2,128,128]{2,1,0:T(8,128)S(1)}, f32[2,128,128]{2,1,0:T(8,128)S(1)}, u32[]{:S(2)}, u32[]{:S(2)}) collective-permute-start(f32[2,128,128]{2,1,0:T(8,128)S(1)} %get-tuple-element.90), channel_id=1, source_target_pairs={{0,2},{1,3},{2,0},{3,1},{4,6},{5,7},{6,4},{7,5},{8,10},{9,11},{10,... | collective-permute-start | bytes 393224 | tf_op jit(solution)/shard_map/ppermute | solution.py:20
  738.5 7.3 collective-permute-start.41
  740.0 6.5 collective-permute-start.40
  747.9 5.7 collective-permute-start.44
  750.6 6.3 collective-permute-start.43
  751.4 5.5 collective-permute-start.42

commit v3 on v2

--- a/solution.py
+++ b/solution.py
@@ -9,7 +9,8 @@
 from jax.sharding import PartitionSpec as P
 
 LANES = 128
-VMEM_BYTES = 60 * 2**20
+SPLIT_BYTES = 40 * 2**20
+PRODUCT_BYTES = 40 * 2**20
 
 
 AXES = ("pair", "blk", "rows")
@@ -67,56 +68,77 @@
         in_specs=[spec],
         out_specs=[spec, spec],
         out_shape=[part, part],
-        compiler_params=pltpu.CompilerParams(vmem_limit_bytes=VMEM_BYTES),
+        compiler_params=pltpu.CompilerParams(vmem_limit_bytes=SPLIT_BYTES),
         cost_estimate=pl.CostEstimate(flops=0, bytes_accessed=8 * rows * depth, transcendentals=0),
         name="split_matrix",
     )(matrix)
 
 
-def product_kernel(added, sign_ref, *refs):
-    high_ref, low_ref, own_ref, partner_ref = refs[:4]
-    total_ref, out_ref, both = (refs[4:] if added else (None, *refs[4:]))
-    width = out_ref.shape[1]
-
-    @pl.when(pl.program_id(0) == 0)
-    def _():
-        combined = partner_ref[...] + sign_ref[0] * own_ref[...]
-        both[:, :width], both[:, width:] = halves(combined)
-
-    right = both[...]
+def product_kernel(added, owned, control_ref, high_ref, low_ref, own_ref, partner_ref, *refs):
+    total_ref = refs[0] if added else None
+    out_refs, sum_ref = refs[added:-1], refs[-1]
+    width = sum_ref.shape[1]
+    step = pl.program_id(0)
+
+    right = jnp.concatenate(halves(partner_ref[...] + control_ref[0] * own_ref[...]), axis=1)
     result = jnp.dot(low_ref[...], right, preferred_element_type=jnp.float32)
     result += jnp.dot(high_ref[...], right, preferred_element_type=jnp.float32)
     result = result[:, width:] + result[:, :width]
-    out_ref[...] = result + total_ref[...] if added else result
-
-
-def product(sign, high, low, own, partner, column, start, total=None):
-    rows = high.shape[0]
-    depth, width = partner.shape
-    step = min(rows, 1024, max(256, 2**21 // depth))
-    place = start // depth
-    matrix_spec = pl.BlockSpec((step, depth), lambda i: (i, place))
-    out_spec = pl.BlockSpec((step, width), lambda i: (i, 0))
+
+    @pl.when(step == 0)
+    def _():
+        sum_ref[...] = result + total_ref[...] if added else result
+
+    @pl.when(step > 0)
+    def _():
+        sum_ref[...] += result
+
+    @pl.when(step == pl.num_programs(0) - 1)
+    def _():
+        if owned:
+            kept_ref, given_ref = out_refs
+            both = sum_ref[...].reshape(-1, 2, *kept_ref.shape[1:])
+            odd = control_ref[1] > 0.5
+            kept_ref[...] = jnp.where(odd, both[:, 1], both[:, 0])
+            given_ref[...] = jnp.where(odd, both[:, 0], both[:, 1])
+        else:
+            out_refs[0][...] = sum_ref[...]
+
+
+def product(control, high, low, own, partner, piece, total=None, owned=0):
+    chunk, start, size = piece
+    rows, width = high.shape[0], partner.shape[1]
+    step = 1024
+    while start % step or size % step or step > max(LANES, size // 2):
+        step //= 2
+    first = start // step
+    matrix_spec = pl.BlockSpec((rows, step), lambda i: (0, first + i))
+    whole_spec = pl.BlockSpec((rows, width), lambda i: (0, 0))
     in_specs = [
         pl.BlockSpec(memory_space=pltpu.SMEM),
         matrix_spec,
         matrix_spec,
-        pl.BlockSpec((depth, width), lambda i: (place, column)),
-        pl.BlockSpec((depth, width), lambda i: (0, 0)),
+        pl.BlockSpec((step, width), lambda i: (first + i, chunk)),
+        pl.BlockSpec((step, width), lambda i: (i, 0)),
     ]
-    operands = [sign, high, low, own, partner]
+    operands = [control, high, low, own, partner]
     if total is not None:
-        in_specs.append(out_spec)
+        in_specs.append(whole_spec)
         operands.append(total)
+    out_specs = whole_spec
+    out_shape = jax.ShapeDtypeStruct((rows, width), jnp.float32)
+    if owned:
+        shape = (rows // (2 * owned), owned, width)
+        out_specs = [pl.BlockSpec(shape, lambda i: (0, 0, 0))] * 2
+        out_shape = [jax.ShapeDtypeStruct(shape, jnp.float32)] * 2
     return pl.pallas_call(
-        functools.partial(product_kernel, total is not None),
-        grid=(rows // step,),
+        functools.partial(product_kernel, total is not None, owned > 0),
+        grid=(size // step,),
         in_specs=in_specs,
-        out_specs=out_spec,
-        out_shape=jax.ShapeDtypeStruct((rows, width), jnp.float32),
-        scratch_shapes=[pltpu.VMEM((depth, 2 * width), jnp.bfloat16)],
-        input_output_aliases={} if total is None else {5: 0},
-        compiler_params=pltpu.CompilerParams(vmem_limit_bytes=VMEM_BYTES),
+        out_specs=out_specs,
+        out_shape=out_shape,
+        scratch_shapes=[pltpu.VMEM((rows, width), jnp.float32)],
+        compiler_params=pltpu.CompilerParams(vmem_limit_bytes=PRODUCT_BYTES),
         cost_estimate=pl.CostEstimate(flops=0, bytes_accessed=0, transcendentals=0),
         name="product",
     )(*operands)
@@ -125,13 +147,15 @@
 def pieces_of(depth, vectors):
     last = vectors // LANES - 1
     least = max(LANES, depth // 16)
-    pieces = [(last, 0, least)] + [(chunk, 0, depth) for chunk in range(last - 1)]
+    head = max(LANES, depth // 8)
+    pieces = [(last, 0, head)] + [(chunk, 0, depth) for chunk in range(last - 1)]
     pieces += [(last - 1, 0, depth // 2), (last - 1, depth // 2, depth // 2)]
-    size = depth // 2
-    while size >= least:
-        pieces.append((last, size, size))
-        size //= 2
-    return pieces
+    start, size = head, depth // 2 - head
+    while start < depth - least:
+        pieces.append((last, start, size))
+        start += size
+        size = max(least, (depth - start) // 2)
+    return pieces + [(last, start, least)]
 
 
 def shards(tiles, trial):
@@ -139,6 +163,8 @@
     depth, vectors = own.shape
     sign = 1.0 - 2.0 * lax.axis_index("pair").astype(jnp.float32)
     pieces = pieces_of(depth, vectors)
+    odd = (lax.axis_index("rows") % 2).astype(jnp.float32)
+    control = jnp.stack([sign, odd])
     pair = lax.axis_size("blk") * lax.axis_size("rows")
     bits = pair.bit_length() - 1
 
@@ -151,8 +177,10 @@
         return source[start : start + size, chunk * LANES : (chunk + 1) * LANES]
 
     ahead, cut_ahead = 2, 6
-    blocks = {index: block(index) for index in range(ahead)}
-    arrived = [swapped(blocks[index], pair) for index in range(ahead)]
+    blocks, arrived = {}, []
+    for index in range(ahead):
+        blocks[index] = block(index, *blocks.values())
+        arrived.append(swapped(blocks[index], pair))
     high, low = split_matrix(after(matrix, *blocks.values()))
     totals, covered, waiting, sums = {}, {}, [], []
     done = high
@@ -164,10 +192,13 @@
                 partner = after(partner, blocks[later])
         if index + ahead < len(pieces):
             arrived.append(swapped(after(blocks[index + ahead], arrived[index], done), pair))
-        done = product(sign[None], high, low, own, partner, chunk, start, totals.get(chunk))
-        totals[chunk] = done
+        operands = (control, high, low, own, partner, pieces[index], totals.get(chunk))
+        if index + 1 == len(pieces):
+            kept, given = product(*operands, owned=matrix.shape[0] // pair)
+            break
+        done = totals[chunk] = product(*operands)
         covered[chunk] = covered.get(chunk, 0) + size
-        if covered[chunk] == depth and index + 1 < len(pieces):
+        if covered[chunk] == depth:
             waiting.append(by_owner(done))
             if len(waiting) == 2 or chunk == pieces[-1][0] - 1:
                 steps = [2] * (bits // 2) + [1] * (bits % 2)
@@ -177,8 +208,9 @@
 
     early = jnp.concatenate(sums, axis=1)
     early_partner = swapped(after(early, arrived[-1]), pair)
-    steps = [1] + [2] * ((bits - 2) // 2) + [1] * (bits % 2)
-    late = after(scattered_sum(by_owner(done), 0, steps), early_partner)
+    late = kept + swapped(given, 1)
+    late = scattered_sum(late, 1, [2] * ((bits - 2) // 2) + [1] * (bits % 2))
+    late = after(late, early_partner)
     result = jnp.concatenate(
         [0.5 * (early_partner + sign * early), scattered_halves(late, bits - 1, 1, sign)[0]], axis=1
     )

time: 759 us -> 752 us (level)
  Pallas kernels: 307 us -> 279 us
  waiting for transfers between devices: 353 us -> 370 us
  starting transfers between devices: 46.2 us -> 60.3 us
    pallas_call x13 -> x14, Pallas kernels: 262 us -> 234 us  [product(): pl.pallas_call(functools.partial(product_kernel, total is not None, owned...]
    ppermute x45 -> x46, waiting for transfers between devices: 353 us -> 370 us  [swapped(): lax.ppermute(value, AXES, [(source, source ^ mask) for source in range(de...]
    ppermute x45 -> x46, starting transfers between devices: 46.2 us -> 60.3 us  [swapped(): lax.ppermute(value, AXES, [(source, source ^ mask) for source in range(de...]
    slice x9 -> x10, local copies, waits for them, and re-layouts: 35.1 us -> 33.7 us  [block(): return source[start:start + size, chunk * LANES:(chunk + 1) * LANES]]
  transfers between devices with their start and end apart: 45 -> 46, of which waited for: 35 -> 36; matrix products, arithmetic and copies ran while one was open for 6% -> 5% of each run, Pallas kernels for 40% -> 37%
where the time goes in v3:
time: 752 us
  waiting for transfers between devices  370 us (49%)
  Pallas kernels  279 us (37%)
  starting transfers between devices  60.3 us (8%)
  local copies, waits for them, and re-layouts  34.7 us (5%)
    ppermute x46, waiting for transfers between devices, swapped(): lax.ppermute(value, AXES, [(source, source ^ mask) for source in range(de...  370 us
    pallas_call x14, Pallas kernels, product(): pl.pallas_call(functools.partial(product_kernel, total is not None, owned...  234 us
    ppermute x46, starting transfers between devices, swapped(): lax.ppermute(value, AXES, [(source, source ^ mask) for source in range(de...  60.3 us
    pallas_call x1, Pallas kernels, split_matrix(): pl.pallas_call(split_kernel, grid=(rows // step,), in_specs=[spec], out_s...  44.9 us
    slice x10, local copies, waits for them, and re-layouts, block(): return source[start:start + size, chunk * LANES:(chunk + 1) * LANES]  33.7 us
  transfers between devices with their start and end apart: 46, of which 36 were waited for; matrix products, arithmetic and copies ran while one was open for 5% of the time, Pallas kernels for 37%

profile of v3, /device:TPU:0, one launch (start us, length us, event | category | flops | bytes accessed | tf_op | source)
XLA Modules:
  0.0 751.6 jit_solution(14040370022168050682)
XLA Ops:
  1.1 3.0 collective-permute-start.1
  4.1 4.5 slice.43
  8.6 44.9 %split_matrix.1 = (bf16[2048,8192]{1,0:T(8,128)(2,1)}, bf16[2048,8192]{1,0:T(8,128)(2,1)}) custom-call(f32[2048,8192]{1,0:T(8,128)} %bitcast.2.matrix_ref), custom_call_target="tpu_custom_call" | custom-call | bytes 134217728 | tf_op jit(solution)/shard_map/split_matrix/pallas_call | solution.py:65
  53.4 15.2 %fusion.37 = (f32[8192,128]{1,0:T(8,128)}, f32[8192,128]{1,0:T(8,128)}, f32[8192,128]{1,0:T(8,128)}, f32[8192,128]{1,0:T(8,128)}, f32[8192,128]{1,0:T(8,128)}) fusion(f32[8192,1024]{1,0:T(8,128)} %bitcast.106), kind=kLoop, calls=%fused_computation.92 | loop fusion | bytes 41943040 | tf_op jit(solution)/shard_map/slice | solution.py:177
  68.7 2.1 collective-permute-start.2
  70.8 5.1 product.14.refs_0_
  75.9 30.9 %collective-permute-done.partner_ref = f32[8192,128]{1,0:T(8,128)} collective-permute-done((f32[8192,128]{1,0:T(8,128)}, f32[8192,128]{1,0:T(8,128)}, u32[]{:S(2)}, u32[]{:S(2)}) %collective-permute-start) | collective-permute-done | bytes 4194336 | tf_op jit(solution)/shard_map/ppermute | solution.py:21
  106.8 2.1 collective-permute-start.9
  108.9 3.0 slice.49
  111.9 27.9 %product.15 = f32[2048,128]{1,0:T(8,128)S(1)} custom-call(f32[2]{0:T(128)S(1)} %pad_maximum_fusion.1.control_ref, bf16[2048,8192]{1,0:T(8,128)(2,1)} %get-tuple-element.47.high_ref, bf16[2048,8192]{1,0:T(8,128)(2,1)} %get-tuple-element.48.low_ref, f32[8192,1024]{1,0:T(8,128)} %bitcast.109, f32[8192,128]{1,0:T(8,128)} %collective-permute-done.partner_ref), custom_call_target="tpu_custom_call" | custom-call | tf_op jit(solution)/shard_map/product/pallas_call | solution.py:134
  139.9 56.8 %collective-permute-done.2.partner_ref = f32[8192,128]{1,0:T(8,128)} collective-permute-done((f32[8192,128]{1,0:T(8,128)}, f32[8192,128]{1,0:T(8,128)}, u32[]{:S(2)}, u32[]{:S(2)}) %collective-permute-start.2) | collective-permute-done | bytes 4194336 | tf_op jit(solution)/shard_map/ppermute | solution.py:21
  196.7 2.1 collective-permute-start.10
  198.8 3.0 slice.50
  201.8 27.9 %product.16 = f32[2048,128]{1,0:T(8,128)S(1)} custom-call(f32[2]{0:T(128)S(1)} %pad_maximum_fusion.1.control_ref, bf16[2048,8192]{1,0:T(8,128)(2,1)} %get-tuple-element.47.high_ref, bf16[2048,8192]{1,0:T(8,128)(2,1)} %get-tuple-element.48.low_ref, f32[8192,1024]{1,0:T(8,128)} %bitcast.111, f32[8192,128]{1,0:T(8,128)} %collective-permute-done.2.partner_ref), custom_call_target="tpu_custom_call" | custom-call | tf_op jit(solution)/shard_map/product/pallas_call | solution.py:134
  233.2 12.8 %collective-permute-done.4 = f32[4,128,256]{2,1,0:T(8,128)} collective-permute-done((f32[4,128,256]{2,1,0:T(8,128)}, f32[4,128,256]{2,1,0:T(8,128)}, u32[]{:S(2)}, u32[]{:S(2)}) %collective-permute-start.4) | collective-permute-done | bytes 524320 | tf_op jit(solution)/shard_map/ppermute | solution.py:21
  246.0 10.5 %collective-permute-done.5 = f32[4,128,256]{2,1,0:T(8,128)} collective-permute-done((f32[4,128,256]{2,1,0:T(8,128)}, f32[4,128,256]{2,1,0:T(8,128)}, u32[]{:S(2)}, u32[]{:S(2)}) %collective-permute-start.5) | collective-permute-done | bytes 524320 | tf_op jit(solution)/shard_map/ppermute | solution.py:21
  260.4 2.5 collective-permute-start.8
  264.8 5.3 collective-permute-done.8
  270.1 5.2 collective-permute-done.7
  277.0 9.6 %collective-permute-done.9.partner_ref = f32[8192,128]{1,0:T(8,128)} collective-permute-done((f32[8192,128]{1,0:T(8,128)}, f32[8192,128]{1,0:T(8,128)}, u32[]{:S(2)}, u32[]{:S(2)}) %collective-permute-start.9) | collective-permute-done | bytes 4194336 | tf_op jit(solution)/shard_map/ppermute | solution.py:21
  286.6 2.1 collective-permute-start.17
  290.2 28.2 %product.17 = f32[2048,128]{1,0:T(8,128)S(1)} custom-call(f32[2]{0:T(128)S(1)} %pad_maximum_fusion.1.control_ref, bf16[2048,8192]{1,0:T(8,128)(2,1)} %get-tuple-element.47.high_ref, bf16[2048,8192]{1,0:T(8,128)(2,1)} %get-tuple-element.48.low_ref, f32[8192,1024]{1,0:T(8,128)} %bitcast.113, f32[8192,128]{1,0:T(8,128)} %collective-permute-done.9.partner_ref), custom_call_target="tpu_custom_call" | custom-call | tf_op jit(solution)/shard_map/product/pallas_call | solution.py:134
  318.4 58.1 %collective-permute-done.10.partner_ref = f32[8192,128]{1,0:T(8,128)} collective-permute-done((f32[8192,128]{1,0:T(8,128)}, f32[8192,128]{1,0:T(8,128)}, u32[]{:S(2)}, u32[]{:S(2)}) %collective-permute-start.10) | collective-permute-done | bytes 4194336 | tf_op jit(solution)/shard_map/ppermute | solution.py:21
  376.5 2.1 collective-permute-start.18
  378.5 2.3 slice.52
  380.8 27.9 %product.18 = f32[2048,128]{1,0:T(8,128)S(1)} custom-call(f32[2]{0:T(128)S(1)} %pad_maximum_fusion.1.control_ref, bf16[2048,8192]{1,0:T(8,128)(2,1)} %get-tuple-element.47.high_ref, bf16[2048,8192]{1,0:T(8,128)(2,1)} %get-tuple-element.48.low_ref, f32[8192,1024]{1,0:T(8,128)} %bitcast.115, f32[8192,128]{1,0:T(8,128)} %collective-permute-done.10.partner_ref), custom_call_target="tpu_custom_call" | custom-call | tf_op jit(solution)/shard_map/product/pallas_call | solution.py:134
  410.9 12.9 %collective-permute-done.12 = f32[4,128,256]{2,1,0:T(8,128)S(1)} collective-permute-done((f32[4,128,256]{2,1,0:T(8,128)S(1)}, f32[4,128,256]{2,1,0:T(8,128)S(1)}, u32[]{:S(2)}, u32[]{:S(2)}) %collective-permute-start.12) | collective-permute-done | bytes 524320 | tf_op jit(solution)/shard_map/ppermute | solution.py:21
  423.8 10.3 %collective-permute-done.13 = f32[4,128,256]{2,1,0:T(8,128)S(1)} collective-permute-done((f32[4,128,256]{2,1,0:T(8,128)S(1)}, f32[4,128,256]{2,1,0:T(8,128)S(1)}, u32[]{:S(2)}, u32[]{:S(2)}) %collective-permute-start.13) | collective-permute-done | bytes 524320 | tf_op jit(solution)/shard_map/ppermute | solution.py:21
  435.9 2.5 collective-permute-start.16
  440.3 5.2 collective-permute-done.16
  445.6 5.3 collective-permute-done.15
  451.6 14.7 %collective-permute-done.17.partner_ref = f32[8192,128]{1,0:T(8,128)S(1)} collective-permute-done((f32[8192,128]{1,0:T(8,128)}, f32[8192,128]{1,0:T(8,128)S(1)}, u32[]{:S(2)}, u32[]{:S(2)}) %collective-permute-start.17) | collective-permute-done | bytes 4194336 | tf_op jit(solution)/shard_map/ppermute | solution.py:21
  466.3 2.1 collective-permute-start.26
  469.4 27.3 %product.19 = f32[2048,128]{1,0:T(8,128)S(1)} custom-call(f32[2]{0:T(128)S(1)} %pad_maximum_fusion.1.control_ref, bf16[2048,8192]{1,0:T(8,128)(2,1)} %get-tuple-element.47.high_ref, bf16[2048,8192]{1,0:T(8,128)(2,1)} %get-tuple-element.48.low_ref, f32[8192,1024]{1,0:T(8,128)} %bitcast.117, f32[8192,128]{1,0:T(8,128)S(1)} %collective-permute-done.17.partner_ref), custom_call_target="tpu_custom_call" | custom-call | tf_op jit(solution)/shard_map/product/pallas_call | solution.py:134
  496.7 59.4 %collective-permute-done.18.partner_ref = f32[8192,128]{1,0:T(8,128)S(1)} collective-permute-done((f32[8192,128]{1,0:T(8,128)S(1)}, f32[8192,128]{1,0:T(8,128)S(1)}, u32[]{:S(2)}, u32[]{:S(2)}) %collective-permute-start.18) | collective-permute-done | bytes 4194336 | tf_op jit(solution)/shard_map/ppermute | solution.py:21
  556.1 2.1 collective-permute-start.25
  559.2 27.2 %product.20 = f32[2048,128]{1,0:T(8,128)S(1)} custom-call(f32[2]{0:T(128)S(1)} %pad_maximum_fusion.1.control_ref, bf16[2048,8192]{1,0:T(8,128)(2,1)} %get-tuple-element.47.high_ref, bf16[2048,8192]{1,0:T(8,128)(2,1)} %get-tuple-element.48.low_ref, f32[8192,1024]{1,0:T(8,128)} %bitcast.119, f32[8192,128]{1,0:T(8,128)S(1)} %collective-permute-done.18.partner_ref), custom_call_target="tpu_custom_call" | custom-call | tf_op jit(solution)/shard_map/product/pallas_call | solution.py:134
  588.4 12.9 %collective-permute-done.20 = f32[4,128,256]{2,1,0:T(8,128)S(1)} collective-permute-done((f32[4,128,256]{2,1,0:T(8,128)S(1)}, f32[4,128,256]{2,1,0:T(8,128)S(1)}, u32[]{:S(2)}, u32[]{:S(2)}) %collective-permute-start.20) | collective-permute-done | bytes 524320 | tf_op jit(solution)/shard_map/ppermute | solution.py:21
  601.3 10.3 %collective-permute-done.21 = f32[4,128,256]{2,1,0:T(8,128)S(1)} collective-permute-done((f32[4,128,256]{2,1,0:T(8,128)S(1)}, f32[4,128,256]{2,1,0:T(8,128)S(1)}, u32[]{:S(2)}, u32[]{:S(2)}) %collective-permute-start.21) | collective-permute-done | bytes 524320 | tf_op jit(solution)/shard_map/ppermute | solution.py:21
  613.5 2.5 collective-permute-start.24
  616.1 1.8 collective-permute-done.22
  617.9 5.2 collective-permute-done.24
  623.1 5.3 collective-permute-done.23
  630.6 14.9 %product.21.refs_0_ = f32[2048,128]{1,0:T(8,128)S(1)} custom-call(f32[2]{0:T(128)S(1)} %pad_maximum_fusion.1.control_ref, bf16[2048,8192]{1,0:T(8,128)(2,1)} %get-tuple-element.47.high_ref, bf16[2048,8192]{1,0:T(8,128)(2,1)} %get-tuple-element.48.low_ref, f32[8192,1024]{1,0:T(8,128)} %bitcast.121, f32[4096,128]{1,0:T(8,128)S(1)} %collective-permute-done.26.partner_ref), custom_call_target="tpu_custom_call" | custom-call | tf_op jit(solution)/shard_map/product/pallas_call | solution.py:134
  646.0 14.9 %product.22 = f32[2048,128]{1,0:T(8,128)S(1)} custom-call(f32[2]{0:T(128)S(1)} %pad_maximum_fusion.1.control_ref, bf16[2048,8192]{1,0:T(8,128)(2,1)} %get-tuple-element.47.high_ref, bf16[2048,8192]{1,0:T(8,128)(2,1)} %get-tuple-element.48.low_ref, f32[8192,1024]{1,0:T(8,128)} %bitcast.122, f32[4096,128]{1,0:T(8,128)S(1)} %collective-permute-done.25.partner_ref, ...), custom_call_target="tpu_custom_call" | custom-call | tf_op jit(solution)/shard_map/product/pallas_call | solution.py:134
  661.1 2.2 collective-permute-start.29
  663.3 2.0 collective-permute-start.35
  665.3 4.6 collective-permute-done.29
  669.9 5.8 collective-permute-done.28
  675.8 1.8 collective-permute-start.30
  677.7 2.5 collective-permute-start.32
  680.3 4.0 collective-permute-done.32
  684.2 2.1 collective-permute-done.31
  687.9 12.1 %product.23.refs_0_ = f32[2048,128]{1,0:T(8,128)S(1)} custom-call(f32[2]{0:T(128)S(1)} %pad_maximum_fusion.1.control_ref, bf16[2048,8192]{1,0:T(8,128)(2,1)} %get-tuple-element.47.high_ref, bf16[2048,8192]{1,0:T(8,128)(2,1)} %get-tuple-element.48.low_ref, f32[8192,1024]{1,0:T(8,128)} %bitcast.123, f32[3072,128]{1,0:T(8,128)S(1)} %collective-permute-done.33.partner_ref, ...), custom_call_target="tpu_custom_call" | custom-call | tf_op jit(solution)/shard_map/product/pallas_call | solution.py:134
  700.0 2.2 collective-permute-done.35.partner_ref
  702.2 2.1 collective-permute-start.38
  704.3 8.7 %product.24.refs_0_ = f32[2048,128]{1,0:T(8,128)S(1)} custom-call(f32[2]{0:T(128)S(1)} %pad_maximum_fusion.1.control_ref, bf16[2048,8192]{1,0:T(8,128)(2,1)} %get-tuple-element.47.high_ref, bf16[2048,8192]{1,0:T(8,128)(2,1)} %get-tuple-element.48.low_ref, f32[8192,1024]{1,0:T(8,128)} %bitcast.124, f32[2048,128]{1,0:T(8,128)S(1)} %collective-permute-done.35.partner_ref, ...), custom_call_target="tpu_custom_call" | custom-call | tf_op jit(solution)/shard_map/product/pallas_call | solution.py:134
  713.4 2.1 collective-permute-start.36
  715.5 5.1 product.25.refs_0_
  720.6 3.4 product.26.refs_0_
  724.1 3.5 product.27
  733.2 4.4 collective-permute-done.40
  740.7 2.6 collective-permute-start.45
  746.4 4.3 collective-permute-done.44
  (94 shorter events, 43.8 us)
Async XLA Ops:
  1.1 67.6 %collective-permute-start.1 = (f32[1024,128]{1,0:T(8,128)S(1)}, f32[1024,128]{1,0:T(8,128)S(1)}, u32[]{:S(2)}, u32[]{:S(2)}) collective-permute-start(f32[1024,128]{1,0:T(8,128)S(1)} %slice.56), channel_id=1, source_target_pairs={{0,16},{1,17},{2,18},{3,19},{4,20},{5,21},{6,22},{7,23},{8,24},{9,... | collective-permute-start | bytes 1572872 | tf_op jit(solution)/shard_map/ppermute | solution.py:21
  8.6 98.3 %collective-permute-start = (f32[8192,128]{1,0:T(8,128)}, f32[8192,128]{1,0:T(8,128)}, u32[]{:S(2)}, u32[]{:S(2)}) collective-permute-start(f32[8192,128]{1,0:T(8,128)} %slice.43), channel_id=1, source_target_pairs={{0,16},{1,17},{2,18},{3,19},{4,20},{5,21},{6,22},{7,23},{8,24},{9,... | collective-permute-start | bytes 12582920 | tf_op jit(solution)/shard_map/ppermute | solution.py:21
  68.7 128.0 %collective-permute-start.2 = (f32[8192,128]{1,0:T(8,128)}, f32[8192,128]{1,0:T(8,128)}, u32[]{:S(2)}, u32[]{:S(2)}) collective-permute-start(f32[8192,128]{1,0:T(8,128)} %get-tuple-element.57), channel_id=1, source_target_pairs={{0,16},{1,17},{2,18},{3,19},{4,20},{5,21},{6,22},{7,23},{8,24},{9,... | collective-permute-start | bytes 12582920 | tf_op jit(solution)/shard_map/ppermute | solution.py:21
  106.8 179.8 %collective-permute-start.9 = (f32[8192,128]{1,0:T(8,128)}, f32[8192,128]{1,0:T(8,128)}, u32[]{:S(2)}, u32[]{:S(2)}) collective-permute-start(f32[8192,128]{1,0:T(8,128)} %get-tuple-element.60), channel_id=1, source_target_pairs={{0,16},{1,17},{2,18},{3,19},{4,20},{5,21},{6,22},{7,23},{8,24},{9,... | collective-permute-start | bytes 12582920 | tf_op jit(solution)/shard_map/ppermute | solution.py:21
  196.7 179.8 %collective-permute-start.10 = (f32[8192,128]{1,0:T(8,128)}, f32[8192,128]{1,0:T(8,128)}, u32[]{:S(2)}, u32[]{:S(2)}) collective-permute-start(f32[8192,128]{1,0:T(8,128)} %get-tuple-element.63), channel_id=1, source_target_pairs={{0,16},{1,17},{2,18},{3,19},{4,20},{5,21},{6,22},{7,23},{8,24},{9,... | collective-permute-start | bytes 12582920 | tf_op jit(solution)/shard_map/ppermute | solution.py:21
  231.0 2.3 collective-permute-start.3
  231.0 15.0 %collective-permute-start.4 = (f32[4,128,256]{2,1,0:T(8,128)}, f32[4,128,256]{2,1,0:T(8,128)}, u32[]{:S(2)}, u32[]{:S(2)}) collective-permute-start(f32[4,128,256]{2,1,0:T(8,128)} %get-tuple-element.97), channel_id=1, source_target_pairs={{0,2},{1,3},{2,0},{3,1},{4,6},{5,7},{6,4},{7,5},{8,10},{9,11},{10,... | collective-permute-start | bytes 1572872 | tf_op jit(solution)/shard_map/ppermute | solution.py:21
  232.5 24.0 %collective-permute-start.5 = (f32[4,128,256]{2,1,0:T(8,128)}, f32[4,128,256]{2,1,0:T(8,128)}, u32[]{:S(2)}, u32[]{:S(2)}) collective-permute-start(f32[4,128,256]{2,1,0:T(8,128)} %get-tuple-element.98), channel_id=1, source_target_pairs={{0,3},{1,2},{2,1},{3,0},{4,7},{5,6},{6,5},{7,4},{8,11},{9,10},{10,... | collective-permute-start | bytes 1572872 | tf_op jit(solution)/shard_map/ppermute | solution.py:21
  258.0 0.8 copy-start.1
  258.8 6.0 collective-permute-start.6
  260.4 9.7 %collective-permute-start.8 = (f32[1,128,256]{2,1,0:T(8,128)S(1)}, f32[1,128,256]{2,1,0:T(8,128)S(1)}, u32[]{:S(2)}, u32[]{:S(2)}) collective-permute-start(f32[1,128,256]{2,1,0:T(8,128)S(1)} %get-tuple-element.112), channel_id=1, source_target_pairs={{0,12},{1,13},{2,14},{3,15},{4,8},{5,9},{6,10},{7,11},{8,4},{9,5},... | collective-permute-start | bytes 393224 | tf_op jit(solution)/shard_map/ppermute | solution.py:21
  262.9 12.4 %collective-permute-start.7 = (f32[1,128,256]{2,1,0:T(8,128)S(1)}, f32[1,128,256]{2,1,0:T(8,128)S(1)}, u32[]{:S(2)}, u32[]{:S(2)}) collective-permute-start(f32[1,128,256]{2,1,0:T(8,128)S(1)} %get-tuple-element.113), channel_id=1, source_target_pairs={{0,8},{1,9},{2,10},{3,11},{4,12},{5,13},{6,14},{7,15},{8,0},{9,1},... | collective-permute-start | bytes 393224 | tf_op jit(solution)/shard_map/ppermute | solution.py:21
  286.6 179.7 %collective-permute-start.17 = (f32[8192,128]{1,0:T(8,128)}, f32[8192,128]{1,0:T(8,128)S(1)}, u32[]{:S(2)}, u32[]{:S(2)}) collective-permute-start(f32[8192,128]{1,0:T(8,128)} %get-tuple-element.66), channel_id=1, source_target_pairs={{0,16},{1,17},{2,18},{3,19},{4,20},{5,21},{6,22},{7,23},{8,24},{9,... | collective-permute-start | bytes 12582920 | tf_op jit(solution)/shard_map/ppermute | solution.py:21
  290.2 86.3 %copy-start = (f32[8192,128]{1,0:T(8,128)S(1)}, f32[8192,128]{1,0:T(8,128)}, u32[]{:S(2)}) copy-start(f32[8192,128]{1,0:T(8,128)} %get-tuple-element.69) | copy-start | bytes 12582916
  376.5 179.7 %collective-permute-start.18 = (f32[8192,128]{1,0:T(8,128)S(1)}, f32[8192,128]{1,0:T(8,128)S(1)}, u32[]{:S(2)}, u32[]{:S(2)}) collective-permute-start(f32[8192,128]{1,0:T(8,128)S(1)} %copy-done), channel_id=1, source_target_pairs={{0,16},{1,17},{2,18},{3,19},{4,20},{5,21},{6,22},{7,23},{8,24},{9,... | collective-permute-start | bytes 12582920 | tf_op jit(solution)/shard_map/ppermute | solution.py:21
  408.9 2.0 collective-permute-start.11
  409.0 14.8 %collective-permute-start.12 = (f32[4,128,256]{2,1,0:T(8,128)S(1)}, f32[4,128,256]{2,1,0:T(8,128)S(1)}, u32[]{:S(2)}, u32[]{:S(2)}) collective-permute-start(f32[4,128,256]{2,1,0:T(8,128)S(1)} %get-tuple-element.94), channel_id=1, source_target_pairs={{0,2},{1,3},{2,0},{3,1},{4,6},{5,7},{6,4},{7,5},{8,10},{9,11},{10,... | collective-permute-start | bytes 1572872 | tf_op jit(solution)/shard_map/ppermute | solution.py:21
  410.6 55.7 %copy-start.2 = (f32[4096,128]{1,0:T(8,128)S(1)}, f32[4096,128]{1,0:T(8,128)}, u32[]{:S(2)}) copy-start(f32[4096,128]{1,0:T(8,128)} %slice.49) | copy-start | bytes 6291460
  410.6 23.5 %collective-permute-start.13 = (f32[4,128,256]{2,1,0:T(8,128)S(1)}, f32[4,128,256]{2,1,0:T(8,128)S(1)}, u32[]{:S(2)}, u32[]{:S(2)}) collective-permute-start(f32[4,128,256]{2,1,0:T(8,128)S(1)} %get-tuple-element.95), channel_id=1, source_target_pairs={{0,3},{1,2},{2,1},{3,0},{4,7},{5,6},{6,5},{7,4},{8,11},{9,10},{10,... | collective-permute-start | bytes 1572872 | tf_op jit(solution)/shard_map/ppermute | solution.py:21
  434.3 6.0 collective-permute-start.14
  435.9 9.6 %collective-permute-start.16 = (f32[1,128,256]{2,1,0:T(8,128)S(1)}, f32[1,128,256]{2,1,0:T(8,128)S(1)}, u32[]{:S(2)}, u32[]{:S(2)}) collective-permute-start(f32[1,128,256]{2,1,0:T(8,128)S(1)} %get-tuple-element.109), channel_id=1, source_target_pairs={{0,12},{1,13},{2,14},{3,15},{4,8},{5,9},{6,10},{7,11},{8,4},{9,5},... | collective-permute-start | bytes 393224 | tf_op jit(solution)/shard_map/ppermute | solution.py:21
  438.4 12.5 %collective-permute-start.15 = (f32[1,128,256]{2,1,0:T(8,128)S(1)}, f32[1,128,256]{2,1,0:T(8,128)S(1)}, u32[]{:S(2)}, u32[]{:S(2)}) collective-permute-start(f32[1,128,256]{2,1,0:T(8,128)S(1)} %get-tuple-element.110), channel_id=1, source_target_pairs={{0,8},{1,9},{2,10},{3,11},{4,12},{5,13},{6,14},{7,15},{8,0},{9,1},... | collective-permute-start | bytes 393224 | tf_op jit(solution)/shard_map/ppermute | solution.py:21
  466.3 162.9 %collective-permute-start.26 = (f32[4096,128]{1,0:T(8,128)S(1)}, f32[4096,128]{1,0:T(8,128)S(1)}, u32[]{:S(2)}, u32[]{:S(2)}) collective-permute-start(f32[4096,128]{1,0:T(8,128)S(1)} %copy-done.2), channel_id=1, source_target_pairs={{0,16},{1,17},{2,18},{3,19},{4,20},{5,21},{6,22},{7,23},{8,24},{9,... | collective-permute-start | bytes 6291464 | tf_op jit(solution)/shard_map/ppermute | solution.py:21
  469.4 86.7 %copy-start.3 = (f32[4096,128]{1,0:T(8,128)S(1)}, f32[4096,128]{1,0:T(8,128)}, u32[]{:S(2)}) copy-start(f32[4096,128]{1,0:T(8,128)} %slice.50) | copy-start | bytes 6291460
  556.1 89.9 %collective-permute-start.25 = (f32[4096,128]{1,0:T(8,128)S(1)}, f32[4096,128]{1,0:T(8,128)S(1)}, u32[]{:S(2)}, u32[]{:S(2)}) collective-permute-start(f32[4096,128]{1,0:T(8,128)S(1)} %copy-done.3), channel_id=1, source_target_pairs={{0,16},{1,17},{2,18},{3,19},{4,20},{5,21},{6,22},{7,23},{8,24},{9,... | collective-permute-start | bytes 6291464 | tf_op jit(solution)/shard_map/ppermute | solution.py:21
  586.5 2.0 collective-permute-start.19
  586.5 14.8 %collective-permute-start.20 = (f32[4,128,256]{2,1,0:T(8,128)S(1)}, f32[4,128,256]{2,1,0:T(8,128)S(1)}, u32[]{:S(2)}, u32[]{:S(2)}) collective-permute-start(f32[4,128,256]{2,1,0:T(8,128)S(1)} %get-tuple-element.91), channel_id=1, source_target_pairs={{0,2},{1,3},{2,0},{3,1},{4,6},{5,7},{6,4},{7,5},{8,10},{9,11},{10,... | collective-permute-start | bytes 1572872 | tf_op jit(solution)/shard_map/ppermute | solution.py:21
  588.1 23.5 %collective-permute-start.21 = (f32[4,128,256]{2,1,0:T(8,128)S(1)}, f32[4,128,256]{2,1,0:T(8,128)S(1)}, u32[]{:S(2)}, u32[]{:S(2)}) collective-permute-start(f32[4,128,256]{2,1,0:T(8,128)S(1)} %get-tuple-element.92), channel_id=1, source_target_pairs={{0,3},{1,2},{2,1},{3,0},{4,7},{5,6},{6,5},{7,4},{8,11},{9,10},{10,... | collective-permute-start | bytes 1572872 | tf_op jit(solution)/shard_map/ppermute | solution.py:21
  611.8 6.0 collective-permute-start.22
  613.5 9.6 %collective-permute-start.24 = (f32[1,128,256]{2,1,0:T(8,128)S(1)}, f32[1,128,256]{2,1,0:T(8,128)S(1)}, u32[]{:S(2)}, u32[]{:S(2)}) collective-permute-start(f32[1,128,256]{2,1,0:T(8,128)S(1)} %get-tuple-element.106), channel_id=1, source_target_pairs={{0,12},{1,13},{2,14},{3,15},{4,8},{5,9},{6,10},{7,11},{8,4},{9,5},... | collective-permute-start | bytes 393224 | tf_op jit(solution)/shard_map/ppermute | solution.py:21
  615.9 12.5 %collective-permute-start.23 = (f32[1,128,256]{2,1,0:T(8,128)S(1)}, f32[1,128,256]{2,1,0:T(8,128)S(1)}, u32[]{:S(2)}, u32[]{:S(2)}) collective-permute-start(f32[1,128,256]{2,1,0:T(8,128)S(1)} %get-tuple-element.107), channel_id=1, source_target_pairs={{0,8},{1,9},{2,10},{3,11},{4,12},{5,13},{6,14},{7,15},{8,0},{9,1},... | collective-permute-start | bytes 393224 | tf_op jit(solution)/shard_map/ppermute | solution.py:21
  629.1 57.2 %collective-permute-start.33 = (f32[3072,128]{1,0:T(8,128)S(1)}, f32[3072,128]{1,0:T(8,128)S(1)}, u32[]{:S(2)}, u32[]{:S(2)}) collective-permute-start(f32[3072,128]{1,0:T(8,128)S(1)} %slice.51), channel_id=1, source_target_pairs={{0,16},{1,17},{2,18},{3,19},{4,20},{5,21},{6,22},{7,23},{8,24},{9,... | collective-permute-start | bytes 4718600 | tf_op jit(solution)/shard_map/ppermute | solution.py:21
  645.5 17.8 %copy-start.7 = (f32[2048,128]{1,0:T(8,128)S(1)}, f32[2048,128]{1,0:T(8,128)}, u32[]{:S(2)}) copy-start(f32[2048,128]{1,0:T(8,128)} %slice.52) | copy-start | bytes 3145732
  661.0 4.3 collective-permute-start.27
  661.1 8.8 %collective-permute-start.29 = (f32[4,128,128]{2,1,0:T(8,128)S(1)}, f32[4,128,128]{2,1,0:T(8,128)S(1)}, u32[]{:S(2)}, u32[]{:S(2)}) collective-permute-start(f32[4,128,128]{2,1,0:T(8,128)S(1)} %get-tuple-element.100), channel_id=1, source_target_pairs={{0,3},{1,2},{2,1},{3,0},{4,7},{5,6},{6,5},{7,4},{8,11},{9,10},{10,... | collective-permute-start | bytes 786440 | tf_op jit(solution)/shard_map/ppermute | solution.py:21
  663.3 12.5 %collective-permute-start.28 = (f32[4,128,128]{2,1,0:T(8,128)S(1)}, f32[4,128,128]{2,1,0:T(8,128)S(1)}, u32[]{:S(2)}, u32[]{:S(2)}) collective-permute-start(f32[4,128,128]{2,1,0:T(8,128)S(1)} %get-tuple-element.101), channel_id=1, source_target_pairs={{0,2},{1,3},{2,0},{3,1},{4,6},{5,7},{6,4},{7,5},{8,10},{9,11},{10,... | collective-permute-start | bytes 786440 | tf_op jit(solution)/shard_map/ppermute | solution.py:21
  663.3 38.9 %collective-permute-start.35 = (f32[2048,128]{1,0:T(8,128)S(1)}, f32[2048,128]{1,0:T(8,128)S(1)}, u32[]{:S(2)}, u32[]{:S(2)}) collective-permute-start(f32[2048,128]{1,0:T(8,128)S(1)} %copy-done.7), channel_id=1, source_target_pairs={{0,16},{1,17},{2,18},{3,19},{4,20},{5,21},{6,22},{7,23},{8,24},{9,... | collective-permute-start | bytes 3145736 | tf_op jit(solution)/shard_map/ppermute | solution.py:21
  675.8 4.4 collective-permute-start.30
  677.7 6.6 collective-permute-start.32
  680.1 6.2 collective-permute-start.31
  686.4 27.1 %collective-permute-start.34 = (f32[1024,128]{1,0:T(8,128)S(1)}, f32[1024,128]{1,0:T(8,128)S(1)}, u32[]{:S(2)}, u32[]{:S(2)}) collective-permute-start(f32[1024,128]{1,0:T(8,128)S(1)} %slice.53), channel_id=1, source_target_pairs={{0,16},{1,17},{2,18},{3,19},{4,20},{5,21},{6,22},{7,23},{8,24},{9,... | collective-permute-start | bytes 1572872 | tf_op jit(solution)/shard_map/ppermute | solution.py:21
  702.2 18.4 %collective-permute-start.38 = (f32[512,128]{1,0:T(8,128)S(1)}, f32[512,128]{1,0:T(8,128)S(1)}, u32[]{:S(2)}, u32[]{:S(2)}) collective-permute-start(f32[512,128]{1,0:T(8,128)S(1)} %slice.54), channel_id=1, source_target_pairs={{0,16},{1,17},{2,18},{3,19},{4,20},{5,21},{6,22},{7,23},{8,24},{9,... | collective-permute-start | bytes 786440 | tf_op jit(solution)/shard_map/ppermute | solution.py:21
  713.4 10.7 %collective-permute-start.36 = (f32[512,128]{1,0:T(8,128)S(1)}, f32[512,128]{1,0:T(8,128)S(1)}, u32[]{:S(2)}, u32[]{:S(2)}) collective-permute-start(f32[512,128]{1,0:T(8,128)S(1)} %slice.55), channel_id=1, source_target_pairs={{0,16},{1,17},{2,18},{3,19},{4,20},{5,21},{6,22},{7,23},{8,24},{9,... | collective-permute-start | bytes 786440 | tf_op jit(solution)/shard_map/ppermute | solution.py:21
  724.0 3.6 copy-start.4
  724.1 3.6 copy-start.5
  724.1 3.6 copy-start.6
  727.6 2.0 collective-permute-start.39
  727.7 12.9 %collective-permute-start.37 = (f32[128,896]{1,0:T(8,128)S(1)}, f32[128,896]{1,0:T(8,128)S(1)}, u32[]{:S(2)}, u32[]{:S(2)}) collective-permute-start(f32[128,896]{1,0:T(8,128)S(1)} %pad_maximum_fusion), channel_id=1, source_target_pairs={{0,16},{1,17},{2,18},{3,19},{4,20},{5,21},{6,22},{7,23},{8,24},{9,... | collective-permute-start | bytes 1376264 | tf_op jit(solution)/shard_map/ppermute | solution.py:21
  729.7 8.0 %collective-permute-start.40 = (f32[2,128,128]{2,1,0:T(8,128)S(1)}, f32[2,128,128]{2,1,0:T(8,128)S(1)}, u32[]{:S(2)}, u32[]{:S(2)}) collective-permute-start(f32[2,128,128]{2,1,0:T(8,128)S(1)} %get-tuple-element.102), channel_id=1, source_target_pairs={{0,2},{1,3},{2,0},{3,1},{4,6},{5,7},{6,4},{7,5},{8,10},{9,11},{10,... | collective-permute-start | bytes 393224 | tf_op jit(solution)/shard_map/ppermute | solution.py:21
  731.3 7.3 collective-permute-start.42
  732.8 6.5 collective-permute-start.41
  740.7 5.7 collective-permute-start.45
  743.3 7.3 collective-permute-start.44
  744.5 6.2 collective-permute-start.43

commit v4 on v3

--- a/solution.py
+++ b/solution.py
@@ -190,8 +190,9 @@
             if later not in blocks:
                 blocks[later] = block(later, done)
                 partner = after(partner, blocks[later])
-        if index + ahead < len(pieces):
-            arrived.append(swapped(after(blocks[index + ahead], arrived[index], done), pair))
+        ready = index + ahead + (index + ahead >= len(pieces) - 4)
+        while len(arrived) < min(ready + 1, len(pieces)):
+            arrived.append(swapped(after(blocks[len(arrived)], arrived[index], done), pair))
         operands = (control, high, low, own, partner, pieces[index], totals.get(chunk))
         if index + 1 == len(pieces):
             kept, given = product(*operands, owned=matrix.shape[0] // pair)

time: 752 us -> 752 us (level)
  transfers between devices with their start and end apart: 46 -> 46, of which waited for: 36 -> 38; matrix products, arithmetic and copies ran while one was open for 5% -> 5% of each run, Pallas kernels for 37% -> 37%
where the time goes in v4:
time: 752 us
  waiting for transfers between devices  372 us (49%)
  Pallas kernels  279 us (37%)
  starting transfers between devices  57.9 us (8%)
  local copies, waits for them, and re-layouts  33.7 us (4%)
  other arithmetic  8.39 us (1%)
    ppermute x46, waiting for transfers between devices, swapped(): lax.ppermute(value, AXES, [(source, source ^ mask) for source in range(de...  372 us
    pallas_call x14, Pallas kernels, product(): pl.pallas_call(functools.partial(product_kernel, total is not None, owned...  234 us
    ppermute x46, starting transfers between devices, swapped(): lax.ppermute(value, AXES, [(source, source ^ mask) for source in range(de...  57.9 us
    pallas_call x1, Pallas kernels, split_matrix(): pl.pallas_call(split_kernel, grid=(rows // step,), in_specs=[spec], out_s...  44.9 us
    slice x10, local copies, waits for them, and re-layouts, block(): return source[start:start + size, chunk * LANES:(chunk + 1) * LANES]  32.6 us
  transfers between devices with their start and end apart: 46, of which 38 were waited for; matrix products, arithmetic and copies ran while one was open for 5% of the time, Pallas kernels for 37%

profile of v4, /device:TPU:0, one launch (start us, length us, event | category | flops | bytes accessed | tf_op | source)
XLA Modules:
  0.0 751.7 jit_solution(11213848709163316534)
XLA Ops:
  1.1 3.0 collective-permute-start.1
  4.1 4.5 slice.43
  8.6 44.9 %split_matrix.1 = (bf16[2048,8192]{1,0:T(8,128)(2,1)}, bf16[2048,8192]{1,0:T(8,128)(2,1)}) custom-call(f32[2048,8192]{1,0:T(8,128)} %bitcast.2.matrix_ref), custom_call_target="tpu_custom_call" | custom-call | bytes 134217728 | tf_op jit(solution)/shard_map/split_matrix/pallas_call | solution.py:65
  53.5 15.2 %fusion.37 = (f32[8192,128]{1,0:T(8,128)}, f32[8192,128]{1,0:T(8,128)}, f32[8192,128]{1,0:T(8,128)}, f32[8192,128]{1,0:T(8,128)}, f32[8192,128]{1,0:T(8,128)}) fusion(f32[8192,1024]{1,0:T(8,128)} %bitcast.106), kind=kLoop, calls=%fused_computation.92 | loop fusion | bytes 41943040 | tf_op jit(solution)/shard_map/slice | solution.py:177
  68.7 2.1 collective-permute-start.2
  70.8 5.1 product.14.refs_0_
  75.9 30.9 %collective-permute-done.partner_ref = f32[8192,128]{1,0:T(8,128)} collective-permute-done((f32[8192,128]{1,0:T(8,128)}, f32[8192,128]{1,0:T(8,128)}, u32[]{:S(2)}, u32[]{:S(2)}) %collective-permute-start) | collective-permute-done | bytes 4194336 | tf_op jit(solution)/shard_map/ppermute | solution.py:21
  106.8 2.1 collective-permute-start.9
  108.9 3.0 slice.49
  111.9 28.0 %product.15 = f32[2048,128]{1,0:T(8,128)S(1)} custom-call(f32[2]{0:T(128)S(1)} %pad_maximum_fusion.1.control_ref, bf16[2048,8192]{1,0:T(8,128)(2,1)} %get-tuple-element.47.high_ref, bf16[2048,8192]{1,0:T(8,128)(2,1)} %get-tuple-element.48.low_ref, f32[8192,1024]{1,0:T(8,128)} %bitcast.109, f32[8192,128]{1,0:T(8,128)} %collective-permute-done.partner_ref), custom_call_target="tpu_custom_call" | custom-call | tf_op jit(solution)/shard_map/product/pallas_call | solution.py:134
  139.9 56.8 %collective-permute-done.2.partner_ref = f32[8192,128]{1,0:T(8,128)} collective-permute-done((f32[8192,128]{1,0:T(8,128)}, f32[8192,128]{1,0:T(8,128)}, u32[]{:S(2)}, u32[]{:S(2)}) %collective-permute-start.2) | collective-permute-done | bytes 4194336 | tf_op jit(solution)/shard_map/ppermute | solution.py:21
  196.7 2.1 collective-permute-start.10
  198.8 3.0 slice.50
  201.8 28.0 %product.16 = f32[2048,128]{1,0:T(8,128)S(1)} custom-call(f32[2]{0:T(128)S(1)} %pad_maximum_fusion.1.control_ref, bf16[2048,8192]{1,0:T(8,128)(2,1)} %get-tuple-element.47.high_ref, bf16[2048,8192]{1,0:T(8,128)(2,1)} %get-tuple-element.48.low_ref, f32[8192,1024]{1,0:T(8,128)} %bitcast.111, f32[8192,128]{1,0:T(8,128)} %collective-permute-done.2.partner_ref), custom_call_target="tpu_custom_call" | custom-call | tf_op jit(solution)/shard_map/product/pallas_call | solution.py:134
  233.2 12.8 %collective-permute-done.4 = f32[4,128,256]{2,1,0:T(8,128)} collective-permute-done((f32[4,128,256]{2,1,0:T(8,128)}, f32[4,128,256]{2,1,0:T(8,128)}, u32[]{:S(2)}, u32[]{:S(2)}) %collective-permute-start.4) | collective-permute-done | bytes 524320 | tf_op jit(solution)/shard_map/ppermute | solution.py:21
  246.0 10.5 %collective-permute-done.5 = f32[4,128,256]{2,1,0:T(8,128)} collective-permute-done((f32[4,128,256]{2,1,0:T(8,128)}, f32[4,128,256]{2,1,0:T(8,128)}, u32[]{:S(2)}, u32[]{:S(2)}) %collective-permute-start.5) | collective-permute-done | bytes 524320 | tf_op jit(solution)/shard_map/ppermute | solution.py:21
  260.4 2.5 collective-permute-start.8
  263.0 1.8 collective-permute-done.6
  264.8 5.3 collective-permute-done.8
  270.1 5.2 collective-permute-done.7
  276.9 9.7 %collective-permute-done.9.partner_ref = f32[8192,128]{1,0:T(8,128)} collective-permute-done((f32[8192,128]{1,0:T(8,128)}, f32[8192,128]{1,0:T(8,128)}, u32[]{:S(2)}, u32[]{:S(2)}) %collective-permute-start.9) | collective-permute-done | bytes 4194336 | tf_op jit(solution)/shard_map/ppermute | solution.py:21
  286.6 2.1 collective-permute-start.17
  290.2 28.2 %product.17 = f32[2048,128]{1,0:T(8,128)S(1)} custom-call(f32[2]{0:T(128)S(1)} %pad_maximum_fusion.1.control_ref, bf16[2048,8192]{1,0:T(8,128)(2,1)} %get-tuple-element.47.high_ref, bf16[2048,8192]{1,0:T(8,128)(2,1)} %get-tuple-element.48.low_ref, f32[8192,1024]{1,0:T(8,128)} %bitcast.113, f32[8192,128]{1,0:T(8,128)} %collective-permute-done.9.partner_ref), custom_call_target="tpu_custom_call" | custom-call | tf_op jit(solution)/shard_map/product/pallas_call | solution.py:134
  318.4 58.1 %collective-permute-done.10.partner_ref = f32[8192,128]{1,0:T(8,128)} collective-permute-done((f32[8192,128]{1,0:T(8,128)}, f32[8192,128]{1,0:T(8,128)}, u32[]{:S(2)}, u32[]{:S(2)}) %collective-permute-start.10) | collective-permute-done | bytes 4194336 | tf_op jit(solution)/shard_map/ppermute | solution.py:21
  376.5 2.1 collective-permute-start.18
  379.8 28.1 %product.18 = f32[2048,128]{1,0:T(8,128)S(1)} custom-call(f32[2]{0:T(128)S(1)} %pad_maximum_fusion.1.control_ref, bf16[2048,8192]{1,0:T(8,128)(2,1)} %get-tuple-element.47.high_ref, bf16[2048,8192]{1,0:T(8,128)(2,1)} %get-tuple-element.48.low_ref, f32[8192,1024]{1,0:T(8,128)} %bitcast.115, f32[8192,128]{1,0:T(8,128)} %collective-permute-done.10.partner_ref), custom_call_target="tpu_custom_call" | custom-call | tf_op jit(solution)/shard_map/product/pallas_call | solution.py:134
  410.1 12.9 %collective-permute-done.12 = f32[4,128,256]{2,1,0:T(8,128)S(1)} collective-permute-done((f32[4,128,256]{2,1,0:T(8,128)S(1)}, f32[4,128,256]{2,1,0:T(8,128)S(1)}, u32[]{:S(2)}, u32[]{:S(2)}) %collective-permute-start.12) | collective-permute-done | bytes 524320 | tf_op jit(solution)/shard_map/ppermute | solution.py:21
  423.0 10.3 %collective-permute-done.13 = f32[4,128,256]{2,1,0:T(8,128)S(1)} collective-permute-done((f32[4,128,256]{2,1,0:T(8,128)S(1)}, f32[4,128,256]{2,1,0:T(8,128)S(1)}, u32[]{:S(2)}, u32[]{:S(2)}) %collective-permute-start.13) | collective-permute-done | bytes 524320 | tf_op jit(solution)/shard_map/ppermute | solution.py:21
  435.1 2.5 collective-permute-start.16
  437.7 1.8 collective-permute-done.14
  439.5 5.2 collective-permute-done.16
  444.8 5.3 collective-permute-done.15
  450.8 15.5 %collective-permute-done.17.partner_ref = f32[8192,128]{1,0:T(8,128)S(1)} collective-permute-done((f32[8192,128]{1,0:T(8,128)}, f32[8192,128]{1,0:T(8,128)S(1)}, u32[]{:S(2)}, u32[]{:S(2)}) %collective-permute-start.17) | collective-permute-done | bytes 4194336 | tf_op jit(solution)/shard_map/ppermute | solution.py:21
  466.3 2.1 collective-permute-start.26
  469.4 27.3 %product.19 = f32[2048,128]{1,0:T(8,128)S(1)} custom-call(f32[2]{0:T(128)S(1)} %pad_maximum_fusion.1.control_ref, bf16[2048,8192]{1,0:T(8,128)(2,1)} %get-tuple-element.47.high_ref, bf16[2048,8192]{1,0:T(8,128)(2,1)} %get-tuple-element.48.low_ref, f32[8192,1024]{1,0:T(8,128)} %bitcast.117, f32[8192,128]{1,0:T(8,128)S(1)} %collective-permute-done.17.partner_ref), custom_call_target="tpu_custom_call" | custom-call | tf_op jit(solution)/shard_map/product/pallas_call | solution.py:134
  496.7 59.4 %collective-permute-done.18.partner_ref = f32[8192,128]{1,0:T(8,128)S(1)} collective-permute-done((f32[8192,128]{1,0:T(8,128)S(1)}, f32[8192,128]{1,0:T(8,128)S(1)}, u32[]{:S(2)}, u32[]{:S(2)}) %collective-permute-start.18) | collective-permute-done | bytes 4194336 | tf_op jit(solution)/shard_map/ppermute | solution.py:21
  556.1 2.1 collective-permute-start.25
  559.2 27.2 %product.20 = f32[2048,128]{1,0:T(8,128)S(1)} custom-call(f32[2]{0:T(128)S(1)} %pad_maximum_fusion.1.control_ref, bf16[2048,8192]{1,0:T(8,128)(2,1)} %get-tuple-element.47.high_ref, bf16[2048,8192]{1,0:T(8,128)(2,1)} %get-tuple-element.48.low_ref, f32[8192,1024]{1,0:T(8,128)} %bitcast.119, f32[8192,128]{1,0:T(8,128)S(1)} %collective-permute-done.18.partner_ref), custom_call_target="tpu_custom_call" | custom-call | tf_op jit(solution)/shard_map/product/pallas_call | solution.py:134
  588.4 12.9 %collective-permute-done.20 = f32[4,128,256]{2,1,0:T(8,128)S(1)} collective-permute-done((f32[4,128,256]{2,1,0:T(8,128)S(1)}, f32[4,128,256]{2,1,0:T(8,128)S(1)}, u32[]{:S(2)}, u32[]{:S(2)}) %collective-permute-start.20) | collective-permute-done | bytes 524320 | tf_op jit(solution)/shard_map/ppermute | solution.py:21
  601.3 10.3 %collective-permute-done.21 = f32[4,128,256]{2,1,0:T(8,128)S(1)} collective-permute-done((f32[4,128,256]{2,1,0:T(8,128)S(1)}, f32[4,128,256]{2,1,0:T(8,128)S(1)}, u32[]{:S(2)}, u32[]{:S(2)}) %collective-permute-start.21) | collective-permute-done | bytes 524320 | tf_op jit(solution)/shard_map/ppermute | solution.py:21
  611.8 1.6 collective-permute-start.22
  613.5 2.5 collective-permute-start.24
  616.1 1.8 collective-permute-done.22
  617.9 5.2 collective-permute-done.24
  623.1 5.3 collective-permute-done.23
  630.6 14.9 %product.21.refs_0_ = f32[2048,128]{1,0:T(8,128)S(1)} custom-call(f32[2]{0:T(128)S(1)} %pad_maximum_fusion.1.control_ref, bf16[2048,8192]{1,0:T(8,128)(2,1)} %get-tuple-element.47.high_ref, bf16[2048,8192]{1,0:T(8,128)(2,1)} %get-tuple-element.48.low_ref, f32[8192,1024]{1,0:T(8,128)} %bitcast.121, f32[4096,128]{1,0:T(8,128)S(1)} %collective-permute-done.26.partner_ref), custom_call_target="tpu_custom_call" | custom-call | tf_op jit(solution)/shard_map/product/pallas_call | solution.py:134
  646.0 2.1 collective-permute-start.33
  648.1 14.9 %product.22 = f32[2048,128]{1,0:T(8,128)S(1)} custom-call(f32[2]{0:T(128)S(1)} %pad_maximum_fusion.1.control_ref, bf16[2048,8192]{1,0:T(8,128)(2,1)} %get-tuple-element.47.high_ref, bf16[2048,8192]{1,0:T(8,128)(2,1)} %get-tuple-element.48.low_ref, f32[8192,1024]{1,0:T(8,128)} %bitcast.122, f32[4096,128]{1,0:T(8,128)S(1)} %collective-permute-done.25.partner_ref, ...), custom_call_target="tpu_custom_call" | custom-call | tf_op jit(solution)/shard_map/product/pallas_call | solution.py:134
  665.3 6.1 collective-permute-done.29
  671.4 6.0 collective-permute-done.28
  679.1 2.5 collective-permute-start.32
  682.3 3.4 collective-permute-done.32
  685.7 2.1 collective-permute-done.31
  688.5 12.1 %product.23.refs_0_ = f32[2048,128]{1,0:T(8,128)S(1)} custom-call(f32[2]{0:T(128)S(1)} %pad_maximum_fusion.1.control_ref, bf16[2048,8192]{1,0:T(8,128)(2,1)} %get-tuple-element.47.high_ref, bf16[2048,8192]{1,0:T(8,128)(2,1)} %get-tuple-element.48.low_ref, f32[8192,1024]{1,0:T(8,128)} %bitcast.123, f32[3072,128]{1,0:T(8,128)S(1)} %collective-permute-done.34.partner_ref, ...), custom_call_target="tpu_custom_call" | custom-call | tf_op jit(solution)/shard_map/product/pallas_call | solution.py:134
  702.2 2.1 collective-permute-start.35
  704.3 8.7 %product.24.refs_0_ = f32[2048,128]{1,0:T(8,128)S(1)} custom-call(f32[2]{0:T(128)S(1)} %pad_maximum_fusion.1.control_ref, bf16[2048,8192]{1,0:T(8,128)(2,1)} %get-tuple-element.47.high_ref, bf16[2048,8192]{1,0:T(8,128)(2,1)} %get-tuple-element.48.low_ref, f32[8192,1024]{1,0:T(8,128)} %bitcast.124, f32[2048,128]{1,0:T(8,128)S(1)} %collective-permute-done.33.partner_ref, ...), custom_call_target="tpu_custom_call" | custom-call | tf_op jit(solution)/shard_map/product/pallas_call | solution.py:134
  713.4 5.1 product.25.refs_0_
  719.0 3.4 product.26.refs_0_
  723.8 3.4 product.27
  727.4 1.8 collective-permute-start.36
  729.3 1.8 collective-permute-start.40
  732.9 4.2 collective-permute-done.40
  740.5 2.9 collective-permute-start.45
  746.3 4.4 collective-permute-done.44
  (92 shorter events, 43.2 us)
Async XLA Ops:
  1.1 67.6 %collective-permute-start.1 = (f32[1024,128]{1,0:T(8,128)S(1)}, f32[1024,128]{1,0:T(8,128)S(1)}, u32[]{:S(2)}, u32[]{:S(2)}) collective-permute-start(f32[1024,128]{1,0:T(8,128)S(1)} %slice.56), channel_id=1, source_target_pairs={{0,16},{1,17},{2,18},{3,19},{4,20},{5,21},{6,22},{7,23},{8,24},{9,... | collective-permute-start | bytes 1572872 | tf_op jit(solution)/shard_map/ppermute | solution.py:21
  8.6 98.3 %collective-permute-start = (f32[8192,128]{1,0:T(8,128)}, f32[8192,128]{1,0:T(8,128)}, u32[]{:S(2)}, u32[]{:S(2)}) collective-permute-start(f32[8192,128]{1,0:T(8,128)} %slice.43), channel_id=1, source_target_pairs={{0,16},{1,17},{2,18},{3,19},{4,20},{5,21},{6,22},{7,23},{8,24},{9,... | collective-permute-start | bytes 12582920 | tf_op jit(solution)/shard_map/ppermute | solution.py:21
  68.7 128.0 %collective-permute-start.2 = (f32[8192,128]{1,0:T(8,128)}, f32[8192,128]{1,0:T(8,128)}, u32[]{:S(2)}, u32[]{:S(2)}) collective-permute-start(f32[8192,128]{1,0:T(8,128)} %get-tuple-element.57), channel_id=1, source_target_pairs={{0,16},{1,17},{2,18},{3,19},{4,20},{5,21},{6,22},{7,23},{8,24},{9,... | collective-permute-start | bytes 12582920 | tf_op jit(solution)/shard_map/ppermute | solution.py:21
  106.8 179.8 %collective-permute-start.9 = (f32[8192,128]{1,0:T(8,128)}, f32[8192,128]{1,0:T(8,128)}, u32[]{:S(2)}, u32[]{:S(2)}) collective-permute-start(f32[8192,128]{1,0:T(8,128)} %get-tuple-element.60), channel_id=1, source_target_pairs={{0,16},{1,17},{2,18},{3,19},{4,20},{5,21},{6,22},{7,23},{8,24},{9,... | collective-permute-start | bytes 12582920 | tf_op jit(solution)/shard_map/ppermute | solution.py:21
  196.7 179.8 %collective-permute-start.10 = (f32[8192,128]{1,0:T(8,128)}, f32[8192,128]{1,0:T(8,128)}, u32[]{:S(2)}, u32[]{:S(2)}) collective-permute-start(f32[8192,128]{1,0:T(8,128)} %get-tuple-element.63), channel_id=1, source_target_pairs={{0,16},{1,17},{2,18},{3,19},{4,20},{5,21},{6,22},{7,23},{8,24},{9,... | collective-permute-start | bytes 12582920 | tf_op jit(solution)/shard_map/ppermute | solution.py:21
  230.9 2.3 collective-permute-start.3
  230.9 15.0 %collective-permute-start.4 = (f32[4,128,256]{2,1,0:T(8,128)}, f32[4,128,256]{2,1,0:T(8,128)}, u32[]{:S(2)}, u32[]{:S(2)}) collective-permute-start(f32[4,128,256]{2,1,0:T(8,128)} %get-tuple-element.97), channel_id=1, source_target_pairs={{0,2},{1,3},{2,0},{3,1},{4,6},{5,7},{6,4},{7,5},{8,10},{9,11},{10,... | collective-permute-start | bytes 1572872 | tf_op jit(solution)/shard_map/ppermute | solution.py:21
  232.5 24.0 %collective-permute-start.5 = (f32[4,128,256]{2,1,0:T(8,128)}, f32[4,128,256]{2,1,0:T(8,128)}, u32[]{:S(2)}, u32[]{:S(2)}) collective-permute-start(f32[4,128,256]{2,1,0:T(8,128)} %get-tuple-element.98), channel_id=1, source_target_pairs={{0,3},{1,2},{2,1},{3,0},{4,7},{5,6},{6,5},{7,4},{8,11},{9,10},{10,... | collective-permute-start | bytes 1572872 | tf_op jit(solution)/shard_map/ppermute | solution.py:21
  258.0 0.8 copy-start.1
  258.8 6.0 collective-permute-start.6
  260.4 9.7 %collective-permute-start.8 = (f32[1,128,256]{2,1,0:T(8,128)S(1)}, f32[1,128,256]{2,1,0:T(8,128)S(1)}, u32[]{:S(2)}, u32[]{:S(2)}) collective-permute-start(f32[1,128,256]{2,1,0:T(8,128)S(1)} %get-tuple-element.112), channel_id=1, source_target_pairs={{0,12},{1,13},{2,14},{3,15},{4,8},{5,9},{6,10},{7,11},{8,4},{9,5},... | collective-permute-start | bytes 393224 | tf_op jit(solution)/shard_map/ppermute | solution.py:21
  262.9 12.4 %collective-permute-start.7 = (f32[1,128,256]{2,1,0:T(8,128)S(1)}, f32[1,128,256]{2,1,0:T(8,128)S(1)}, u32[]{:S(2)}, u32[]{:S(2)}) collective-permute-start(f32[1,128,256]{2,1,0:T(8,128)S(1)} %get-tuple-element.113), channel_id=1, source_target_pairs={{0,8},{1,9},{2,10},{3,11},{4,12},{5,13},{6,14},{7,15},{8,0},{9,1},... | collective-permute-start | bytes 393224 | tf_op jit(solution)/shard_map/ppermute | solution.py:21
  286.6 179.7 %collective-permute-start.17 = (f32[8192,128]{1,0:T(8,128)}, f32[8192,128]{1,0:T(8,128)S(1)}, u32[]{:S(2)}, u32[]{:S(2)}) collective-permute-start(f32[8192,128]{1,0:T(8,128)} %get-tuple-element.66), channel_id=1, source_target_pairs={{0,16},{1,17},{2,18},{3,19},{4,20},{5,21},{6,22},{7,23},{8,24},{9,... | collective-permute-start | bytes 12582920 | tf_op jit(solution)/shard_map/ppermute | solution.py:21
  290.2 86.3 %copy-start = (f32[8192,128]{1,0:T(8,128)S(1)}, f32[8192,128]{1,0:T(8,128)}, u32[]{:S(2)}) copy-start(f32[8192,128]{1,0:T(8,128)} %get-tuple-element.69) | copy-start | bytes 12582916
  376.5 179.7 %collective-permute-start.18 = (f32[8192,128]{1,0:T(8,128)S(1)}, f32[8192,128]{1,0:T(8,128)S(1)}, u32[]{:S(2)}, u32[]{:S(2)}) collective-permute-start(f32[8192,128]{1,0:T(8,128)S(1)} %copy-done), channel_id=1, source_target_pairs={{0,16},{1,17},{2,18},{3,19},{4,20},{5,21},{6,22},{7,23},{8,24},{9,... | collective-permute-start | bytes 12582920 | tf_op jit(solution)/shard_map/ppermute | solution.py:21
  408.1 2.0 collective-permute-start.11
  408.2 14.8 %collective-permute-start.12 = (f32[4,128,256]{2,1,0:T(8,128)S(1)}, f32[4,128,256]{2,1,0:T(8,128)S(1)}, u32[]{:S(2)}, u32[]{:S(2)}) collective-permute-start(f32[4,128,256]{2,1,0:T(8,128)S(1)} %get-tuple-element.94), channel_id=1, source_target_pairs={{0,2},{1,3},{2,0},{3,1},{4,6},{5,7},{6,4},{7,5},{8,10},{9,11},{10,... | collective-permute-start | bytes 1572872 | tf_op jit(solution)/shard_map/ppermute | solution.py:21
  409.8 56.5 %copy-start.2 = (f32[4096,128]{1,0:T(8,128)S(1)}, f32[4096,128]{1,0:T(8,128)}, u32[]{:S(2)}) copy-start(f32[4096,128]{1,0:T(8,128)} %slice.49) | copy-start | bytes 6291460
  409.8 23.5 %collective-permute-start.13 = (f32[4,128,256]{2,1,0:T(8,128)S(1)}, f32[4,128,256]{2,1,0:T(8,128)S(1)}, u32[]{:S(2)}, u32[]{:S(2)}) collective-permute-start(f32[4,128,256]{2,1,0:T(8,128)S(1)} %get-tuple-element.95), channel_id=1, source_target_pairs={{0,3},{1,2},{2,1},{3,0},{4,7},{5,6},{6,5},{7,4},{8,11},{9,10},{10,... | collective-permute-start | bytes 1572872 | tf_op jit(solution)/shard_map/ppermute | solution.py:21
  433.5 6.0 collective-permute-start.14
  435.1 9.6 %collective-permute-start.16 = (f32[1,128,256]{2,1,0:T(8,128)S(1)}, f32[1,128,256]{2,1,0:T(8,128)S(1)}, u32[]{:S(2)}, u32[]{:S(2)}) collective-permute-start(f32[1,128,256]{2,1,0:T(8,128)S(1)} %get-tuple-element.109), channel_id=1, source_target_pairs={{0,12},{1,13},{2,14},{3,15},{4,8},{5,9},{6,10},{7,11},{8,4},{9,5},... | collective-permute-start | bytes 393224 | tf_op jit(solution)/shard_map/ppermute | solution.py:21
  437.6 12.5 %collective-permute-start.15 = (f32[1,128,256]{2,1,0:T(8,128)S(1)}, f32[1,128,256]{2,1,0:T(8,128)S(1)}, u32[]{:S(2)}, u32[]{:S(2)}) collective-permute-start(f32[1,128,256]{2,1,0:T(8,128)S(1)} %get-tuple-element.110), channel_id=1, source_target_pairs={{0,8},{1,9},{2,10},{3,11},{4,12},{5,13},{6,14},{7,15},{8,0},{9,1},... | collective-permute-start | bytes 393224 | tf_op jit(solution)/shard_map/ppermute | solution.py:21
  466.3 162.9 %collective-permute-start.26 = (f32[4096,128]{1,0:T(8,128)S(1)}, f32[4096,128]{1,0:T(8,128)S(1)}, u32[]{:S(2)}, u32[]{:S(2)}) collective-permute-start(f32[4096,128]{1,0:T(8,128)S(1)} %copy-done.2), channel_id=1, source_target_pairs={{0,16},{1,17},{2,18},{3,19},{4,20},{5,21},{6,22},{7,23},{8,24},{9,... | collective-permute-start | bytes 6291464 | tf_op jit(solution)/shard_map/ppermute | solution.py:21
  469.4 86.7 %copy-start.3 = (f32[4096,128]{1,0:T(8,128)S(1)}, f32[4096,128]{1,0:T(8,128)}, u32[]{:S(2)}) copy-start(f32[4096,128]{1,0:T(8,128)} %slice.50) | copy-start | bytes 6291460
  556.1 89.9 %collective-permute-start.25 = (f32[4096,128]{1,0:T(8,128)S(1)}, f32[4096,128]{1,0:T(8,128)S(1)}, u32[]{:S(2)}, u32[]{:S(2)}) collective-permute-start(f32[4096,128]{1,0:T(8,128)S(1)} %copy-done.3), channel_id=1, source_target_pairs={{0,16},{1,17},{2,18},{3,19},{4,20},{5,21},{6,22},{7,23},{8,24},{9,... | collective-permute-start | bytes 6291464 | tf_op jit(solution)/shard_map/ppermute | solution.py:21
  586.5 2.0 collective-permute-start.19
  586.5 14.8 %collective-permute-start.20 = (f32[4,128,256]{2,1,0:T(8,128)S(1)}, f32[4,128,256]{2,1,0:T(8,128)S(1)}, u32[]{:S(2)}, u32[]{:S(2)}) collective-permute-start(f32[4,128,256]{2,1,0:T(8,128)S(1)} %get-tuple-element.91), channel_id=1, source_target_pairs={{0,2},{1,3},{2,0},{3,1},{4,6},{5,7},{6,4},{7,5},{8,10},{9,11},{10,... | collective-permute-start | bytes 1572872 | tf_op jit(solution)/shard_map/ppermute | solution.py:21
  588.1 23.5 %collective-permute-start.21 = (f32[4,128,256]{2,1,0:T(8,128)S(1)}, f32[4,128,256]{2,1,0:T(8,128)S(1)}, u32[]{:S(2)}, u32[]{:S(2)}) collective-permute-start(f32[4,128,256]{2,1,0:T(8,128)S(1)} %get-tuple-element.92), channel_id=1, source_target_pairs={{0,3},{1,2},{2,1},{3,0},{4,7},{5,6},{6,5},{7,4},{8,11},{9,10},{10,... | collective-permute-start | bytes 1572872 | tf_op jit(solution)/shard_map/ppermute | solution.py:21
  611.8 6.0 collective-permute-start.22
  613.5 9.6 %collective-permute-start.24 = (f32[1,128,256]{2,1,0:T(8,128)S(1)}, f32[1,128,256]{2,1,0:T(8,128)S(1)}, u32[]{:S(2)}, u32[]{:S(2)}) collective-permute-start(f32[1,128,256]{2,1,0:T(8,128)S(1)} %get-tuple-element.106), channel_id=1, source_target_pairs={{0,12},{1,13},{2,14},{3,15},{4,8},{5,9},{6,10},{7,11},{8,4},{9,5},... | collective-permute-start | bytes 393224 | tf_op jit(solution)/shard_map/ppermute | solution.py:21
  615.9 12.5 %collective-permute-start.23 = (f32[1,128,256]{2,1,0:T(8,128)S(1)}, f32[1,128,256]{2,1,0:T(8,128)S(1)}, u32[]{:S(2)}, u32[]{:S(2)}) collective-permute-start(f32[1,128,256]{2,1,0:T(8,128)S(1)} %get-tuple-element.107), channel_id=1, source_target_pairs={{0,8},{1,9},{2,10},{3,11},{4,12},{5,13},{6,14},{7,15},{8,0},{9,1},... | collective-permute-start | bytes 393224 | tf_op jit(solution)/shard_map/ppermute | solution.py:21
  629.1 58.7 %collective-permute-start.34 = (f32[3072,128]{1,0:T(8,128)S(1)}, f32[3072,128]{1,0:T(8,128)S(1)}, u32[]{:S(2)}, u32[]{:S(2)}) collective-permute-start(f32[3072,128]{1,0:T(8,128)S(1)} %slice.51), channel_id=1, source_target_pairs={{0,16},{1,17},{2,18},{3,19},{4,20},{5,21},{6,22},{7,23},{8,24},{9,... | collective-permute-start | bytes 4718600 | tf_op jit(solution)/shard_map/ppermute | solution.py:21
  646.0 56.2 %collective-permute-start.33 = (f32[2048,128]{1,0:T(8,128)S(1)}, f32[2048,128]{1,0:T(8,128)S(1)}, u32[]{:S(2)}, u32[]{:S(2)}) collective-permute-start(f32[2048,128]{1,0:T(8,128)S(1)} %slice.52), channel_id=1, source_target_pairs={{0,16},{1,17},{2,18},{3,19},{4,20},{5,21},{6,22},{7,23},{8,24},{9,... | collective-permute-start | bytes 3145736 | tf_op jit(solution)/shard_map/ppermute | solution.py:21
  663.0 2.2 collective-permute-start.27
  663.1 8.3 %collective-permute-start.29 = (f32[4,128,128]{2,1,0:T(8,128)S(1)}, f32[4,128,128]{2,1,0:T(8,128)S(1)}, u32[]{:S(2)}, u32[]{:S(2)}) collective-permute-start(f32[4,128,128]{2,1,0:T(8,128)S(1)} %get-tuple-element.100), channel_id=1, source_target_pairs={{0,3},{1,2},{2,1},{3,0},{4,7},{5,6},{6,5},{7,4},{8,11},{9,10},{10,... | collective-permute-start | bytes 786440 | tf_op jit(solution)/shard_map/ppermute | solution.py:21
  664.8 12.7 %collective-permute-start.28 = (f32[4,128,128]{2,1,0:T(8,128)S(1)}, f32[4,128,128]{2,1,0:T(8,128)S(1)}, u32[]{:S(2)}, u32[]{:S(2)}) collective-permute-start(f32[4,128,128]{2,1,0:T(8,128)S(1)} %get-tuple-element.101), channel_id=1, source_target_pairs={{0,2},{1,3},{2,0},{3,1},{4,6},{5,7},{6,4},{7,5},{8,10},{9,11},{10,... | collective-permute-start | bytes 786440 | tf_op jit(solution)/shard_map/ppermute | solution.py:21
  677.5 4.3 collective-permute-start.30
  679.1 6.6 collective-permute-start.32
  681.6 6.2 collective-permute-start.31
  681.8 31.6 %collective-permute-start.38 = (f32[1024,128]{1,0:T(8,128)S(1)}, f32[1024,128]{1,0:T(8,128)S(1)}, u32[]{:S(2)}, u32[]{:S(2)}) collective-permute-start(f32[1024,128]{1,0:T(8,128)S(1)} %slice.53), channel_id=1, source_target_pairs={{0,16},{1,17},{2,18},{3,19},{4,20},{5,21},{6,22},{7,23},{8,24},{9,... | collective-permute-start | bytes 1572872 | tf_op jit(solution)/shard_map/ppermute | solution.py:21
  687.9 31.2 %collective-permute-start.37 = (f32[512,128]{1,0:T(8,128)S(1)}, f32[512,128]{1,0:T(8,128)S(1)}, u32[]{:S(2)}, u32[]{:S(2)}) collective-permute-start(f32[512,128]{1,0:T(8,128)S(1)} %slice.54), channel_id=1, source_target_pairs={{0,16},{1,17},{2,18},{3,19},{4,20},{5,21},{6,22},{7,23},{8,24},{9,... | collective-permute-start | bytes 786440 | tf_op jit(solution)/shard_map/ppermute | solution.py:21
  702.2 21.6 %collective-permute-start.35 = (f32[512,128]{1,0:T(8,128)S(1)}, f32[512,128]{1,0:T(8,128)S(1)}, u32[]{:S(2)}, u32[]{:S(2)}) collective-permute-start(f32[512,128]{1,0:T(8,128)S(1)} %slice.55), channel_id=1, source_target_pairs={{0,16},{1,17},{2,18},{3,19},{4,20},{5,21},{6,22},{7,23},{8,24},{9,... | collective-permute-start | bytes 786440 | tf_op jit(solution)/shard_map/ppermute | solution.py:21
  722.4 4.9 copy-start.4
  722.4 4.9 copy-start.5
  722.4 4.9 copy-start.6
  727.2 2.0 collective-permute-start.39
  727.4 13.0 %collective-permute-start.36 = (f32[128,896]{1,0:T(8,128)S(1)}, f32[128,896]{1,0:T(8,128)}, u32[]{:S(2)}, u32[]{:S(2)}) collective-permute-start(f32[128,896]{1,0:T(8,128)S(1)} %pad_maximum_fusion), channel_id=1, source_target_pairs={{0,16},{1,17},{2,18},{3,19},{4,20},{5,21},{6,22},{7,23},{8,24},{9,... | collective-permute-start | bytes 1376264 | tf_op jit(solution)/shard_map/ppermute | solution.py:21
  729.3 7.8 %collective-permute-start.40 = (f32[2,128,128]{2,1,0:T(8,128)S(1)}, f32[2,128,128]{2,1,0:T(8,128)S(1)}, u32[]{:S(2)}, u32[]{:S(2)}) collective-permute-start(f32[2,128,128]{2,1,0:T(8,128)S(1)} %get-tuple-element.102), channel_id=1, source_target_pairs={{0,2},{1,3},{2,0},{3,1},{4,6},{5,7},{6,4},{7,5},{8,10},{9,11},{10,... | collective-permute-start | bytes 393224 | tf_op jit(solution)/shard_map/ppermute | solution.py:21
  731.2 7.3 collective-permute-start.42
  732.7 6.4 collective-permute-start.41
  740.5 5.9 collective-permute-start.45
  743.3 7.4 collective-permute-start.44
  744.6 6.2 collective-permute-start.43

commit v5 on v3

--- a/solution.py
+++ b/solution.py
@@ -206,14 +206,15 @@
                 sums.append(done)
                 waiting = []
 
-    early = jnp.concatenate(sums, axis=1)
-    early_partner = swapped(after(early, arrived[-1]), pair)
+    first, rest = sums[0], jnp.concatenate(sums[1:], axis=1)
+    first_partner = swapped(after(first, arrived[-1]), pair)
+    rest_partner = swapped(after(rest, first_partner), pair)
     late = kept + swapped(given, 1)
     late = scattered_sum(late, 1, [2] * ((bits - 2) // 2) + [1] * (bits % 2))
-    late = after(late, early_partner)
-    result = jnp.concatenate(
-        [0.5 * (early_partner + sign * early), scattered_halves(late, bits - 1, 1, sign)[0]], axis=1
-    )
+    late = after(scattered_sum(late, bits - 1, [1])[0], rest_partner)
+    late_partner = swapped(late, pair)
+    early = [0.5 * (first_partner + sign * first), 0.5 * (rest_partner + sign * rest)]
+    result = jnp.concatenate([*early, 0.5 * (late_partner + sign * late)], axis=1)
     return result[None]
 
 

time: 752 us -> 750 us (level)
  no operation moved by 1% of the time
where the time goes in v5:
time: 750 us
  waiting for transfers between devices  367 us (49%)
  Pallas kernels  279 us (37%)
  starting transfers between devices  61.5 us (8%)
  local copies, waits for them, and re-layouts  34.7 us (5%)
    ppermute x46, waiting for transfers between devices, swapped(): lax.ppermute(value, AXES, [(source, source ^ mask) for source in range(de...  367 us
    pallas_call x14, Pallas kernels, product(): pl.pallas_call(functools.partial(product_kernel, total is not None, owned...  234 us
    ppermute x46, starting transfers between devices, swapped(): lax.ppermute(value, AXES, [(source, source ^ mask) for source in range(de...  61.5 us
    pallas_call x1, Pallas kernels, split_matrix(): pl.pallas_call(split_kernel, grid=(rows // step,), in_specs=[spec], out_s...  44.9 us
    slice x10, local copies, waits for them, and re-layouts, block(): return source[start:start + size, chunk * LANES:(chunk + 1) * LANES]  33.6 us
  transfers between devices with their start and end apart: 46, of which 36 were waited for; matrix products, arithmetic and copies ran while one was open for 5% of the time, Pallas kernels for 37%

profile of v5, /device:TPU:0, one launch (start us, length us, event | category | flops | bytes accessed | tf_op | source)
XLA Modules:
  0.0 749.8 jit_solution(16820336804841957180)
XLA Ops:
  1.1 3.0 collective-permute-start.1
  4.1 4.5 slice.43
  8.6 44.9 %split_matrix.1 = (bf16[2048,8192]{1,0:T(8,128)(2,1)}, bf16[2048,8192]{1,0:T(8,128)(2,1)}) custom-call(f32[2048,8192]{1,0:T(8,128)} %bitcast.2.matrix_ref), custom_call_target="tpu_custom_call" | custom-call | bytes 134217728 | tf_op jit(solution)/shard_map/split_matrix/pallas_call | solution.py:65
  53.5 15.2 %fusion.37 = (f32[8192,128]{1,0:T(8,128)}, f32[8192,128]{1,0:T(8,128)}, f32[8192,128]{1,0:T(8,128)}, f32[8192,128]{1,0:T(8,128)}, f32[8192,128]{1,0:T(8,128)}) fusion(f32[8192,1024]{1,0:T(8,128)} %bitcast.106), kind=kLoop, calls=%fused_computation.93 | loop fusion | bytes 41943040 | tf_op jit(solution)/shard_map/slice | solution.py:177
  68.7 2.1 collective-permute-start.2
  70.8 5.1 product.14.refs_0_
  75.9 30.9 %collective-permute-done.partner_ref = f32[8192,128]{1,0:T(8,128)} collective-permute-done((f32[8192,128]{1,0:T(8,128)}, f32[8192,128]{1,0:T(8,128)}, u32[]{:S(2)}, u32[]{:S(2)}) %collective-permute-start) | collective-permute-done | bytes 4194336 | tf_op jit(solution)/shard_map/ppermute | solution.py:21
  106.8 2.1 collective-permute-start.9
  108.9 3.0 slice.49
  111.9 28.0 %product.15 = f32[2048,128]{1,0:T(8,128)S(1)} custom-call(f32[2]{0:T(128)S(1)} %pad_maximum_fusion.1.control_ref, bf16[2048,8192]{1,0:T(8,128)(2,1)} %get-tuple-element.48.high_ref, bf16[2048,8192]{1,0:T(8,128)(2,1)} %get-tuple-element.49.low_ref, f32[8192,1024]{1,0:T(8,128)} %bitcast.109, f32[8192,128]{1,0:T(8,128)} %collective-permute-done.partner_ref), custom_call_target="tpu_custom_call" | custom-call | tf_op jit(solution)/shard_map/product/pallas_call | solution.py:134
  139.9 56.8 %collective-permute-done.2.partner_ref = f32[8192,128]{1,0:T(8,128)} collective-permute-done((f32[8192,128]{1,0:T(8,128)}, f32[8192,128]{1,0:T(8,128)}, u32[]{:S(2)}, u32[]{:S(2)}) %collective-permute-start.2) | collective-permute-done | bytes 4194336 | tf_op jit(solution)/shard_map/ppermute | solution.py:21
  196.7 2.1 collective-permute-start.11
  198.8 3.0 slice.50
  201.8 28.0 %product.16 = f32[2048,128]{1,0:T(8,128)S(1)} custom-call(f32[2]{0:T(128)S(1)} %pad_maximum_fusion.1.control_ref, bf16[2048,8192]{1,0:T(8,128)(2,1)} %get-tuple-element.48.high_ref, bf16[2048,8192]{1,0:T(8,128)(2,1)} %get-tuple-element.49.low_ref, f32[8192,1024]{1,0:T(8,128)} %bitcast.111, f32[8192,128]{1,0:T(8,128)} %collective-permute-done.2.partner_ref), custom_call_target="tpu_custom_call" | custom-call | tf_op jit(solution)/shard_map/product/pallas_call | solution.py:134
  233.2 12.8 %collective-permute-done.4 = f32[4,128,256]{2,1,0:T(8,128)} collective-permute-done((f32[4,128,256]{2,1,0:T(8,128)}, f32[4,128,256]{2,1,0:T(8,128)}, u32[]{:S(2)}, u32[]{:S(2)}) %collective-permute-start.4) | collective-permute-done | bytes 524320 | tf_op jit(solution)/shard_map/ppermute | solution.py:21
  246.0 10.5 %collective-permute-done.5 = f32[4,128,256]{2,1,0:T(8,128)} collective-permute-done((f32[4,128,256]{2,1,0:T(8,128)}, f32[4,128,256]{2,1,0:T(8,128)}, u32[]{:S(2)}, u32[]{:S(2)}) %collective-permute-start.5) | collective-permute-done | bytes 524320 | tf_op jit(solution)/shard_map/ppermute | solution.py:21
  260.4 2.5 collective-permute-start.8
  264.8 5.3 collective-permute-done.8
  270.1 5.2 collective-permute-done.7
  276.9 9.7 %collective-permute-done.9.partner_ref = f32[8192,128]{1,0:T(8,128)} collective-permute-done((f32[8192,128]{1,0:T(8,128)}, f32[8192,128]{1,0:T(8,128)}, u32[]{:S(2)}, u32[]{:S(2)}) %collective-permute-start.9) | collective-permute-done | bytes 4194336 | tf_op jit(solution)/shard_map/ppermute | solution.py:21
  286.6 2.1 collective-permute-start.10
  290.2 28.2 %product.17 = f32[2048,128]{1,0:T(8,128)S(1)} custom-call(f32[2]{0:T(128)S(1)} %pad_maximum_fusion.1.control_ref, bf16[2048,8192]{1,0:T(8,128)(2,1)} %get-tuple-element.48.high_ref, bf16[2048,8192]{1,0:T(8,128)(2,1)} %get-tuple-element.49.low_ref, f32[8192,1024]{1,0:T(8,128)} %bitcast.113, f32[8192,128]{1,0:T(8,128)} %collective-permute-done.9.partner_ref), custom_call_target="tpu_custom_call" | custom-call | tf_op jit(solution)/shard_map/product/pallas_call | solution.py:134
  318.4 58.1 %collective-permute-done.11.partner_ref = f32[8192,128]{1,0:T(8,128)} collective-permute-done((f32[8192,128]{1,0:T(8,128)}, f32[8192,128]{1,0:T(8,128)}, u32[]{:S(2)}, u32[]{:S(2)}) %collective-permute-start.11) | collective-permute-done | bytes 4194336 | tf_op jit(solution)/shard_map/ppermute | solution.py:21
  376.5 2.1 collective-permute-start.18
  378.5 2.3 slice.52
  380.8 28.0 %product.18 = f32[2048,128]{1,0:T(8,128)S(1)} custom-call(f32[2]{0:T(128)S(1)} %pad_maximum_fusion.1.control_ref, bf16[2048,8192]{1,0:T(8,128)(2,1)} %get-tuple-element.48.high_ref, bf16[2048,8192]{1,0:T(8,128)(2,1)} %get-tuple-element.49.low_ref, f32[8192,1024]{1,0:T(8,128)} %bitcast.115, f32[8192,128]{1,0:T(8,128)} %collective-permute-done.11.partner_ref), custom_call_target="tpu_custom_call" | custom-call | tf_op jit(solution)/shard_map/product/pallas_call | solution.py:134
  410.9 12.9 %collective-permute-done.13 = f32[4,128,256]{2,1,0:T(8,128)S(1)} collective-permute-done((f32[4,128,256]{2,1,0:T(8,128)S(1)}, f32[4,128,256]{2,1,0:T(8,128)S(1)}, u32[]{:S(2)}, u32[]{:S(2)}) %collective-permute-start.13) | collective-permute-done | bytes 524320 | tf_op jit(solution)/shard_map/ppermute | solution.py:21
  423.8 10.3 %collective-permute-done.14 = f32[4,128,256]{2,1,0:T(8,128)S(1)} collective-permute-done((f32[4,128,256]{2,1,0:T(8,128)S(1)}, f32[4,128,256]{2,1,0:T(8,128)S(1)}, u32[]{:S(2)}, u32[]{:S(2)}) %collective-permute-start.14) | collective-permute-done | bytes 524320 | tf_op jit(solution)/shard_map/ppermute | solution.py:21
  435.9 2.5 collective-permute-start.17
  440.3 5.2 collective-permute-done.17
  445.6 5.3 collective-permute-done.16
  451.6 14.7 %collective-permute-done.10.partner_ref = f32[8192,128]{1,0:T(8,128)S(1)} collective-permute-done((f32[8192,128]{1,0:T(8,128)}, f32[8192,128]{1,0:T(8,128)S(1)}, u32[]{:S(2)}, u32[]{:S(2)}) %collective-permute-start.10) | collective-permute-done | bytes 4194336 | tf_op jit(solution)/shard_map/ppermute | solution.py:21
  466.3 2.1 collective-permute-start.25
  469.4 27.3 %product.19 = f32[2048,128]{1,0:T(8,128)S(1)} custom-call(f32[2]{0:T(128)S(1)} %pad_maximum_fusion.1.control_ref, bf16[2048,8192]{1,0:T(8,128)(2,1)} %get-tuple-element.48.high_ref, bf16[2048,8192]{1,0:T(8,128)(2,1)} %get-tuple-element.49.low_ref, f32[8192,1024]{1,0:T(8,128)} %bitcast.117, f32[8192,128]{1,0:T(8,128)S(1)} %collective-permute-done.10.partner_ref), custom_call_target="tpu_custom_call" | custom-call | tf_op jit(solution)/shard_map/product/pallas_call | solution.py:134
  496.7 59.4 %collective-permute-done.18.partner_ref = f32[8192,128]{1,0:T(8,128)S(1)} collective-permute-done((f32[8192,128]{1,0:T(8,128)S(1)}, f32[8192,128]{1,0:T(8,128)S(1)}, u32[]{:S(2)}, u32[]{:S(2)}) %collective-permute-start.18) | collective-permute-done | bytes 4194336 | tf_op jit(solution)/shard_map/ppermute | solution.py:21
  556.1 2.1 collective-permute-start.27
  559.2 27.2 %product.20 = f32[2048,128]{1,0:T(8,128)S(1)} custom-call(f32[2]{0:T(128)S(1)} %pad_maximum_fusion.1.control_ref, bf16[2048,8192]{1,0:T(8,128)(2,1)} %get-tuple-element.48.high_ref, bf16[2048,8192]{1,0:T(8,128)(2,1)} %get-tuple-element.49.low_ref, f32[8192,1024]{1,0:T(8,128)} %bitcast.119, f32[8192,128]{1,0:T(8,128)S(1)} %collective-permute-done.18.partner_ref), custom_call_target="tpu_custom_call" | custom-call | tf_op jit(solution)/shard_map/product/pallas_call | solution.py:134
  588.4 12.9 %collective-permute-done.20 = f32[4,128,256]{2,1,0:T(8,128)S(1)} collective-permute-done((f32[4,128,256]{2,1,0:T(8,128)S(1)}, f32[4,128,256]{2,1,0:T(8,128)S(1)}, u32[]{:S(2)}, u32[]{:S(2)}) %collective-permute-start.20) | collective-permute-done | bytes 524320 | tf_op jit(solution)/shard_map/ppermute | solution.py:21
  601.3 10.3 %collective-permute-done.21 = f32[4,128,256]{2,1,0:T(8,128)S(1)} collective-permute-done((f32[4,128,256]{2,1,0:T(8,128)S(1)}, f32[4,128,256]{2,1,0:T(8,128)S(1)}, u32[]{:S(2)}, u32[]{:S(2)}) %collective-permute-start.21) | collective-permute-done | bytes 524320 | tf_op jit(solution)/shard_map/ppermute | solution.py:21
  613.5 2.5 collective-permute-start.24
  617.9 5.2 collective-permute-done.24
  623.1 5.3 collective-permute-done.23
  630.6 14.9 %product.21.refs_0_ = f32[2048,128]{1,0:T(8,128)S(1)} custom-call(f32[2]{0:T(128)S(1)} %pad_maximum_fusion.1.control_ref, bf16[2048,8192]{1,0:T(8,128)(2,1)} %get-tuple-element.48.high_ref, bf16[2048,8192]{1,0:T(8,128)(2,1)} %get-tuple-element.49.low_ref, f32[8192,1024]{1,0:T(8,128)} %bitcast.121, f32[4096,128]{1,0:T(8,128)S(1)} %collective-permute-done.25.partner_ref), custom_call_target="tpu_custom_call" | custom-call | tf_op jit(solution)/shard_map/product/pallas_call | solution.py:134
  646.0 14.9 %product.22 = f32[2048,128]{1,0:T(8,128)S(1)} custom-call(f32[2]{0:T(128)S(1)} %pad_maximum_fusion.1.control_ref, bf16[2048,8192]{1,0:T(8,128)(2,1)} %get-tuple-element.48.high_ref, bf16[2048,8192]{1,0:T(8,128)(2,1)} %get-tuple-element.49.low_ref, f32[8192,1024]{1,0:T(8,128)} %bitcast.122, f32[4096,128]{1,0:T(8,128)S(1)} %collective-permute-done.27.partner_ref, ...), custom_call_target="tpu_custom_call" | custom-call | tf_op jit(solution)/shard_map/product/pallas_call | solution.py:134
  661.1 2.2 collective-permute-start.30
  663.3 2.0 collective-permute-start.35
  665.3 4.6 collective-permute-done.30
  669.9 5.8 collective-permute-done.29
  675.8 1.8 collective-permute-start.31
  677.7 2.5 collective-permute-start.33
  680.3 4.0 collective-permute-done.33
  684.2 2.1 collective-permute-done.32
  687.9 12.1 %product.23.refs_0_ = f32[2048,128]{1,0:T(8,128)S(1)} custom-call(f32[2]{0:T(128)S(1)} %pad_maximum_fusion.1.control_ref, bf16[2048,8192]{1,0:T(8,128)(2,1)} %get-tuple-element.48.high_ref, bf16[2048,8192]{1,0:T(8,128)(2,1)} %get-tuple-element.49.low_ref, f32[8192,1024]{1,0:T(8,128)} %bitcast.123, f32[3072,128]{1,0:T(8,128)S(1)} %collective-permute-done.26.partner_ref, ...), custom_call_target="tpu_custom_call" | custom-call | tf_op jit(solution)/shard_map/product/pallas_call | solution.py:134
  700.0 2.2 collective-permute-done.35.partner_ref
  702.2 2.1 collective-permute-start.39
  704.3 8.7 %product.24.refs_0_ = f32[2048,128]{1,0:T(8,128)S(1)} custom-call(f32[2]{0:T(128)S(1)} %pad_maximum_fusion.1.control_ref, bf16[2048,8192]{1,0:T(8,128)(2,1)} %get-tuple-element.48.high_ref, bf16[2048,8192]{1,0:T(8,128)(2,1)} %get-tuple-element.49.low_ref, f32[8192,1024]{1,0:T(8,128)} %bitcast.124, f32[2048,128]{1,0:T(8,128)S(1)} %collective-permute-done.35.partner_ref, ...), custom_call_target="tpu_custom_call" | custom-call | tf_op jit(solution)/shard_map/product/pallas_call | solution.py:134
  713.4 2.1 collective-permute-start.36
  715.5 5.1 product.25.refs_0_
  720.6 3.4 product.26.refs_0_
  724.1 3.4 product.27
  735.0 2.6 collective-permute-done.41
  739.3 2.7 collective-permute-start.44
  742.0 2.6 collective-permute-done.44
  746.2 2.8 collective-permute-done.45
  (96 shorter events, 44.6 us)
Async XLA Ops:
  1.1 67.6 %collective-permute-start.1 = (f32[1024,128]{1,0:T(8,128)S(1)}, f32[1024,128]{1,0:T(8,128)S(1)}, u32[]{:S(2)}, u32[]{:S(2)}) collective-permute-start(f32[1024,128]{1,0:T(8,128)S(1)} %slice.56), channel_id=1, source_target_pairs={{0,16},{1,17},{2,18},{3,19},{4,20},{5,21},{6,22},{7,23},{8,24},{9,... | collective-permute-start | bytes 1572872 | tf_op jit(solution)/shard_map/ppermute | solution.py:21
  8.6 98.3 %collective-permute-start = (f32[8192,128]{1,0:T(8,128)}, f32[8192,128]{1,0:T(8,128)}, u32[]{:S(2)}, u32[]{:S(2)}) collective-permute-start(f32[8192,128]{1,0:T(8,128)} %slice.43), channel_id=1, source_target_pairs={{0,16},{1,17},{2,18},{3,19},{4,20},{5,21},{6,22},{7,23},{8,24},{9,... | collective-permute-start | bytes 12582920 | tf_op jit(solution)/shard_map/ppermute | solution.py:21
  68.7 128.0 %collective-permute-start.2 = (f32[8192,128]{1,0:T(8,128)}, f32[8192,128]{1,0:T(8,128)}, u32[]{:S(2)}, u32[]{:S(2)}) collective-permute-start(f32[8192,128]{1,0:T(8,128)} %get-tuple-element.58), channel_id=1, source_target_pairs={{0,16},{1,17},{2,18},{3,19},{4,20},{5,21},{6,22},{7,23},{8,24},{9,... | collective-permute-start | bytes 12582920 | tf_op jit(solution)/shard_map/ppermute | solution.py:21
  106.8 179.8 %collective-permute-start.9 = (f32[8192,128]{1,0:T(8,128)}, f32[8192,128]{1,0:T(8,128)}, u32[]{:S(2)}, u32[]{:S(2)}) collective-permute-start(f32[8192,128]{1,0:T(8,128)} %get-tuple-element.61), channel_id=1, source_target_pairs={{0,16},{1,17},{2,18},{3,19},{4,20},{5,21},{6,22},{7,23},{8,24},{9,... | collective-permute-start | bytes 12582920 | tf_op jit(solution)/shard_map/ppermute | solution.py:21
  196.7 179.8 %collective-permute-start.11 = (f32[8192,128]{1,0:T(8,128)}, f32[8192,128]{1,0:T(8,128)}, u32[]{:S(2)}, u32[]{:S(2)}) collective-permute-start(f32[8192,128]{1,0:T(8,128)} %get-tuple-element.65), channel_id=1, source_target_pairs={{0,16},{1,17},{2,18},{3,19},{4,20},{5,21},{6,22},{7,23},{8,24},{9,... | collective-permute-start | bytes 12582920 | tf_op jit(solution)/shard_map/ppermute | solution.py:21
  230.9 2.3 collective-permute-start.3
  230.9 15.0 %collective-permute-start.4 = (f32[4,128,256]{2,1,0:T(8,128)}, f32[4,128,256]{2,1,0:T(8,128)}, u32[]{:S(2)}, u32[]{:S(2)}) collective-permute-start(f32[4,128,256]{2,1,0:T(8,128)} %get-tuple-element.99), channel_id=1, source_target_pairs={{0,2},{1,3},{2,0},{3,1},{4,6},{5,7},{6,4},{7,5},{8,10},{9,11},{10,... | collective-permute-start | bytes 1572872 | tf_op jit(solution)/shard_map/ppermute | solution.py:21
  232.5 24.0 %collective-permute-start.5 = (f32[4,128,256]{2,1,0:T(8,128)}, f32[4,128,256]{2,1,0:T(8,128)}, u32[]{:S(2)}, u32[]{:S(2)}) collective-permute-start(f32[4,128,256]{2,1,0:T(8,128)} %get-tuple-element.100), channel_id=1, source_target_pairs={{0,3},{1,2},{2,1},{3,0},{4,7},{5,6},{6,5},{7,4},{8,11},{9,10},{10,... | collective-permute-start | bytes 1572872 | tf_op jit(solution)/shard_map/ppermute | solution.py:21
  258.0 0.8 copy-start.1
  258.8 6.0 collective-permute-start.6
  260.4 9.7 %collective-permute-start.8 = (f32[1,128,256]{2,1,0:T(8,128)S(1)}, f32[1,128,256]{2,1,0:T(8,128)S(1)}, u32[]{:S(2)}, u32[]{:S(2)}) collective-permute-start(f32[1,128,256]{2,1,0:T(8,128)S(1)} %get-tuple-element.114), channel_id=1, source_target_pairs={{0,12},{1,13},{2,14},{3,15},{4,8},{5,9},{6,10},{7,11},{8,4},{9,5},... | collective-permute-start | bytes 393224 | tf_op jit(solution)/shard_map/ppermute | solution.py:21
  262.9 12.4 %collective-permute-start.7 = (f32[1,128,256]{2,1,0:T(8,128)S(1)}, f32[1,128,256]{2,1,0:T(8,128)S(1)}, u32[]{:S(2)}, u32[]{:S(2)}) collective-permute-start(f32[1,128,256]{2,1,0:T(8,128)S(1)} %get-tuple-element.115), channel_id=1, source_target_pairs={{0,8},{1,9},{2,10},{3,11},{4,12},{5,13},{6,14},{7,15},{8,0},{9,1},... | collective-permute-start | bytes 393224 | tf_op jit(solution)/shard_map/ppermute | solution.py:21
  286.6 179.7 %collective-permute-start.10 = (f32[8192,128]{1,0:T(8,128)}, f32[8192,128]{1,0:T(8,128)S(1)}, u32[]{:S(2)}, u32[]{:S(2)}) collective-permute-start(f32[8192,128]{1,0:T(8,128)} %get-tuple-element.62), channel_id=1, source_target_pairs={{0,16},{1,17},{2,18},{3,19},{4,20},{5,21},{6,22},{7,23},{8,24},{9,... | collective-permute-start | bytes 12582920 | tf_op jit(solution)/shard_map/ppermute | solution.py:21
  290.2 86.3 %copy-start = (f32[8192,128]{1,0:T(8,128)S(1)}, f32[8192,128]{1,0:T(8,128)}, u32[]{:S(2)}) copy-start(f32[8192,128]{1,0:T(8,128)} %get-tuple-element.70) | copy-start | bytes 12582916
  376.5 179.7 %collective-permute-start.18 = (f32[8192,128]{1,0:T(8,128)S(1)}, f32[8192,128]{1,0:T(8,128)S(1)}, u32[]{:S(2)}, u32[]{:S(2)}) collective-permute-start(f32[8192,128]{1,0:T(8,128)S(1)} %copy-done), channel_id=1, source_target_pairs={{0,16},{1,17},{2,18},{3,19},{4,20},{5,21},{6,22},{7,23},{8,24},{9,... | collective-permute-start | bytes 12582920 | tf_op jit(solution)/shard_map/ppermute | solution.py:21
  408.9 2.0 collective-permute-start.12
  409.0 14.8 %collective-permute-start.13 = (f32[4,128,256]{2,1,0:T(8,128)S(1)}, f32[4,128,256]{2,1,0:T(8,128)S(1)}, u32[]{:S(2)}, u32[]{:S(2)}) collective-permute-start(f32[4,128,256]{2,1,0:T(8,128)S(1)} %get-tuple-element.96), channel_id=1, source_target_pairs={{0,2},{1,3},{2,0},{3,1},{4,6},{5,7},{6,4},{7,5},{8,10},{9,11},{10,... | collective-permute-start | bytes 1572872 | tf_op jit(solution)/shard_map/ppermute | solution.py:21
  410.6 55.7 %copy-start.2 = (f32[4096,128]{1,0:T(8,128)S(1)}, f32[4096,128]{1,0:T(8,128)}, u32[]{:S(2)}) copy-start(f32[4096,128]{1,0:T(8,128)} %slice.49) | copy-start | bytes 6291460
  410.6 23.5 %collective-permute-start.14 = (f32[4,128,256]{2,1,0:T(8,128)S(1)}, f32[4,128,256]{2,1,0:T(8,128)S(1)}, u32[]{:S(2)}, u32[]{:S(2)}) collective-permute-start(f32[4,128,256]{2,1,0:T(8,128)S(1)} %get-tuple-element.97), channel_id=1, source_target_pairs={{0,3},{1,2},{2,1},{3,0},{4,7},{5,6},{6,5},{7,4},{8,11},{9,10},{10,... | collective-permute-start | bytes 1572872 | tf_op jit(solution)/shard_map/ppermute | solution.py:21
  434.3 6.0 collective-permute-start.15
  435.9 9.6 %collective-permute-start.17 = (f32[1,128,256]{2,1,0:T(8,128)S(1)}, f32[1,128,256]{2,1,0:T(8,128)S(1)}, u32[]{:S(2)}, u32[]{:S(2)}) collective-permute-start(f32[1,128,256]{2,1,0:T(8,128)S(1)} %get-tuple-element.111), channel_id=1, source_target_pairs={{0,12},{1,13},{2,14},{3,15},{4,8},{5,9},{6,10},{7,11},{8,4},{9,5},... | collective-permute-start | bytes 393224 | tf_op jit(solution)/shard_map/ppermute | solution.py:21
  438.4 12.5 %collective-permute-start.16 = (f32[1,128,256]{2,1,0:T(8,128)S(1)}, f32[1,128,256]{2,1,0:T(8,128)S(1)}, u32[]{:S(2)}, u32[]{:S(2)}) collective-permute-start(f32[1,128,256]{2,1,0:T(8,128)S(1)} %get-tuple-element.112), channel_id=1, source_target_pairs={{0,8},{1,9},{2,10},{3,11},{4,12},{5,13},{6,14},{7,15},{8,0},{9,1},... | collective-permute-start | bytes 393224 | tf_op jit(solution)/shard_map/ppermute | solution.py:21
  466.3 162.9 %collective-permute-start.25 = (f32[4096,128]{1,0:T(8,128)S(1)}, f32[4096,128]{1,0:T(8,128)S(1)}, u32[]{:S(2)}, u32[]{:S(2)}) collective-permute-start(f32[4096,128]{1,0:T(8,128)S(1)} %copy-done.2), channel_id=1, source_target_pairs={{0,16},{1,17},{2,18},{3,19},{4,20},{5,21},{6,22},{7,23},{8,24},{9,... | collective-permute-start | bytes 6291464 | tf_op jit(solution)/shard_map/ppermute | solution.py:21
  469.4 86.7 %copy-start.3 = (f32[4096,128]{1,0:T(8,128)S(1)}, f32[4096,128]{1,0:T(8,128)}, u32[]{:S(2)}) copy-start(f32[4096,128]{1,0:T(8,128)} %slice.50) | copy-start | bytes 6291460
  556.1 89.9 %collective-permute-start.27 = (f32[4096,128]{1,0:T(8,128)S(1)}, f32[4096,128]{1,0:T(8,128)S(1)}, u32[]{:S(2)}, u32[]{:S(2)}) collective-permute-start(f32[4096,128]{1,0:T(8,128)S(1)} %copy-done.3), channel_id=1, source_target_pairs={{0,16},{1,17},{2,18},{3,19},{4,20},{5,21},{6,22},{7,23},{8,24},{9,... | collective-permute-start | bytes 6291464 | tf_op jit(solution)/shard_map/ppermute | solution.py:21
  586.5 2.0 collective-permute-start.19
  586.5 14.8 %collective-permute-start.20 = (f32[4,128,256]{2,1,0:T(8,128)S(1)}, f32[4,128,256]{2,1,0:T(8,128)S(1)}, u32[]{:S(2)}, u32[]{:S(2)}) collective-permute-start(f32[4,128,256]{2,1,0:T(8,128)S(1)} %get-tuple-element.93), channel_id=1, source_target_pairs={{0,2},{1,3},{2,0},{3,1},{4,6},{5,7},{6,4},{7,5},{8,10},{9,11},{10,... | collective-permute-start | bytes 1572872 | tf_op jit(solution)/shard_map/ppermute | solution.py:21
  588.1 23.5 %collective-permute-start.21 = (f32[4,128,256]{2,1,0:T(8,128)S(1)}, f32[4,128,256]{2,1,0:T(8,128)S(1)}, u32[]{:S(2)}, u32[]{:S(2)}) collective-permute-start(f32[4,128,256]{2,1,0:T(8,128)S(1)} %get-tuple-element.94), channel_id=1, source_target_pairs={{0,3},{1,2},{2,1},{3,0},{4,7},{5,6},{6,5},{7,4},{8,11},{9,10},{10,... | collective-permute-start | bytes 1572872 | tf_op jit(solution)/shard_map/ppermute | solution.py:21
  611.8 6.0 collective-permute-start.22
  613.5 9.6 %collective-permute-start.24 = (f32[1,128,256]{2,1,0:T(8,128)S(1)}, f32[1,128,256]{2,1,0:T(8,128)S(1)}, u32[]{:S(2)}, u32[]{:S(2)}) collective-permute-start(f32[1,128,256]{2,1,0:T(8,128)S(1)} %get-tuple-element.108), channel_id=1, source_target_pairs={{0,12},{1,13},{2,14},{3,15},{4,8},{5,9},{6,10},{7,11},{8,4},{9,5},... | collective-permute-start | bytes 393224 | tf_op jit(solution)/shard_map/ppermute | solution.py:21
  615.9 12.5 %collective-permute-start.23 = (f32[1,128,256]{2,1,0:T(8,128)S(1)}, f32[1,128,256]{2,1,0:T(8,128)S(1)}, u32[]{:S(2)}, u32[]{:S(2)}) collective-permute-start(f32[1,128,256]{2,1,0:T(8,128)S(1)} %get-tuple-element.109), channel_id=1, source_target_pairs={{0,8},{1,9},{2,10},{3,11},{4,12},{5,13},{6,14},{7,15},{8,0},{9,1},... | collective-permute-start | bytes 393224 | tf_op jit(solution)/shard_map/ppermute | solution.py:21
  629.1 57.2 %collective-permute-start.26 = (f32[3072,128]{1,0:T(8,128)S(1)}, f32[3072,128]{1,0:T(8,128)S(1)}, u32[]{:S(2)}, u32[]{:S(2)}) collective-permute-start(f32[3072,128]{1,0:T(8,128)S(1)} %slice.51), channel_id=1, source_target_pairs={{0,16},{1,17},{2,18},{3,19},{4,20},{5,21},{6,22},{7,23},{8,24},{9,... | collective-permute-start | bytes 4718600 | tf_op jit(solution)/shard_map/ppermute | solution.py:21
  645.5 17.8 %copy-start.6 = (f32[2048,128]{1,0:T(8,128)S(1)}, f32[2048,128]{1,0:T(8,128)}, u32[]{:S(2)}) copy-start(f32[2048,128]{1,0:T(8,128)} %slice.52) | copy-start | bytes 3145732
  661.0 4.3 collective-permute-start.28
  661.1 8.8 %collective-permute-start.30 = (f32[4,128,128]{2,1,0:T(8,128)S(1)}, f32[4,128,128]{2,1,0:T(8,128)S(1)}, u32[]{:S(2)}, u32[]{:S(2)}) collective-permute-start(f32[4,128,128]{2,1,0:T(8,128)S(1)} %get-tuple-element.102), channel_id=1, source_target_pairs={{0,3},{1,2},{2,1},{3,0},{4,7},{5,6},{6,5},{7,4},{8,11},{9,10},{10,... | collective-permute-start | bytes 786440 | tf_op jit(solution)/shard_map/ppermute | solution.py:21
  663.3 12.5 %collective-permute-start.29 = (f32[4,128,128]{2,1,0:T(8,128)S(1)}, f32[4,128,128]{2,1,0:T(8,128)S(1)}, u32[]{:S(2)}, u32[]{:S(2)}) collective-permute-start(f32[4,128,128]{2,1,0:T(8,128)S(1)} %get-tuple-element.103), channel_id=1, source_target_pairs={{0,2},{1,3},{2,0},{3,1},{4,6},{5,7},{6,4},{7,5},{8,10},{9,11},{10,... | collective-permute-start | bytes 786440 | tf_op jit(solution)/shard_map/ppermute | solution.py:21
  663.3 38.9 %collective-permute-start.35 = (f32[2048,128]{1,0:T(8,128)S(1)}, f32[2048,128]{1,0:T(8,128)S(1)}, u32[]{:S(2)}, u32[]{:S(2)}) collective-permute-start(f32[2048,128]{1,0:T(8,128)S(1)} %copy-done.6), channel_id=1, source_target_pairs={{0,16},{1,17},{2,18},{3,19},{4,20},{5,21},{6,22},{7,23},{8,24},{9,... | collective-permute-start | bytes 3145736 | tf_op jit(solution)/shard_map/ppermute | solution.py:21
  675.8 4.4 collective-permute-start.31
  677.7 6.6 collective-permute-start.33
  680.1 6.2 collective-permute-start.32
  686.4 27.1 %collective-permute-start.34 = (f32[1024,128]{1,0:T(8,128)S(1)}, f32[1024,128]{1,0:T(8,128)S(1)}, u32[]{:S(2)}, u32[]{:S(2)}) collective-permute-start(f32[1024,128]{1,0:T(8,128)S(1)} %slice.53), channel_id=1, source_target_pairs={{0,16},{1,17},{2,18},{3,19},{4,20},{5,21},{6,22},{7,23},{8,24},{9,... | collective-permute-start | bytes 1572872 | tf_op jit(solution)/shard_map/ppermute | solution.py:21
  702.2 18.4 %collective-permute-start.39 = (f32[512,128]{1,0:T(8,128)S(1)}, f32[512,128]{1,0:T(8,128)S(1)}, u32[]{:S(2)}, u32[]{:S(2)}) collective-permute-start(f32[512,128]{1,0:T(8,128)S(1)} %slice.54), channel_id=1, source_target_pairs={{0,16},{1,17},{2,18},{3,19},{4,20},{5,21},{6,22},{7,23},{8,24},{9,... | collective-permute-start | bytes 786440 | tf_op jit(solution)/shard_map/ppermute | solution.py:21
  713.4 10.6 %collective-permute-start.36 = (f32[512,128]{1,0:T(8,128)S(1)}, f32[512,128]{1,0:T(8,128)S(1)}, u32[]{:S(2)}, u32[]{:S(2)}) collective-permute-start(f32[512,128]{1,0:T(8,128)S(1)} %slice.55), channel_id=1, source_target_pairs={{0,16},{1,17},{2,18},{3,19},{4,20},{5,21},{6,22},{7,23},{8,24},{9,... | collective-permute-start | bytes 786440 | tf_op jit(solution)/shard_map/ppermute | solution.py:21
  724.0 3.6 copy-start.7
  727.5 5.7 copy-start.4
  727.5 5.7 copy-start.5
  727.5 2.0 collective-permute-start.40
  727.6 5.9 collective-permute-start.37
  729.6 8.0 %collective-permute-start.41 = (f32[2,128,128]{2,1,0:T(8,128)S(1)}, f32[2,128,128]{2,1,0:T(8,128)S(1)}, u32[]{:S(2)}, u32[]{:S(2)}) collective-permute-start(f32[2,128,128]{2,1,0:T(8,128)S(1)} %get-tuple-element.104), channel_id=1, source_target_pairs={{0,2},{1,3},{2,0},{3,1},{4,6},{5,7},{6,4},{7,5},{8,10},{9,11},{10,... | collective-permute-start | bytes 393224 | tf_op jit(solution)/shard_map/ppermute | solution.py:21
  731.2 7.3 collective-permute-start.43
  732.7 6.5 collective-permute-start.42
  733.5 11.0 %collective-permute-start.38 = (f32[128,640]{1,0:T(8,128)S(1)}, f32[128,640]{1,0:T(8,128)S(1)}, u32[]{:S(2)}, u32[]{:S(2)}) collective-permute-start(f32[128,640]{1,0:T(8,128)S(1)} %pad_maximum_fusion), channel_id=1, source_target_pairs={{0,16},{1,17},{2,18},{3,19},{4,20},{5,21},{6,22},{7,23},{8,24},{9,... | collective-permute-start | bytes 983048 | tf_op jit(solution)/shard_map/ppermute | solution.py:21
  739.3 5.2 collective-permute-start.44
  744.6 4.3 collective-permute-start.45

commit v6 on v5

--- a/solution.py
+++ b/solution.py
@@ -190,8 +190,9 @@
             if later not in blocks:
                 blocks[later] = block(later, done)
                 partner = after(partner, blocks[later])
-        if index + ahead < len(pieces):
-            arrived.append(swapped(after(blocks[index + ahead], arrived[index], done), pair))
+        ready = index + ahead + (index + ahead >= len(pieces) - 4)
+        while len(arrived) < min(ready + 1, len(pieces)):
+            arrived.append(swapped(after(blocks[len(arrived)], arrived[index], done), pair))
         operands = (control, high, low, own, partner, pieces[index], totals.get(chunk))
         if index + 1 == len(pieces):
             kept, given = product(*operands, owned=matrix.shape[0] // pair)

time: 750 us -> 750 us (level)
  transfers between devices with their start and end apart: 46 -> 46, of which waited for: 36 -> 39; matrix products, arithmetic and copies ran while one was open for 5% -> 5% of each run, Pallas kernels for 37% -> 37%
where the time goes in v6:
time: 750 us
  waiting for transfers between devices  369 us (49%)
  Pallas kernels  279 us (37%)
  starting transfers between devices  59.6 us (8%)
  local copies, waits for them, and re-layouts  33.7 us (4%)
    ppermute x46, waiting for transfers between devices, swapped(): lax.ppermute(value, AXES, [(source, source ^ mask) for source in range(de...  369 us
    pallas_call x14, Pallas kernels, product(): pl.pallas_call(functools.partial(product_kernel, total is not None, owned...  234 us
    ppermute x46, starting transfers between devices, swapped(): lax.ppermute(value, AXES, [(source, source ^ mask) for source in range(de...  59.6 us
    pallas_call x1, Pallas kernels, split_matrix(): pl.pallas_call(split_kernel, grid=(rows // step,), in_specs=[spec], out_s...  44.9 us
    slice x10, local copies, waits for them, and re-layouts, block(): return source[start:start + size, chunk * LANES:(chunk + 1) * LANES]  32.7 us
  transfers between devices with their start and end apart: 46, of which 39 were waited for; matrix products, arithmetic and copies ran while one was open for 5% of the time, Pallas kernels for 37%

profile of v6, /device:TPU:0, one launch (start us, length us, event | category | flops | bytes accessed | tf_op | source)
XLA Modules:
  0.0 749.6 jit_solution(2626018622576932169)
XLA Ops:
  1.1 3.0 collective-permute-start.1
  4.1 4.5 slice.43
  8.6 44.9 %split_matrix.1 = (bf16[2048,8192]{1,0:T(8,128)(2,1)}, bf16[2048,8192]{1,0:T(8,128)(2,1)}) custom-call(f32[2048,8192]{1,0:T(8,128)} %bitcast.2.matrix_ref), custom_call_target="tpu_custom_call" | custom-call | bytes 134217728 | tf_op jit(solution)/shard_map/split_matrix/pallas_call | solution.py:65
  53.4 15.2 %fusion.37 = (f32[8192,128]{1,0:T(8,128)}, f32[8192,128]{1,0:T(8,128)}, f32[8192,128]{1,0:T(8,128)}, f32[8192,128]{1,0:T(8,128)}, f32[8192,128]{1,0:T(8,128)}) fusion(f32[8192,1024]{1,0:T(8,128)} %bitcast.106), kind=kLoop, calls=%fused_computation.93 | loop fusion | bytes 41943040 | tf_op jit(solution)/shard_map/slice | solution.py:177
  68.7 2.1 collective-permute-start.2
  70.8 5.1 product.14.refs_0_
  75.9 30.9 %collective-permute-done.partner_ref = f32[8192,128]{1,0:T(8,128)} collective-permute-done((f32[8192,128]{1,0:T(8,128)}, f32[8192,128]{1,0:T(8,128)}, u32[]{:S(2)}, u32[]{:S(2)}) %collective-permute-start) | collective-permute-done | bytes 4194336 | tf_op jit(solution)/shard_map/ppermute | solution.py:21
  106.8 2.1 collective-permute-start.9
  108.9 3.0 slice.49
  111.9 27.9 %product.15 = f32[2048,128]{1,0:T(8,128)S(1)} custom-call(f32[2]{0:T(128)S(1)} %pad_maximum_fusion.1.control_ref, bf16[2048,8192]{1,0:T(8,128)(2,1)} %get-tuple-element.48.high_ref, bf16[2048,8192]{1,0:T(8,128)(2,1)} %get-tuple-element.49.low_ref, f32[8192,1024]{1,0:T(8,128)} %bitcast.109, f32[8192,128]{1,0:T(8,128)} %collective-permute-done.partner_ref), custom_call_target="tpu_custom_call" | custom-call | tf_op jit(solution)/shard_map/product/pallas_call | solution.py:134
  139.9 56.8 %collective-permute-done.2.partner_ref = f32[8192,128]{1,0:T(8,128)} collective-permute-done((f32[8192,128]{1,0:T(8,128)}, f32[8192,128]{1,0:T(8,128)}, u32[]{:S(2)}, u32[]{:S(2)}) %collective-permute-start.2) | collective-permute-done | bytes 4194336 | tf_op jit(solution)/shard_map/ppermute | solution.py:21
  196.7 2.1 collective-permute-start.11
  198.8 3.0 slice.50
  201.8 27.9 %product.16 = f32[2048,128]{1,0:T(8,128)S(1)} custom-call(f32[2]{0:T(128)S(1)} %pad_maximum_fusion.1.control_ref, bf16[2048,8192]{1,0:T(8,128)(2,1)} %get-tuple-element.48.high_ref, bf16[2048,8192]{1,0:T(8,128)(2,1)} %get-tuple-element.49.low_ref, f32[8192,1024]{1,0:T(8,128)} %bitcast.111, f32[8192,128]{1,0:T(8,128)} %collective-permute-done.2.partner_ref), custom_call_target="tpu_custom_call" | custom-call | tf_op jit(solution)/shard_map/product/pallas_call | solution.py:134
  233.2 12.8 %collective-permute-done.4 = f32[4,128,256]{2,1,0:T(8,128)} collective-permute-done((f32[4,128,256]{2,1,0:T(8,128)}, f32[4,128,256]{2,1,0:T(8,128)}, u32[]{:S(2)}, u32[]{:S(2)}) %collective-permute-start.4) | collective-permute-done | bytes 524320 | tf_op jit(solution)/shard_map/ppermute | solution.py:21
  246.0 10.5 %collective-permute-done.5 = f32[4,128,256]{2,1,0:T(8,128)} collective-permute-done((f32[4,128,256]{2,1,0:T(8,128)}, f32[4,128,256]{2,1,0:T(8,128)}, u32[]{:S(2)}, u32[]{:S(2)}) %collective-permute-start.5) | collective-permute-done | bytes 524320 | tf_op jit(solution)/shard_map/ppermute | solution.py:21
  260.4 2.5 collective-permute-start.8
  264.7 5.3 collective-permute-done.8
  270.1 5.2 collective-permute-done.7
  276.9 9.7 %collective-permute-done.9.partner_ref = f32[8192,128]{1,0:T(8,128)} collective-permute-done((f32[8192,128]{1,0:T(8,128)}, f32[8192,128]{1,0:T(8,128)}, u32[]{:S(2)}, u32[]{:S(2)}) %collective-permute-start.9) | collective-permute-done | bytes 4194336 | tf_op jit(solution)/shard_map/ppermute | solution.py:21
  286.6 2.1 collective-permute-start.10
  290.2 28.2 %product.17 = f32[2048,128]{1,0:T(8,128)S(1)} custom-call(f32[2]{0:T(128)S(1)} %pad_maximum_fusion.1.control_ref, bf16[2048,8192]{1,0:T(8,128)(2,1)} %get-tuple-element.48.high_ref, bf16[2048,8192]{1,0:T(8,128)(2,1)} %get-tuple-element.49.low_ref, f32[8192,1024]{1,0:T(8,128)} %bitcast.113, f32[8192,128]{1,0:T(8,128)} %collective-permute-done.9.partner_ref), custom_call_target="tpu_custom_call" | custom-call | tf_op jit(solution)/shard_map/product/pallas_call | solution.py:134
  318.4 58.1 %collective-permute-done.11.partner_ref = f32[8192,128]{1,0:T(8,128)} collective-permute-done((f32[8192,128]{1,0:T(8,128)}, f32[8192,128]{1,0:T(8,128)}, u32[]{:S(2)}, u32[]{:S(2)}) %collective-permute-start.11) | collective-permute-done | bytes 4194336 | tf_op jit(solution)/shard_map/ppermute | solution.py:21
  376.5 2.1 collective-permute-start.18
  379.8 28.1 %product.18 = f32[2048,128]{1,0:T(8,128)S(1)} custom-call(f32[2]{0:T(128)S(1)} %pad_maximum_fusion.1.control_ref, bf16[2048,8192]{1,0:T(8,128)(2,1)} %get-tuple-element.48.high_ref, bf16[2048,8192]{1,0:T(8,128)(2,1)} %get-tuple-element.49.low_ref, f32[8192,1024]{1,0:T(8,128)} %bitcast.115, f32[8192,128]{1,0:T(8,128)} %collective-permute-done.11.partner_ref), custom_call_target="tpu_custom_call" | custom-call | tf_op jit(solution)/shard_map/product/pallas_call | solution.py:134
  410.1 12.9 %collective-permute-done.13 = f32[4,128,256]{2,1,0:T(8,128)S(1)} collective-permute-done((f32[4,128,256]{2,1,0:T(8,128)S(1)}, f32[4,128,256]{2,1,0:T(8,128)S(1)}, u32[]{:S(2)}, u32[]{:S(2)}) %collective-permute-start.13) | collective-permute-done | bytes 524320 | tf_op jit(solution)/shard_map/ppermute | solution.py:21
  423.0 10.3 %collective-permute-done.14 = f32[4,128,256]{2,1,0:T(8,128)S(1)} collective-permute-done((f32[4,128,256]{2,1,0:T(8,128)S(1)}, f32[4,128,256]{2,1,0:T(8,128)S(1)}, u32[]{:S(2)}, u32[]{:S(2)}) %collective-permute-start.14) | collective-permute-done | bytes 524320 | tf_op jit(solution)/shard_map/ppermute | solution.py:21
  435.1 2.5 collective-permute-start.17
  437.7 1.8 collective-permute-done.15
  439.5 5.2 collective-permute-done.17
  444.8 5.3 collective-permute-done.16
  450.8 15.5 %collective-permute-done.10.partner_ref = f32[8192,128]{1,0:T(8,128)S(1)} collective-permute-done((f32[8192,128]{1,0:T(8,128)}, f32[8192,128]{1,0:T(8,128)S(1)}, u32[]{:S(2)}, u32[]{:S(2)}) %collective-permute-start.10) | collective-permute-done | bytes 4194336 | tf_op jit(solution)/shard_map/ppermute | solution.py:21
  466.3 2.1 collective-permute-start.26
  469.4 27.3 %product.19 = f32[2048,128]{1,0:T(8,128)S(1)} custom-call(f32[2]{0:T(128)S(1)} %pad_maximum_fusion.1.control_ref, bf16[2048,8192]{1,0:T(8,128)(2,1)} %get-tuple-element.48.high_ref, bf16[2048,8192]{1,0:T(8,128)(2,1)} %get-tuple-element.49.low_ref, f32[8192,1024]{1,0:T(8,128)} %bitcast.117, f32[8192,128]{1,0:T(8,128)S(1)} %collective-permute-done.10.partner_ref), custom_call_target="tpu_custom_call" | custom-call | tf_op jit(solution)/shard_map/product/pallas_call | solution.py:134
  496.7 59.4 %collective-permute-done.18.partner_ref = f32[8192,128]{1,0:T(8,128)S(1)} collective-permute-done((f32[8192,128]{1,0:T(8,128)S(1)}, f32[8192,128]{1,0:T(8,128)S(1)}, u32[]{:S(2)}, u32[]{:S(2)}) %collective-permute-start.18) | collective-permute-done | bytes 4194336 | tf_op jit(solution)/shard_map/ppermute | solution.py:21
  556.1 2.1 collective-permute-start.25
  559.2 27.2 %product.20 = f32[2048,128]{1,0:T(8,128)S(1)} custom-call(f32[2]{0:T(128)S(1)} %pad_maximum_fusion.1.control_ref, bf16[2048,8192]{1,0:T(8,128)(2,1)} %get-tuple-element.48.high_ref, bf16[2048,8192]{1,0:T(8,128)(2,1)} %get-tuple-element.49.low_ref, f32[8192,1024]{1,0:T(8,128)} %bitcast.119, f32[8192,128]{1,0:T(8,128)S(1)} %collective-permute-done.18.partner_ref), custom_call_target="tpu_custom_call" | custom-call | tf_op jit(solution)/shard_map/product/pallas_call | solution.py:134
  588.4 12.9 %collective-permute-done.20 = f32[4,128,256]{2,1,0:T(8,128)S(1)} collective-permute-done((f32[4,128,256]{2,1,0:T(8,128)S(1)}, f32[4,128,256]{2,1,0:T(8,128)S(1)}, u32[]{:S(2)}, u32[]{:S(2)}) %collective-permute-start.20) | collective-permute-done | bytes 524320 | tf_op jit(solution)/shard_map/ppermute | solution.py:21
  601.3 10.3 %collective-permute-done.21 = f32[4,128,256]{2,1,0:T(8,128)S(1)} collective-permute-done((f32[4,128,256]{2,1,0:T(8,128)S(1)}, f32[4,128,256]{2,1,0:T(8,128)S(1)}, u32[]{:S(2)}, u32[]{:S(2)}) %collective-permute-start.21) | collective-permute-done | bytes 524320 | tf_op jit(solution)/shard_map/ppermute | solution.py:21
  613.5 2.5 collective-permute-start.24
  616.1 1.8 collective-permute-done.22
  617.9 5.2 collective-permute-done.24
  623.1 5.3 collective-permute-done.23
  630.6 14.9 %product.21.refs_0_ = f32[2048,128]{1,0:T(8,128)S(1)} custom-call(f32[2]{0:T(128)S(1)} %pad_maximum_fusion.1.control_ref, bf16[2048,8192]{1,0:T(8,128)(2,1)} %get-tuple-element.48.high_ref, bf16[2048,8192]{1,0:T(8,128)(2,1)} %get-tuple-element.49.low_ref, f32[8192,1024]{1,0:T(8,128)} %bitcast.121, f32[4096,128]{1,0:T(8,128)S(1)} %collective-permute-done.26.partner_ref), custom_call_target="tpu_custom_call" | custom-call | tf_op jit(solution)/shard_map/product/pallas_call | solution.py:134
  646.0 2.1 collective-permute-start.27
  648.1 14.9 %product.23 = f32[2048,128]{1,0:T(8,128)S(1)} custom-call(f32[2]{0:T(128)S(1)} %pad_maximum_fusion.1.control_ref, bf16[2048,8192]{1,0:T(8,128)(2,1)} %get-tuple-element.48.high_ref, bf16[2048,8192]{1,0:T(8,128)(2,1)} %get-tuple-element.49.low_ref, f32[8192,1024]{1,0:T(8,128)} %bitcast.122, f32[4096,128]{1,0:T(8,128)S(1)} %collective-permute-done.25.partner_ref, ...), custom_call_target="tpu_custom_call" | custom-call | tf_op jit(solution)/shard_map/product/pallas_call | solution.py:134
  665.3 6.1 collective-permute-done.33
  671.4 6.0 collective-permute-done.32
  679.1 2.5 collective-permute-start.36
  682.3 3.4 collective-permute-done.36
  685.7 2.1 collective-permute-done.35
  688.5 12.1 %product.22.refs_0_ = f32[2048,128]{1,0:T(8,128)S(1)} custom-call(f32[2]{0:T(128)S(1)} %pad_maximum_fusion.1.control_ref, bf16[2048,8192]{1,0:T(8,128)(2,1)} %get-tuple-element.48.high_ref, bf16[2048,8192]{1,0:T(8,128)(2,1)} %get-tuple-element.49.low_ref, f32[8192,1024]{1,0:T(8,128)} %bitcast.123, f32[3072,128]{1,0:T(8,128)S(1)} %collective-permute-done.28.partner_ref, ...), custom_call_target="tpu_custom_call" | custom-call | tf_op jit(solution)/shard_map/product/pallas_call | solution.py:134
  702.2 2.1 collective-permute-start.29
  704.3 8.7 %product.24.refs_0_ = f32[2048,128]{1,0:T(8,128)S(1)} custom-call(f32[2]{0:T(128)S(1)} %pad_maximum_fusion.1.control_ref, bf16[2048,8192]{1,0:T(8,128)(2,1)} %get-tuple-element.48.high_ref, bf16[2048,8192]{1,0:T(8,128)(2,1)} %get-tuple-element.49.low_ref, f32[8192,1024]{1,0:T(8,128)} %bitcast.124, f32[2048,128]{1,0:T(8,128)S(1)} %collective-permute-done.27.partner_ref, ...), custom_call_target="tpu_custom_call" | custom-call | tf_op jit(solution)/shard_map/product/pallas_call | solution.py:134
  713.4 5.1 product.25.refs_0_
  719.0 3.4 product.26.refs_0_
  723.8 3.4 product.27
  727.4 1.8 collective-permute-start.30
  729.4 1.8 collective-permute-start.41
  733.3 1.7 collective-permute-start.37
  735.0 2.1 collective-permute-done.41
  739.2 2.8 collective-permute-start.44
  742.0 2.4 collective-permute-done.44
  746.2 2.6 collective-permute-done.45
  (94 shorter events, 44.5 us)
Async XLA Ops:
  1.1 67.6 %collective-permute-start.1 = (f32[1024,128]{1,0:T(8,128)S(1)}, f32[1024,128]{1,0:T(8,128)S(1)}, u32[]{:S(2)}, u32[]{:S(2)}) collective-permute-start(f32[1024,128]{1,0:T(8,128)S(1)} %slice.56), channel_id=1, source_target_pairs={{0,16},{1,17},{2,18},{3,19},{4,20},{5,21},{6,22},{7,23},{8,24},{9,... | collective-permute-start | bytes 1572872 | tf_op jit(solution)/shard_map/ppermute | solution.py:21
  8.6 98.2 %collective-permute-start = (f32[8192,128]{1,0:T(8,128)}, f32[8192,128]{1,0:T(8,128)}, u32[]{:S(2)}, u32[]{:S(2)}) collective-permute-start(f32[8192,128]{1,0:T(8,128)} %slice.43), channel_id=1, source_target_pairs={{0,16},{1,17},{2,18},{3,19},{4,20},{5,21},{6,22},{7,23},{8,24},{9,... | collective-permute-start | bytes 12582920 | tf_op jit(solution)/shard_map/ppermute | solution.py:21
  68.7 128.0 %collective-permute-start.2 = (f32[8192,128]{1,0:T(8,128)}, f32[8192,128]{1,0:T(8,128)}, u32[]{:S(2)}, u32[]{:S(2)}) collective-permute-start(f32[8192,128]{1,0:T(8,128)} %get-tuple-element.58), channel_id=1, source_target_pairs={{0,16},{1,17},{2,18},{3,19},{4,20},{5,21},{6,22},{7,23},{8,24},{9,... | collective-permute-start | bytes 12582920 | tf_op jit(solution)/shard_map/ppermute | solution.py:21
  106.8 179.8 %collective-permute-start.9 = (f32[8192,128]{1,0:T(8,128)}, f32[8192,128]{1,0:T(8,128)}, u32[]{:S(2)}, u32[]{:S(2)}) collective-permute-start(f32[8192,128]{1,0:T(8,128)} %get-tuple-element.61), channel_id=1, source_target_pairs={{0,16},{1,17},{2,18},{3,19},{4,20},{5,21},{6,22},{7,23},{8,24},{9,... | collective-permute-start | bytes 12582920 | tf_op jit(solution)/shard_map/ppermute | solution.py:21
  196.7 179.8 %collective-permute-start.11 = (f32[8192,128]{1,0:T(8,128)}, f32[8192,128]{1,0:T(8,128)}, u32[]{:S(2)}, u32[]{:S(2)}) collective-permute-start(f32[8192,128]{1,0:T(8,128)} %get-tuple-element.65), channel_id=1, source_target_pairs={{0,16},{1,17},{2,18},{3,19},{4,20},{5,21},{6,22},{7,23},{8,24},{9,... | collective-permute-start | bytes 12582920 | tf_op jit(solution)/shard_map/ppermute | solution.py:21
  230.9 2.3 collective-permute-start.3
  230.9 15.0 %collective-permute-start.4 = (f32[4,128,256]{2,1,0:T(8,128)}, f32[4,128,256]{2,1,0:T(8,128)}, u32[]{:S(2)}, u32[]{:S(2)}) collective-permute-start(f32[4,128,256]{2,1,0:T(8,128)} %get-tuple-element.99), channel_id=1, source_target_pairs={{0,2},{1,3},{2,0},{3,1},{4,6},{5,7},{6,4},{7,5},{8,10},{9,11},{10,... | collective-permute-start | bytes 1572872 | tf_op jit(solution)/shard_map/ppermute | solution.py:21
  232.5 24.0 %collective-permute-start.5 = (f32[4,128,256]{2,1,0:T(8,128)}, f32[4,128,256]{2,1,0:T(8,128)}, u32[]{:S(2)}, u32[]{:S(2)}) collective-permute-start(f32[4,128,256]{2,1,0:T(8,128)} %get-tuple-element.100), channel_id=1, source_target_pairs={{0,3},{1,2},{2,1},{3,0},{4,7},{5,6},{6,5},{7,4},{8,11},{9,10},{10,... | collective-permute-start | bytes 1572872 | tf_op jit(solution)/shard_map/ppermute | solution.py:21
  257.9 0.8 copy-start.1
  258.8 6.0 collective-permute-start.6
  260.4 9.7 %collective-permute-start.8 = (f32[1,128,256]{2,1,0:T(8,128)S(1)}, f32[1,128,256]{2,1,0:T(8,128)S(1)}, u32[]{:S(2)}, u32[]{:S(2)}) collective-permute-start(f32[1,128,256]{2,1,0:T(8,128)S(1)} %get-tuple-element.114), channel_id=1, source_target_pairs={{0,12},{1,13},{2,14},{3,15},{4,8},{5,9},{6,10},{7,11},{8,4},{9,5},... | collective-permute-start | bytes 393224 | tf_op jit(solution)/shard_map/ppermute | solution.py:21
  262.9 12.4 %collective-permute-start.7 = (f32[1,128,256]{2,1,0:T(8,128)S(1)}, f32[1,128,256]{2,1,0:T(8,128)S(1)}, u32[]{:S(2)}, u32[]{:S(2)}) collective-permute-start(f32[1,128,256]{2,1,0:T(8,128)S(1)} %get-tuple-element.115), channel_id=1, source_target_pairs={{0,8},{1,9},{2,10},{3,11},{4,12},{5,13},{6,14},{7,15},{8,0},{9,1},... | collective-permute-start | bytes 393224 | tf_op jit(solution)/shard_map/ppermute | solution.py:21
  286.6 179.7 %collective-permute-start.10 = (f32[8192,128]{1,0:T(8,128)}, f32[8192,128]{1,0:T(8,128)S(1)}, u32[]{:S(2)}, u32[]{:S(2)}) collective-permute-start(f32[8192,128]{1,0:T(8,128)} %get-tuple-element.62), channel_id=1, source_target_pairs={{0,16},{1,17},{2,18},{3,19},{4,20},{5,21},{6,22},{7,23},{8,24},{9,... | collective-permute-start | bytes 12582920 | tf_op jit(solution)/shard_map/ppermute | solution.py:21
  290.2 86.3 %copy-start = (f32[8192,128]{1,0:T(8,128)S(1)}, f32[8192,128]{1,0:T(8,128)}, u32[]{:S(2)}) copy-start(f32[8192,128]{1,0:T(8,128)} %get-tuple-element.70) | copy-start | bytes 12582916
  376.5 179.7 %collective-permute-start.18 = (f32[8192,128]{1,0:T(8,128)S(1)}, f32[8192,128]{1,0:T(8,128)S(1)}, u32[]{:S(2)}, u32[]{:S(2)}) collective-permute-start(f32[8192,128]{1,0:T(8,128)S(1)} %copy-done), channel_id=1, source_target_pairs={{0,16},{1,17},{2,18},{3,19},{4,20},{5,21},{6,22},{7,23},{8,24},{9,... | collective-permute-start | bytes 12582920 | tf_op jit(solution)/shard_map/ppermute | solution.py:21
  408.1 2.0 collective-permute-start.12
  408.2 14.8 %collective-permute-start.13 = (f32[4,128,256]{2,1,0:T(8,128)S(1)}, f32[4,128,256]{2,1,0:T(8,128)S(1)}, u32[]{:S(2)}, u32[]{:S(2)}) collective-permute-start(f32[4,128,256]{2,1,0:T(8,128)S(1)} %get-tuple-element.96), channel_id=1, source_target_pairs={{0,2},{1,3},{2,0},{3,1},{4,6},{5,7},{6,4},{7,5},{8,10},{9,11},{10,... | collective-permute-start | bytes 1572872 | tf_op jit(solution)/shard_map/ppermute | solution.py:21
  409.8 56.5 %copy-start.2 = (f32[4096,128]{1,0:T(8,128)S(1)}, f32[4096,128]{1,0:T(8,128)}, u32[]{:S(2)}) copy-start(f32[4096,128]{1,0:T(8,128)} %slice.49) | copy-start | bytes 6291460
  409.8 23.5 %collective-permute-start.14 = (f32[4,128,256]{2,1,0:T(8,128)S(1)}, f32[4,128,256]{2,1,0:T(8,128)S(1)}, u32[]{:S(2)}, u32[]{:S(2)}) collective-permute-start(f32[4,128,256]{2,1,0:T(8,128)S(1)} %get-tuple-element.97), channel_id=1, source_target_pairs={{0,3},{1,2},{2,1},{3,0},{4,7},{5,6},{6,5},{7,4},{8,11},{9,10},{10,... | collective-permute-start | bytes 1572872 | tf_op jit(solution)/shard_map/ppermute | solution.py:21
  433.5 6.0 collective-permute-start.15
  435.1 9.6 %collective-permute-start.17 = (f32[1,128,256]{2,1,0:T(8,128)S(1)}, f32[1,128,256]{2,1,0:T(8,128)S(1)}, u32[]{:S(2)}, u32[]{:S(2)}) collective-permute-start(f32[1,128,256]{2,1,0:T(8,128)S(1)} %get-tuple-element.111), channel_id=1, source_target_pairs={{0,12},{1,13},{2,14},{3,15},{4,8},{5,9},{6,10},{7,11},{8,4},{9,5},... | collective-permute-start | bytes 393224 | tf_op jit(solution)/shard_map/ppermute | solution.py:21
  437.6 12.5 %collective-permute-start.16 = (f32[1,128,256]{2,1,0:T(8,128)S(1)}, f32[1,128,256]{2,1,0:T(8,128)S(1)}, u32[]{:S(2)}, u32[]{:S(2)}) collective-permute-start(f32[1,128,256]{2,1,0:T(8,128)S(1)} %get-tuple-element.112), channel_id=1, source_target_pairs={{0,8},{1,9},{2,10},{3,11},{4,12},{5,13},{6,14},{7,15},{8,0},{9,1},... | collective-permute-start | bytes 393224 | tf_op jit(solution)/shard_map/ppermute | solution.py:21
  466.3 162.9 %collective-permute-start.26 = (f32[4096,128]{1,0:T(8,128)S(1)}, f32[4096,128]{1,0:T(8,128)S(1)}, u32[]{:S(2)}, u32[]{:S(2)}) collective-permute-start(f32[4096,128]{1,0:T(8,128)S(1)} %copy-done.2), channel_id=1, source_target_pairs={{0,16},{1,17},{2,18},{3,19},{4,20},{5,21},{6,22},{7,23},{8,24},{9,... | collective-permute-start | bytes 6291464 | tf_op jit(solution)/shard_map/ppermute | solution.py:21
  469.4 86.7 %copy-start.3 = (f32[4096,128]{1,0:T(8,128)S(1)}, f32[4096,128]{1,0:T(8,128)}, u32[]{:S(2)}) copy-start(f32[4096,128]{1,0:T(8,128)} %slice.50) | copy-start | bytes 6291460
  556.1 89.9 %collective-permute-start.25 = (f32[4096,128]{1,0:T(8,128)S(1)}, f32[4096,128]{1,0:T(8,128)S(1)}, u32[]{:S(2)}, u32[]{:S(2)}) collective-permute-start(f32[4096,128]{1,0:T(8,128)S(1)} %copy-done.3), channel_id=1, source_target_pairs={{0,16},{1,17},{2,18},{3,19},{4,20},{5,21},{6,22},{7,23},{8,24},{9,... | collective-permute-start | bytes 6291464 | tf_op jit(solution)/shard_map/ppermute | solution.py:21
  586.5 2.0 collective-permute-start.19
  586.5 14.8 %collective-permute-start.20 = (f32[4,128,256]{2,1,0:T(8,128)S(1)}, f32[4,128,256]{2,1,0:T(8,128)S(1)}, u32[]{:S(2)}, u32[]{:S(2)}) collective-permute-start(f32[4,128,256]{2,1,0:T(8,128)S(1)} %get-tuple-element.93), channel_id=1, source_target_pairs={{0,2},{1,3},{2,0},{3,1},{4,6},{5,7},{6,4},{7,5},{8,10},{9,11},{10,... | collective-permute-start | bytes 1572872 | tf_op jit(solution)/shard_map/ppermute | solution.py:21
  588.1 23.5 %collective-permute-start.21 = (f32[4,128,256]{2,1,0:T(8,128)S(1)}, f32[4,128,256]{2,1,0:T(8,128)S(1)}, u32[]{:S(2)}, u32[]{:S(2)}) collective-permute-start(f32[4,128,256]{2,1,0:T(8,128)S(1)} %get-tuple-element.94), channel_id=1, source_target_pairs={{0,3},{1,2},{2,1},{3,0},{4,7},{5,6},{6,5},{7,4},{8,11},{9,10},{10,... | collective-permute-start | bytes 1572872 | tf_op jit(solution)/shard_map/ppermute | solution.py:21
  611.8 6.0 collective-permute-start.22
  613.5 9.6 %collective-permute-start.24 = (f32[1,128,256]{2,1,0:T(8,128)S(1)}, f32[1,128,256]{2,1,0:T(8,128)S(1)}, u32[]{:S(2)}, u32[]{:S(2)}) collective-permute-start(f32[1,128,256]{2,1,0:T(8,128)S(1)} %get-tuple-element.108), channel_id=1, source_target_pairs={{0,12},{1,13},{2,14},{3,15},{4,8},{5,9},{6,10},{7,11},{8,4},{9,5},... | collective-permute-start | bytes 393224 | tf_op jit(solution)/shard_map/ppermute | solution.py:21
  615.9 12.5 %collective-permute-start.23 = (f32[1,128,256]{2,1,0:T(8,128)S(1)}, f32[1,128,256]{2,1,0:T(8,128)S(1)}, u32[]{:S(2)}, u32[]{:S(2)}) collective-permute-start(f32[1,128,256]{2,1,0:T(8,128)S(1)} %get-tuple-element.109), channel_id=1, source_target_pairs={{0,8},{1,9},{2,10},{3,11},{4,12},{5,13},{6,14},{7,15},{8,0},{9,1},... | collective-permute-start | bytes 393224 | tf_op jit(solution)/shard_map/ppermute | solution.py:21
  629.1 58.7 %collective-permute-start.28 = (f32[3072,128]{1,0:T(8,128)S(1)}, f32[3072,128]{1,0:T(8,128)S(1)}, u32[]{:S(2)}, u32[]{:S(2)}) collective-permute-start(f32[3072,128]{1,0:T(8,128)S(1)} %slice.51), channel_id=1, source_target_pairs={{0,16},{1,17},{2,18},{3,19},{4,20},{5,21},{6,22},{7,23},{8,24},{9,... | collective-permute-start | bytes 4718600 | tf_op jit(solution)/shard_map/ppermute | solution.py:21
  646.0 56.2 %collective-permute-start.27 = (f32[2048,128]{1,0:T(8,128)S(1)}, f32[2048,128]{1,0:T(8,128)S(1)}, u32[]{:S(2)}, u32[]{:S(2)}) collective-permute-start(f32[2048,128]{1,0:T(8,128)S(1)} %slice.52), channel_id=1, source_target_pairs={{0,16},{1,17},{2,18},{3,19},{4,20},{5,21},{6,22},{7,23},{8,24},{9,... | collective-permute-start | bytes 3145736 | tf_op jit(solution)/shard_map/ppermute | solution.py:21
  663.0 2.2 collective-permute-start.31
  663.1 8.3 %collective-permute-start.33 = (f32[4,128,128]{2,1,0:T(8,128)S(1)}, f32[4,128,128]{2,1,0:T(8,128)S(1)}, u32[]{:S(2)}, u32[]{:S(2)}) collective-permute-start(f32[4,128,128]{2,1,0:T(8,128)S(1)} %get-tuple-element.102), channel_id=1, source_target_pairs={{0,3},{1,2},{2,1},{3,0},{4,7},{5,6},{6,5},{7,4},{8,11},{9,10},{10,... | collective-permute-start | bytes 786440 | tf_op jit(solution)/shard_map/ppermute | solution.py:21
  664.8 12.7 %collective-permute-start.32 = (f32[4,128,128]{2,1,0:T(8,128)S(1)}, f32[4,128,128]{2,1,0:T(8,128)S(1)}, u32[]{:S(2)}, u32[]{:S(2)}) collective-permute-start(f32[4,128,128]{2,1,0:T(8,128)S(1)} %get-tuple-element.103), channel_id=1, source_target_pairs={{0,2},{1,3},{2,0},{3,1},{4,6},{5,7},{6,4},{7,5},{8,10},{9,11},{10,... | collective-permute-start | bytes 786440 | tf_op jit(solution)/shard_map/ppermute | solution.py:21
  677.5 4.3 collective-permute-start.34
  679.1 6.6 collective-permute-start.36
  681.6 6.2 collective-permute-start.35
  681.8 31.6 %collective-permute-start.39 = (f32[1024,128]{1,0:T(8,128)S(1)}, f32[1024,128]{1,0:T(8,128)S(1)}, u32[]{:S(2)}, u32[]{:S(2)}) collective-permute-start(f32[1024,128]{1,0:T(8,128)S(1)} %slice.53), channel_id=1, source_target_pairs={{0,16},{1,17},{2,18},{3,19},{4,20},{5,21},{6,22},{7,23},{8,24},{9,... | collective-permute-start | bytes 1572872 | tf_op jit(solution)/shard_map/ppermute | solution.py:21
  687.9 31.2 %collective-permute-start.38 = (f32[512,128]{1,0:T(8,128)S(1)}, f32[512,128]{1,0:T(8,128)S(1)}, u32[]{:S(2)}, u32[]{:S(2)}) collective-permute-start(f32[512,128]{1,0:T(8,128)S(1)} %slice.54), channel_id=1, source_target_pairs={{0,16},{1,17},{2,18},{3,19},{4,20},{5,21},{6,22},{7,23},{8,24},{9,... | collective-permute-start | bytes 786440 | tf_op jit(solution)/shard_map/ppermute | solution.py:21
  702.2 21.6 %collective-permute-start.29 = (f32[512,128]{1,0:T(8,128)S(1)}, f32[512,128]{1,0:T(8,128)S(1)}, u32[]{:S(2)}, u32[]{:S(2)}) collective-permute-start(f32[512,128]{1,0:T(8,128)S(1)} %slice.55), channel_id=1, source_target_pairs={{0,16},{1,17},{2,18},{3,19},{4,20},{5,21},{6,22},{7,23},{8,24},{9,... | collective-permute-start | bytes 786440 | tf_op jit(solution)/shard_map/ppermute | solution.py:21
  722.4 4.9 copy-start.6
  727.2 5.7 copy-start.4
  727.2 5.7 copy-start.5
  727.3 2.0 collective-permute-start.40
  727.4 5.9 collective-permute-start.30
  729.4 7.8 %collective-permute-start.41 = (f32[2,128,128]{2,1,0:T(8,128)S(1)}, f32[2,128,128]{2,1,0:T(8,128)S(1)}, u32[]{:S(2)}, u32[]{:S(2)}) collective-permute-start(f32[2,128,128]{2,1,0:T(8,128)S(1)} %get-tuple-element.104), channel_id=1, source_target_pairs={{0,2},{1,3},{2,0},{3,1},{4,6},{5,7},{6,4},{7,5},{8,10},{9,11},{10,... | collective-permute-start | bytes 393224 | tf_op jit(solution)/shard_map/ppermute | solution.py:21
  731.2 7.3 collective-permute-start.43
  732.7 6.4 collective-permute-start.42
  733.3 11.2 %collective-permute-start.37 = (f32[128,640]{1,0:T(8,128)S(1)}, f32[128,640]{1,0:T(8,128)S(1)}, u32[]{:S(2)}, u32[]{:S(2)}) collective-permute-start(f32[128,640]{1,0:T(8,128)S(1)} %pad_maximum_fusion), channel_id=1, source_target_pairs={{0,16},{1,17},{2,18},{3,19},{4,20},{5,21},{6,22},{7,23},{8,24},{9,... | collective-permute-start | bytes 983048 | tf_op jit(solution)/shard_map/ppermute | solution.py:21
  739.2 5.2 collective-permute-start.44
  744.4 4.3 collective-permute-start.45
